TPU v7x, 256 devices: a whole 4x4x8 slice. The times are simulated.
256 devices in a mesh: pipe: 8 (over y, x_lo), dp: 32 (over x_hi, z, core).
Axes of the slice: x: 4 (x_hi: 2, x_lo: 2; x = x_hi * 2 + x_lo), y: 4, z: 8, core: 2. Of those that a mesh axis runs over, the one named last changes fastest.
Arguments:
- latents: bfloat16 [4, 32, 56, 1536], P(None, 'dp'), may hold values from -6 to 6
- out_grad: bfloat16 [4, 32, 56, 1536], P(None, 'dp'), may hold values from -0.0625 to 0.0625
- w_qkv: bfloat16 [8, 1536, 4608], P('pipe', 'dp'), may hold values from -0.15625 to 0.15625
- mod_table: float32 [8, 16, 3, 1536], P('pipe'), may hold values from -4 to 4
- timesteps: int32 [4, 32], P(None, 'dp'), may hold values from 0 to 15
- text_len: int32 [4, 32], P(None, 'dp'), may hold values from 1 to 16, as said below
Outputs:
- grad_qkv: float32 [8, 1536, 4608], P('pipe', 'dp')
Inputs may be any that keep to these rules, and one draw needn't show every extreme that they name: `text_len`: some sample has all 16 text tokens live.
All inputs are finite; a program needn't handle non-finite values.
Results may differ from a plain program's by a relative error of at most 0.024.
Values may be sent and summed in bfloat16 or wider, within the bound.
No kernel may reach another device: no remote copies, remote signals or barrier semaphores. Data moves between devices by JAX's collectives and lax.ppermute only.
A program may use at most 128 MiB of HBM per device.

v0:
```python
import math

import jax
import jax.numpy as jnp
from jax import lax
from jax.sharding import PartitionSpec as P

HEADS = 12
HDIM = 128
IMG = 40


EPS = 1e-06


def from_behind(block, axis, distance):
    devices = range(lax.axis_size(axis))
    route = [(i - distance, i) for i in devices if i - distance in devices]
    return lax.ppermute(block, axis, route)


def modnorm(hidden, modulation):
    average = jnp.mean(hidden, axis=-1, keepdims=True)
    centered = hidden - average
    variance = jnp.mean(centered * centered, axis=-1, keepdims=True)
    return (1.0 + modulation[1]) * (centered * lax.rsqrt(variance + EPS)) + modulation[0]


def attend(projected, hidden, modulation, length):
    seq_len = hidden.shape[0]
    model_width = hidden.shape[1]
    queries = projected[:, :model_width].reshape(seq_len, HEADS, HDIM)
    key_rows = projected[:, model_width : 2 * model_width].reshape(seq_len, HEADS, HDIM)
    values = projected[:, 2 * model_width :].reshape(seq_len, HEADS, HDIM)
    queries = queries * lax.rsqrt(jnp.mean(queries * queries, axis=-1, keepdims=True) + EPS)
    key_rows = key_rows * lax.rsqrt(jnp.mean(key_rows * key_rows, axis=-1, keepdims=True) + EPS)
    scores = jnp.einsum("qhc,khc->hqk", queries, key_rows) / math.sqrt(HDIM)
    position = jnp.arange(seq_len, dtype=jnp.int32)
    usable = ((position < IMG) | (position - IMG < length)).astype(jnp.float32)
    weights = jnp.exp(scores) * usable
    attention = weights / jnp.sum(weights, axis=-1, keepdims=True)
    mixture = jnp.einsum("hqk,khc->qhc", attention, values).reshape(seq_len, model_width)
    return hidden + modulation[2] * mixture


def section_forward(hidden_in, weight_full, modulation, length):
    hidden = hidden_in.astype(jnp.float32)
    normed = modnorm(hidden, modulation).astype(jnp.bfloat16)
    projected = jnp.dot(normed, weight_full, preferred_element_type=jnp.float32)
    output = attend(projected, hidden, modulation, length).astype(jnp.bfloat16)
    return (output, normed, projected)


def section_backward(cotangent, projected, hidden_in, weight_full, modulation, length):
    hidden = hidden_in.astype(jnp.float32)
    _, pullback = jax.vjp(
        lambda proj, state: attend(proj, state, modulation, length), projected, hidden
    )
    proj_grad, direct_grad = pullback(cotangent.astype(jnp.float32))
    proj_low = proj_grad.astype(jnp.bfloat16)
    norm_grad = lax.dot_general(
        proj_low, weight_full, (((1,), (1,)), ((), ())), preferred_element_type=jnp.float32
    )
    _, norm_pull = jax.vjp(lambda state: modnorm(state, modulation), hidden)
    (input_grad,) = norm_pull(norm_grad)
    return ((direct_grad + input_grad).astype(jnp.bfloat16), proj_low)


def shards(latents, out_grad, w_qkv, mod_table, timesteps, text_len):
    section_index = lax.axis_index("pipe")
    section_count = lax.axis_size("pipe")
    micro_count = latents.shape[0]
    seq_len = latents.shape[2]
    model_width = latents.shape[3]
    weight_full = lax.all_gather(w_qkv[0], "dp", axis=0, tiled=True)
    levels = mod_table.shape[1]
    onehot = (timesteps[:, 0][:, None] == jnp.arange(levels, dtype=jnp.int32)[None, :]).astype(
        jnp.float32
    )
    modulations = jnp.dot(
        onehot, mod_table[0].reshape(levels, 3 * model_width), precision=lax.Precision.HIGHEST
    ).reshape(micro_count, 3, model_width)
    lengths = text_len[:, 0]
    inputs_first = latents[:, 0]
    grads_last = out_grad[:, 0]
    tick_total = micro_count + section_count - 1
    zero_rows = jnp.zeros((seq_len, model_width), jnp.bfloat16)
    saved_in = jnp.zeros((micro_count, seq_len, model_width), jnp.bfloat16)
    saved_norm = jnp.zeros((micro_count, seq_len, model_width), jnp.bfloat16)
    saved_proj = jnp.zeros((micro_count, seq_len, 3 * model_width), jnp.float32)

    def forward_tick(tick_index, carried):
        incoming, stash_in, stash_norm, stash_proj = carried
        micro = tick_index - section_index
        active = (micro >= 0) & (micro < micro_count)
        slot_index = jnp.clip(micro, 0, micro_count - 1)
        entering = jnp.where(section_index == 0, inputs_first[slot_index], incoming)
        modulation = modulations[slot_index]
        length = lengths[slot_index]

        def forward_compute(operands):
            keep_in, keep_norm, keep_proj = operands
            output, normed, projected = section_forward(entering, weight_full, modulation, length)
            keep_in = keep_in.at[slot_index].set(entering)
            keep_norm = keep_norm.at[slot_index].set(normed)
            keep_proj = keep_proj.at[slot_index].set(projected)
            return (output, keep_in, keep_norm, keep_proj)

        def forward_passing(operands):
            return (zero_rows,) + tuple(operands)

        output, stash_in, stash_norm, stash_proj = lax.cond(
            active, forward_compute, forward_passing, (stash_in, stash_norm, stash_proj)
        )
        outgoing = from_behind(output, "pipe", 1)
        return (outgoing, stash_in, stash_norm, stash_proj)

    _, saved_in, saved_norm, saved_proj = lax.fori_loop(
        0, tick_total, forward_tick, (zero_rows, saved_in, saved_norm, saved_proj)
    )
    holder = jnp.zeros((micro_count, seq_len, 3 * model_width), jnp.bfloat16)

    def backward_tick(tick_index, carried):
        incoming, keeper = carried
        micro = tick_index - (section_count - 1 - section_index)
        active = (micro >= 0) & (micro < micro_count)
        slot_index = jnp.clip(micro, 0, micro_count - 1)
        cotangent = jnp.where(section_index == section_count - 1, grads_last[slot_index], incoming)
        modulation = modulations[slot_index]
        length = lengths[slot_index]

        def backward_compute(kept):
            projected = saved_proj[slot_index]
            back_grad, proj_low = section_backward(
                cotangent, projected, saved_in[slot_index], weight_full, modulation, length
            )
            update = kept.at[slot_index].set(proj_low)
            return (back_grad, update)

        def backward_passing(kept):
            return (zero_rows, kept)

        back_grad, keeper = lax.cond(active, backward_compute, backward_passing, keeper)
        outgoing = from_behind(back_grad, "pipe", -1)
        return (outgoing, keeper)

    _, keeper = lax.fori_loop(0, tick_total, backward_tick, (zero_rows, holder))
    norm_rows = saved_norm.reshape(micro_count * seq_len, model_width)
    grad_rows = keeper.reshape(micro_count * seq_len, 3 * model_width)
    grads = lax.psum_scatter(
        lax.dot_general(
            norm_rows, grad_rows, (((0,), (0,)), ((), ())), preferred_element_type=jnp.float32
        ).astype(jnp.bfloat16),
        "dp",
        scatter_dimension=0,
        tiled=True,
    ).astype(jnp.float32)
    return grads[None]


def solution(mesh):
    return jax.shard_map(
        shards,
        mesh=mesh,
        in_specs=(
            P(None, "dp", None, None),
            P(None, "dp", None, None),
            P("pipe", "dp", None),
            P("pipe", None, None, None),
            P(None, "dp"),
            P(None, "dp"),
        ),
        out_specs=P("pipe", "dp", None),
        check_vma=False,
    )
```

profile of v0, /device:TPU:8, one launch (start us, length us, event | category | flops | bytes accessed | tf_op | source)
XLA Modules:
  0.0 981.7 jit_solution(17312440614065253503)
XLA Ops:
  10.1 127.7 %all-gather.3.cloned.1.call-done = bf16[1,1536,4608]{2,1,0:T(8,128)(2,1)} async-done(((bf16[1,48,4608]{2,1,0:T(8,128)(2,1)}), bf16[1,1536,4608]{2,1,0:T(8,128)(2,1)}) %all-gather.3.cloned.1.call-update) | async-done | bytes 14155792 | tf_op jit(solution)/shard_map/all_gather | solution.py:75
  141.2 253.5 %while.44 = (s32[]{:T(128)}, bf16[56,1536]{1,0:T(8,128)(2,1)S(1)}, bf16[4,56,1536]{2,1,0:T(8,128)(2,1)S(1)}, bf16[4,56,1536]{2,1,0:T(8,128)(2,1)}, f32[4,56,4608...) while((s32[]{:T(128)}, bf16[56,1536]{1,0:T(8,128)(2,1)S(1)}, ...), condition=%wide.region_9.0_spmd, body=%wide.region_0.9_spmd.sunk | while | flops 815204352 | bytes 26787108 | solution.py:118
  152.6 42.1 %collective-permute-done = bf16[56,1536]{1,0:T(8,128)(2,1)S(1)} collective-permute-done((bf16[56,1536]{1,0:T(8,128)(2,1)S(1)}, bf16[56,1536]{1,0:T(8,128)(2,1)S(1)}, u32[]{:S(2)}, u32[]{:S(2)}) %collective-permute-start) | collective-permute-done | bytes 172064 | tf_op jit(solution)/shard_map/while/body/eval_jaxpr/ppermute | solution.py:19
  194.7 19.6 %conditional.4 = (bf16[56,1536]{1,0:T(8,128)(2,1)S(1)}, bf16[4,56,1536]{2,1,0:T(8,128)(2,1)S(1)}, bf16[4,56,1536]{2,1,0:T(8,128)(2,1)}, f32[4,56,4608]{2,1,0:T(8,128)}) conditional(s32[]{:T(128)} %convert_element_type.153, (bf16[4,56,1536]{2,1,0:T(8,128)(2,1)S(1)}, bf16[4,56,1536]{2,1,0:T(8,128)(2,1)}, f32[4,56,4608]{2,1,0:T(8,128)}) %tuple.147, ...), branch_computations={%region_1.1_spmd, %region_2.8_spmd} | conditional | flops 815204352 | bytes 26098664 | solution.py:112
  222.6 19.6 %conditional.4 = (bf16[56,1536]{1,0:T(8,128)(2,1)S(1)}, bf16[4,56,1536]{2,1,0:T(8,128)(2,1)S(1)}, bf16[4,56,1536]{2,1,0:T(8,128)(2,1)}, f32[4,56,4608]{2,1,0:T(8,128)}) conditional(s32[]{:T(128)} %convert_element_type.153, (bf16[4,56,1536]{2,1,0:T(8,128)(2,1)S(1)}, bf16[4,56,1536]{2,1,0:T(8,128)(2,1)}, f32[4,56,4608]{2,1,0:T(8,128)}) %tuple.147, ...), branch_computations={%region_1.1_spmd, %region_2.8_spmd} | conditional | flops 815204352 | bytes 26098664 | solution.py:112
  250.4 19.6 %conditional.4 = (bf16[56,1536]{1,0:T(8,128)(2,1)S(1)}, bf16[4,56,1536]{2,1,0:T(8,128)(2,1)S(1)}, bf16[4,56,1536]{2,1,0:T(8,128)(2,1)}, f32[4,56,4608]{2,1,0:T(8,128)}) conditional(s32[]{:T(128)} %convert_element_type.153, (bf16[4,56,1536]{2,1,0:T(8,128)(2,1)S(1)}, bf16[4,56,1536]{2,1,0:T(8,128)(2,1)}, f32[4,56,4608]{2,1,0:T(8,128)}) %tuple.147, ...), branch_computations={%region_1.1_spmd, %region_2.8_spmd} | conditional | flops 815204352 | bytes 26098664 | solution.py:112
  278.2 19.6 %conditional.4 = (bf16[56,1536]{1,0:T(8,128)(2,1)S(1)}, bf16[4,56,1536]{2,1,0:T(8,128)(2,1)S(1)}, bf16[4,56,1536]{2,1,0:T(8,128)(2,1)}, f32[4,56,4608]{2,1,0:T(8,128)}) conditional(s32[]{:T(128)} %convert_element_type.153, (bf16[4,56,1536]{2,1,0:T(8,128)(2,1)S(1)}, bf16[4,56,1536]{2,1,0:T(8,128)(2,1)}, f32[4,56,4608]{2,1,0:T(8,128)}) %tuple.147, ...), branch_computations={%region_1.1_spmd, %region_2.8_spmd} | conditional | flops 815204352 | bytes 26098664 | solution.py:112
  306.0 20.6 %collective-permute-start = (bf16[56,1536]{1,0:T(8,128)(2,1)S(1)}, bf16[56,1536]{1,0:T(8,128)(2,1)S(1)}, u32[]{:S(2)}, u32[]{:S(2)}) collective-permute-start(bf16[56,1536]{1,0:T(8,128)(2,1)S(1)} %get-tuple-element.1085), channel_id=1, source_target_pairs={{0,32},{32,64},{64,96},{96,128},{128,160},{160,192},{192,224},{1,3... | collective-permute-start | bytes 516104 | tf_op jit(solution)/shard_map/while/body/eval_jaxpr/ppermute | solution.py:19
  340.6 20.5 %collective-permute-start = (bf16[56,1536]{1,0:T(8,128)(2,1)S(1)}, bf16[56,1536]{1,0:T(8,128)(2,1)S(1)}, u32[]{:S(2)}, u32[]{:S(2)}) collective-permute-start(bf16[56,1536]{1,0:T(8,128)(2,1)S(1)} %get-tuple-element.1085), channel_id=1, source_target_pairs={{0,32},{32,64},{64,96},{96,128},{128,160},{160,192},{192,224},{1,3... | collective-permute-start | bytes 516104 | tf_op jit(solution)/shard_map/while/body/eval_jaxpr/ppermute | solution.py:19
  374.0 17.8 %collective-permute-start = (bf16[56,1536]{1,0:T(8,128)(2,1)S(1)}, bf16[56,1536]{1,0:T(8,128)(2,1)S(1)}, u32[]{:S(2)}, u32[]{:S(2)}) collective-permute-start(bf16[56,1536]{1,0:T(8,128)(2,1)S(1)} %get-tuple-element.1085), channel_id=1, source_target_pairs={{0,32},{32,64},{64,96},{96,128},{128,160},{160,192},{192,224},{1,3... | collective-permute-start | bytes 516104 | tf_op jit(solution)/shard_map/while/body/eval_jaxpr/ppermute | solution.py:19
  396.8 367.3 %while.45 = (s32[]{:T(128)}, bf16[56,1536]{1,0:T(8,128)(2,1)}, bf16[4,56,4608]{2,1,0:T(8,128)(2,1)}, s32[]{:T(128)}, pred[]{:T(512)}, /*index=5*/bf16[4,56,1536]...) while((s32[]{:T(128)}, bf16[56,1536]{1,0:T(8,128)(2,1)}, ...), condition=%wide.region_24.0_spmd, body=%wide.region_10.24_spmd.sunk | while | flops 847811392 | bytes 37955212 | solution.py:147
  409.7 24.4 %collective-permute-done.1 = bf16[56,1536]{1,0:T(8,128)(2,1)S(1)} collective-permute-done((bf16[56,1536]{1,0:T(8,128)(2,1)}, bf16[56,1536]{1,0:T(8,128)(2,1)S(1)}, u32[]{:S(2)}, u32[]{:S(2)}) %collective-permute-start.1) | collective-permute-done | bytes 172064 | tf_op jit(solution)/shard_map/while/body/eval_jaxpr/ppermute | solution.py:19
  447.1 21.0 %collective-permute-done.1 = bf16[56,1536]{1,0:T(8,128)(2,1)S(1)} collective-permute-done((bf16[56,1536]{1,0:T(8,128)(2,1)}, bf16[56,1536]{1,0:T(8,128)(2,1)S(1)}, u32[]{:S(2)}, u32[]{:S(2)}) %collective-permute-start.1) | collective-permute-done | bytes 172064 | tf_op jit(solution)/shard_map/while/body/eval_jaxpr/ppermute | solution.py:19
  471.3 121.2 %collective-permute-done.1 = bf16[56,1536]{1,0:T(8,128)(2,1)S(1)} collective-permute-done((bf16[56,1536]{1,0:T(8,128)(2,1)}, bf16[56,1536]{1,0:T(8,128)(2,1)S(1)}, u32[]{:S(2)}, u32[]{:S(2)}) %collective-permute-start.1) | collective-permute-done | bytes 172064 | tf_op jit(solution)/shard_map/while/body/eval_jaxpr/ppermute | solution.py:19
  593.1 23.8 %conditional.5 = (bf16[56,1536]{1,0:T(8,128)(2,1)}, bf16[4,56,4608]{2,1,0:T(8,128)(2,1)}) conditional(s32[]{:T(128)} %convert_element_type.154, bf16[4,56,4608]{2,1,0:T(8,128)(2,1)} %get-tuple-element.1172, (pred[]{:T(512)}, s32[]{:T(128)}, bf16[4,56,1536]{2,1,0:T(8,128)(2,1)}, bf16[56,1536]{1,0:T(8,128)(2,1)}, f32[4,3,1536]{2,1,0:T(4,128)}, ...), branch_computations={%region_11.11_spmd, %region_12.23_spmd} | conditional | flops 847811392 | bytes 36578640 | solution.py:143
  605.4 9.5 fusion.30
  626.0 23.8 %conditional.5 = (bf16[56,1536]{1,0:T(8,128)(2,1)}, bf16[4,56,4608]{2,1,0:T(8,128)(2,1)}) conditional(s32[]{:T(128)} %convert_element_type.154, bf16[4,56,4608]{2,1,0:T(8,128)(2,1)} %get-tuple-element.1172, (pred[]{:T(512)}, s32[]{:T(128)}, bf16[4,56,1536]{2,1,0:T(8,128)(2,1)}, bf16[56,1536]{1,0:T(8,128)(2,1)}, f32[4,3,1536]{2,1,0:T(4,128)}, ...), branch_computations={%region_11.11_spmd, %region_12.23_spmd} | conditional | flops 847811392 | bytes 36578640 | solution.py:143
  638.3 9.5 fusion.30
  658.9 23.8 %conditional.5 = (bf16[56,1536]{1,0:T(8,128)(2,1)}, bf16[4,56,4608]{2,1,0:T(8,128)(2,1)}) conditional(s32[]{:T(128)} %convert_element_type.154, bf16[4,56,4608]{2,1,0:T(8,128)(2,1)} %get-tuple-element.1172, (pred[]{:T(512)}, s32[]{:T(128)}, bf16[4,56,1536]{2,1,0:T(8,128)(2,1)}, bf16[56,1536]{1,0:T(8,128)(2,1)}, f32[4,3,1536]{2,1,0:T(4,128)}, ...), branch_computations={%region_11.11_spmd, %region_12.23_spmd} | conditional | flops 847811392 | bytes 36578640 | solution.py:143
  671.2 9.5 fusion.30
  691.8 23.8 %conditional.5 = (bf16[56,1536]{1,0:T(8,128)(2,1)}, bf16[4,56,4608]{2,1,0:T(8,128)(2,1)}) conditional(s32[]{:T(128)} %convert_element_type.154, bf16[4,56,4608]{2,1,0:T(8,128)(2,1)} %get-tuple-element.1172, (pred[]{:T(512)}, s32[]{:T(128)}, bf16[4,56,1536]{2,1,0:T(8,128)(2,1)}, bf16[56,1536]{1,0:T(8,128)(2,1)}, f32[4,3,1536]{2,1,0:T(4,128)}, ...), branch_computations={%region_11.11_spmd, %region_12.23_spmd} | conditional | flops 847811392 | bytes 36578640 | solution.py:143
  724.5 26.0 %collective-permute-start.1 = (bf16[56,1536]{1,0:T(8,128)(2,1)}, bf16[56,1536]{1,0:T(8,128)(2,1)S(1)}, u32[]{:S(2)}, u32[]{:S(2)}) collective-permute-start(bf16[56,1536]{1,0:T(8,128)(2,1)} %get-tuple-element.1100), channel_id=1, source_target_pairs={{32,0},{64,32},{96,64},{128,96},{160,128},{192,160},{224,192},{33,... | collective-permute-start | bytes 516104 | tf_op jit(solution)/shard_map/while/body/eval_jaxpr/ppermute | solution.py:19
  764.1 10.7 %bitcast_convert_fusion = bf16[1536,4608]{1,0:T(8,128)(2,1)} fusion(bf16[4,56,1536]{2,1,0:T(8,128)(2,1)} %get-tuple-element.766, bf16[4,56,4608]{2,1,0:T(8,128)(2,1)} %get-tuple-element.769), kind=kOutput, calls=%fused_computation.126 | convolution fusion | flops 3177971712 | bytes 16908288 | tf_op jit(solution)/shard_map/dot_general | solution.py:151
  774.9 198.0 %reduce-scatter.2.cloned.1.call-done = bf16[48,4608]{1,0:T(8,128)(2,1)} async-done(((bf16[1536,4608]{1,0:T(8,128)(2,1)}), bf16[48,4608]{1,0:T(8,128)(2,1)}) %reduce-scatter.2.cloned.1.call-update) | async-done | bytes 442384 | tf_op jit(solution)/shard_map/reduce_scatter | solution.py:150
  (349 shorter events, 313.1 us)
Async XLA Ops:
  6.5 131.3 %all-gather.3.cloned.1.call-start = ((), (), s32[]{:S(2)}) async-start(), calls=%async_computation.2 | async-start | bytes 14598144 | tf_op jit(solution)/shard_map/all_gather | solution.py:75
  7.3 965.7 %reduce-scatter.2.cloned.1.call-start = ((), (), s32[]{:S(2)}) async-start(), calls=%async_computation.1 | async-start | bytes 14598144 | tf_op jit(solution)/shard_map/reduce_scatter | solution.py:150
  141.3 9.3 collective-permute-start
  150.6 44.1 %collective-permute-start = (bf16[56,1536]{1,0:T(8,128)(2,1)S(1)}, bf16[56,1536]{1,0:T(8,128)(2,1)S(1)}, u32[]{:S(2)}, u32[]{:S(2)}) collective-permute-start(bf16[56,1536]{1,0:T(8,128)(2,1)S(1)} %get-tuple-element.1085), channel_id=1, source_target_pairs={{0,32},{32,64},{64,96},{96,128},{128,160},{160,192},{192,224},{1,3... | collective-permute-start | bytes 516104 | tf_op jit(solution)/shard_map/while/body/eval_jaxpr/ppermute | solution.py:19
  214.3 8.3 collective-permute-start
  242.2 8.2 collective-permute-start
  270.0 8.2 collective-permute-start
  297.8 8.2 collective-permute-start
  306.0 25.0 %collective-permute-start = (bf16[56,1536]{1,0:T(8,128)(2,1)S(1)}, bf16[56,1536]{1,0:T(8,128)(2,1)S(1)}, u32[]{:S(2)}, u32[]{:S(2)}) collective-permute-start(bf16[56,1536]{1,0:T(8,128)(2,1)S(1)} %get-tuple-element.1085), channel_id=1, source_target_pairs={{0,32},{32,64},{64,96},{96,128},{128,160},{160,192},{192,224},{1,3... | collective-permute-start | bytes 516104 | tf_op jit(solution)/shard_map/while/body/eval_jaxpr/ppermute | solution.py:19
  331.1 9.5 collective-permute-start
  340.6 24.6 %collective-permute-start = (bf16[56,1536]{1,0:T(8,128)(2,1)S(1)}, bf16[56,1536]{1,0:T(8,128)(2,1)S(1)}, u32[]{:S(2)}, u32[]{:S(2)}) collective-permute-start(bf16[56,1536]{1,0:T(8,128)(2,1)S(1)} %get-tuple-element.1085), channel_id=1, source_target_pairs={{0,32},{32,64},{64,96},{96,128},{128,160},{160,192},{192,224},{1,3... | collective-permute-start | bytes 516104 | tf_op jit(solution)/shard_map/while/body/eval_jaxpr/ppermute | solution.py:19
  365.3 8.6 collective-permute-start
  374.0 20.7 %collective-permute-start = (bf16[56,1536]{1,0:T(8,128)(2,1)S(1)}, bf16[56,1536]{1,0:T(8,128)(2,1)S(1)}, u32[]{:S(2)}, u32[]{:S(2)}) collective-permute-start(bf16[56,1536]{1,0:T(8,128)(2,1)S(1)} %get-tuple-element.1085), channel_id=1, source_target_pairs={{0,32},{32,64},{64,96},{96,128},{128,160},{160,192},{192,224},{1,3... | collective-permute-start | bytes 516104 | tf_op jit(solution)/shard_map/while/body/eval_jaxpr/ppermute | solution.py:19
  397.5 8.9 collective-permute-start.1
  407.7 26.4 %collective-permute-start.1 = (bf16[56,1536]{1,0:T(8,128)(2,1)}, bf16[56,1536]{1,0:T(8,128)(2,1)S(1)}, u32[]{:S(2)}, u32[]{:S(2)}) collective-permute-start(bf16[56,1536]{1,0:T(8,128)(2,1)} %get-tuple-element.1100), channel_id=1, source_target_pairs={{32,0},{64,32},{96,64},{128,96},{160,128},{192,160},{224,192},{33,... | collective-permute-start | bytes 516104 | tf_op jit(solution)/shard_map/while/body/eval_jaxpr/ppermute | solution.py:19
  435.4 8.0 collective-permute-start.1
  444.8 23.2 %collective-permute-start.1 = (bf16[56,1536]{1,0:T(8,128)(2,1)}, bf16[56,1536]{1,0:T(8,128)(2,1)S(1)}, u32[]{:S(2)}, u32[]{:S(2)}) collective-permute-start(bf16[56,1536]{1,0:T(8,128)(2,1)} %get-tuple-element.1100), channel_id=1, source_target_pairs={{32,0},{64,32},{96,64},{128,96},{160,128},{192,160},{224,192},{33,... | collective-permute-start | bytes 516104 | tf_op jit(solution)/shard_map/while/body/eval_jaxpr/ppermute | solution.py:19
  469.4 123.1 %collective-permute-start.1 = (bf16[56,1536]{1,0:T(8,128)(2,1)}, bf16[56,1536]{1,0:T(8,128)(2,1)S(1)}, u32[]{:S(2)}, u32[]{:S(2)}) collective-permute-start(bf16[56,1536]{1,0:T(8,128)(2,1)} %get-tuple-element.1100), channel_id=1, source_target_pairs={{32,0},{64,32},{96,64},{128,96},{160,128},{192,160},{224,192},{33,... | collective-permute-start | bytes 516104 | tf_op jit(solution)/shard_map/while/body/eval_jaxpr/ppermute | solution.py:19
  617.0 8.4 collective-permute-start.1
  649.9 8.4 collective-permute-start.1
  682.8 8.4 collective-permute-start.1
  715.6 7.5 collective-permute-start.1
  724.5 29.2 %collective-permute-start.1 = (bf16[56,1536]{1,0:T(8,128)(2,1)}, bf16[56,1536]{1,0:T(8,128)(2,1)S(1)}, u32[]{:S(2)}, u32[]{:S(2)}) collective-permute-start(bf16[56,1536]{1,0:T(8,128)(2,1)} %get-tuple-element.1100), channel_id=1, source_target_pairs={{32,0},{64,32},{96,64},{128,96},{160,128},{192,160},{224,192},{33,... | collective-permute-start | bytes 516104 | tf_op jit(solution)/shard_map/while/body/eval_jaxpr/ppermute | solution.py:19
  755.1 8.4 collective-permute-start.1
  (19 other events, 53.6 us)
Sparse Core Ops, SparseCore 0:
  10.1 127.6 all-gather.2
  775.0 197.8 reduce-scatter.1
where the time goes:
time: 984 us; the launch traced here: 982 us
  waiting for transfers between devices  632 us (64%)
  starting transfers between devices  129 us (13%)
  matrix products  97.5 us (10%)
  other arithmetic  70.1 us (7%)
  local copies, waits for them, and re-layouts  38.2 us (4%)
  between operations  13.4 us (1%)
    ppermute x22, waiting for transfers between devices, from_behind(): return lax.ppermute(block, axis, route)  306 us
    reduce_scatter x1, waiting for transfers between devices, shards(): lax.psum_scatter(lax.dot_general(norm_rows, grad_rows, (((0,), (0,)), (()...  198 us
    ppermute x22, starting transfers between devices, from_behind(): return lax.ppermute(block, axis, route)  129 us
    all_gather x1, waiting for transfers between devices, shards(): weight_full = lax.all_gather(w_qkv[0], 'dp', axis=0, tiled=True)  128 us
    dot_general x4, matrix products, section_backward(): lax.dot_general(proj_low, weight_full, (((1,), (1,)), ((), ())), preferre...  38 us
    dot_general x4, matrix products, section_forward(): projected = jnp.dot(normed, weight_full, preferred_element_type=jnp.float32)  37.7 us
  transfers between devices with their start and end apart: 24, of which 24 were waited for; matrix products, arithmetic and copies ran while one was open for 0% of the time, Pallas kernels for 0%

commit v1 on v0

v1 whole, which is shorter than its diff:
```python
import functools
import math

import jax
import jax.numpy as jnp
from jax import lax
from jax.experimental import pallas as pl
from jax.experimental.pallas import tpu as pltpu
from jax.sharding import Mesh
from jax.sharding import PartitionSpec as P

IMG = 40
EPS = 1e-06
HDIM = 128
BLOCKS = 8
QUART = 4
PAIR = 2
F32 = jnp.float32
BF16 = jnp.bfloat16
VM = pl.BlockSpec(memory_space=pltpu.VMEM)
SM = pl.BlockSpec(memory_space=pltpu.SMEM)
ANY = pl.BlockSpec(memory_space=pl.ANY)


def place(scal, k):
    p = scal[2]
    j = lax.max((k - p + 2) // 2 - 1, 0)
    j = lax.min(j, BLOCKS // 2 - 1)
    return lax.rem(k + p, 2), j


def fetch_weights(scal, pieces, wscr, sem):
    c = scal[1]
    halves = wscr.shape[0]

    def start(own, other):
        for t in range(halves):
            pltpu.make_async_copy(own.at[:, t], wscr.at[t, :, c], sem).start()
            pltpu.make_async_copy(other.at[:, t], wscr.at[t, :, 1 - c], sem).start()

    if len(pieces) == 2:
        start(*pieces)
    else:

        @pl.when(scal[2] == 0)
        def _():
            start(*pieces[:2])

        @pl.when(scal[2] != 0)
        def _():
            start(*pieces[2:])


def await_weights(wscr, sem):
    pltpu.make_async_copy(wscr, wscr, sem).wait()


def half_weights(wscr, t):
    value = wscr[t]
    return value.reshape(value.shape[0] * value.shape[1] * value.shape[2], value.shape[3])


def standardize(hidden):
    average = jnp.mean(hidden, axis=-1, keepdims=True)
    centered = hidden - average
    variance = jnp.mean(centered * centered, axis=-1, keepdims=True)
    scale = lax.rsqrt(variance + EPS)
    return centered * scale, scale


def nt(a, b):
    return lax.dot_general(
        a.astype(BF16), b.astype(BF16), (((1,), (1,)), ((), ())), preferred_element_type=F32
    )


def nn(a, b):
    return lax.dot_general(
        a.astype(BF16), b.astype(BF16), (((1,), (0,)), ((), ())), preferred_element_type=F32
    )


def tn(a, b):
    return lax.dot_general(
        a.astype(BF16), b.astype(BF16), (((0,), (0,)), ((), ())), preferred_element_type=F32
    )


def unit(rows):
    scale = lax.rsqrt(jnp.mean(rows * rows, axis=-1, keepdims=True) + EPS)
    return rows * scale, scale


def weights_of(q, k, length):
    scores = nt(q, k) * (1.0 / math.sqrt(HDIM))
    position = lax.broadcasted_iota(jnp.int32, scores.shape, 1)
    usable = (position < IMG) | (position - IMG < length)
    weights = jnp.where(usable, jnp.exp(scores), 0.0)
    return weights / jnp.sum(weights, axis=-1, keepdims=True)


def forward_kernel(k, n_in, n_w, send, scal, *refs):
    ins, refs = refs[:n_in], refs[n_in:]
    mods, gates = refs[:2]
    pieces, refs = refs[2 : 2 + n_w], refs[2 + n_w :]
    if send:
        out_ref, refs = refs[0], refs[1:]
    hidden_ref, normed_ref, proj_ref, wscr, hs, sem = refs
    fetch_weights(scal, pieces, wscr, sem)
    y = scal[0]
    micro, j = place(scal, k)
    chunk = hs.shape[2]

    def from_whole(ref):
        for t in range(QUART):
            hs[t] = ref[:, t * chunk : (t + 1) * chunk]

    def from_chunks(parts):
        for d in range(QUART):
            hs[lax.rem(y + QUART - d, QUART)] = parts[d][...]

    if n_in == 1:
        from_whole(ins[0])
    elif n_in == QUART:
        from_chunks(ins)
    else:

        @pl.when(scal[2] == 0)
        def _():
            from_whole(ins[0])

        @pl.when(scal[2] != 0)
        def _():
            from_chunks(ins[1:])

    for t in range(QUART):
        hidden_ref[:, t * chunk : (t + 1) * chunk] = hs[t]
    rows, width = hidden_ref.shape
    seq = rows // PAIR
    normal, _ = standardize(hidden_ref[...].astype(F32))
    normal = normal.reshape(PAIR, seq, width)
    normed = jnp.concatenate(
        [
            (1.0 + mods[j, PAIR * micro + s, 1:2, :]) * normal[s]
            + mods[j, PAIR * micro + s, 0:1, :]
            for s in range(PAIR)
        ],
        axis=0,
    ).astype(BF16)
    normed_ref[...] = normed
    await_weights(wscr, sem)
    halves = wscr.shape[0]
    span = width // halves
    projected = nn(normed[:, :span], half_weights(wscr, 0))
    for t in range(1, halves):
        projected += nn(normed[:, t * span : (t + 1) * span], half_weights(wscr, t))
    proj_ref[...] = projected
    if not send:
        return
    own = hs[y].astype(F32)
    for s in range(PAIR):
        length = scal[3 + PAIR * micro + s]
        r = slice(s * seq, (s + 1) * seq)
        mixed = []
        for h in range(chunk // HDIM):
            lo = h * HDIM
            q, _ = unit(proj_ref[r, lo : lo + HDIM])
            key, _ = unit(proj_ref[r, chunk + lo : chunk + lo + HDIM])
            v = proj_ref[r, 2 * chunk + lo : 2 * chunk + lo + HDIM]
            mixed.append(nn(weights_of(q, key, length), v))
        mixture = jnp.concatenate(mixed, axis=1)
        gate = gates[j, PAIR * micro + s]
        hs_rows = own[r] + gate * mixture
        if s == 0:
            first = hs_rows
    out_ref[...] = jnp.concatenate([first, hs_rows], axis=0).astype(BF16)


def backward_kernel(k, n_in, n_w, send, scal, *refs):
    ins, refs = refs[:n_in], refs[n_in:]
    mods, gates, hidden_ref, proj_ref = refs[:4]
    pieces, refs = refs[4 : 4 + n_w], refs[4 + n_w :]
    outs, refs = refs[: QUART * send], refs[QUART * send :]
    low_ref, wscr, gs, dp, ds, sem = refs
    if send:
        fetch_weights(scal, pieces, wscr, sem)
    y = scal[0]
    micro, j = place(scal, k)
    rows, width = hidden_ref.shape
    chunk = width // QUART
    seq = rows // PAIR

    def total(parts):
        gs[...] = sum([part[...].astype(F32) for part in parts[1:]], parts[0][...].astype(F32))

    if n_in == 1:
        total(ins)
    elif n_in == QUART:
        total(ins)
    else:

        @pl.when(scal[2] != 0)
        def _():
            total(ins[:1])

        @pl.when(scal[2] == 0)
        def _():
            total(ins[1:])

    root = 1.0 / math.sqrt(HDIM)
    for s in range(PAIR):
        length = scal[3 + PAIR * micro + s]
        r = slice(s * seq, (s + 1) * seq)
        for h in range(chunk // HDIM):
            lo = h * HDIM
            c = slice(lo, lo + HDIM)
            gate = gates[j, PAIR * micro + s, :, c]
            dmix = gs[r, c] * gate
            q, rq = unit(proj_ref[r, lo : lo + HDIM])
            key, rk = unit(proj_ref[r, chunk + lo : chunk + lo + HDIM])
            v = proj_ref[r, 2 * chunk + lo : 2 * chunk + lo + HDIM]
            att = weights_of(q, key, length)
            datt = nt(dmix, v)
            dscore = att * (datt - jnp.sum(att * datt, axis=-1, keepdims=True)) * root
            dqn = nn(dscore, key)
            dkn = tn(dscore, q)
            dp[r, c] = rq * (dqn - q * jnp.mean(dqn * q, axis=-1, keepdims=True))
            dp[r, chunk + lo : chunk + lo + HDIM] = rk * (
                dkn - key * jnp.mean(dkn * key, axis=-1, keepdims=True)
            )
            dp[r, 2 * chunk + lo : 2 * chunk + lo + HDIM] = tn(att, dmix)
    low = dp[...].astype(BF16)
    low_ref[...] = low
    if not send:
        return
    normal, scale = standardize(hidden_ref[...].astype(F32))
    await_weights(wscr, sem)
    halves = wscr.shape[0]
    norm_grad = jnp.concatenate([nt(low, half_weights(wscr, t)) for t in range(halves)], axis=1)
    norm_grad = norm_grad.reshape(PAIR, seq, width)
    grad = jnp.concatenate(
        [(1.0 + mods[j, PAIR * micro + s, 1:2, :]) * norm_grad[s] for s in range(PAIR)], axis=0
    )
    back = scale * (
        grad
        - jnp.mean(grad, axis=-1, keepdims=True)
        - normal * jnp.mean(grad * normal, axis=-1, keepdims=True)
    )
    for t in range(QUART):
        ds[t] = back[:, t * chunk : (t + 1) * chunk]
    ds[y] = ds[y] + gs[...]
    for d in range(QUART):
        outs[d][...] = ds[lax.rem(y + d, QUART)].astype(BF16)


def weight_grad_kernel(scal, n0, n1, n2, g0, g1, g2, out, nscr, gscr, sems):
    c = scal[1]
    rows = n0.shape[0]

    def start(normed, grad):
        pltpu.make_async_copy(normed, nscr.at[0:rows], sems.at[0]).start()
        pltpu.make_async_copy(grad, gscr.at[0:rows], sems.at[1]).start()

    pltpu.make_async_copy(n1, nscr.at[rows : 2 * rows], sems.at[2]).start()
    pltpu.make_async_copy(g1, gscr.at[rows : 2 * rows], sems.at[3]).start()

    @pl.when(scal[2] == 0)
    def _():
        start(n0, g0)

    @pl.when(scal[2] != 0)
    def _():
        start(n2, g2)

    pltpu.make_async_copy(n0, nscr.at[0:rows], sems.at[0]).wait()
    pltpu.make_async_copy(g0, gscr.at[0:rows], sems.at[1]).wait()
    pltpu.make_async_copy(n1, nscr.at[rows : 2 * rows], sems.at[2]).wait()
    pltpu.make_async_copy(g1, gscr.at[rows : 2 * rows], sems.at[3]).wait()
    cores, depth, halves, share, _ = out.shape
    width = nscr.shape[1]
    per = 384
    groups = per // share
    right = gscr[...]
    for t in range(width // per):
        value = tn(nscr[:, t * per : (t + 1) * per], right).astype(BF16)
        for u in range(groups):
            at = t * groups + u
            core = at % cores
            half, z = divmod(at // cores, depth)
            where = lax.rem(core + c, cores)
            out[where, z, half] = value[u * share : (u + 1) * share]


def shards(latents, out_grad, w_qkv, mod_table, timesteps, text_len):
    y = lax.axis_index("y")
    p = lax.axis_index("xl")
    half = lax.axis_index("xh")
    core = lax.axis_index("c")
    halves = lax.axis_size("xh")
    depth = lax.axis_size("z")
    cores = lax.axis_size("c")
    count, _, seq, width = latents.shape
    share = w_qkv.shape[1]
    chunk = width // QUART
    cols = 3 * chunk
    rows = PAIR * seq
    nj = BLOCKS // 2
    levels = mod_table.shape[1]

    def swap(value, axis):
        return lax.ppermute(value, axis, [(0, 1), (1, 0)])

    quarters = w_qkv[0].reshape(share, 3, QUART, chunk)
    quarters = quarters.transpose(2, 0, 1, 3).reshape(QUART, share, cols)
    mine = lax.all_to_all(quarters, "y", 0, 0)
    if halves == 2:
        other = swap(mine, "xh")
        both = jnp.stack(
            [jnp.where(half == 0, mine, other), jnp.where(half == 0, other, mine)], axis=1
        )
    else:
        both = mine[:, None]
    pieces = []
    for j in range(nj):
        own = lax.all_gather(both[j], "z", axis=0)
        pieces.append((own, swap(own, "c")))

    onehot = (timesteps[:, 0][:, None] == jnp.arange(levels, dtype=jnp.int32)[None, :]).astype(F32)
    table, _ = lax.optimization_barrier((mod_table, mine))
    modulations = jnp.dot(
        onehot, table[0].reshape(levels, 3 * width), precision=lax.Precision.HIGHEST
    ).reshape(count, 3, width)
    mods = lax.all_gather(modulations, "y", axis=0)
    gates = lax.dynamic_slice_in_dim(mods[:, :, 2:3, :], y * chunk, chunk, axis=3)
    scal = jnp.concatenate(
        [jnp.stack([y, core, p]).astype(jnp.int32), text_len[:, 0].astype(jnp.int32)]
    )
    entering = latents.reshape(count // PAIR, rows, width)
    leaving = lax.dynamic_slice_in_dim(
        out_grad.reshape(count // PAIR, rows, width), y * chunk, chunk, axis=2
    )

    routes = [
        [
            (yy * 2 + pp, ((yy + d) % QUART) * 2 + (1 - pp))
            for yy in range(QUART)
            for pp in range(2)
        ]
        for d in range(QUART)
    ]

    def send(parts):
        return [lax.ppermute(parts[d], ("y", "xl"), routes[d]) for d in range(QUART)]

    wscr = pltpu.VMEM((halves, depth, cores, share, cols), BF16)
    params = pltpu.CompilerParams(vmem_limit_bytes=40 * 1024 * 1024)

    def held(k):
        first, second = min(k // 2, nj - 1), max((k - 1) // 2, 0)
        if first == second:
            return pieces[first]
        return pieces[first] + pieces[second]

    def shape(cols, kind):
        return jax.ShapeDtypeStruct((rows, cols), kind)

    steps = BLOCKS + 1
    saved = []
    received = None
    for k in range(steps):
        if k == 0:
            ins = [entering[0]]
        elif k == 1:
            ins = [entering[1]] + received
        else:
            ins = received
        weights = held(k)
        sending = k < steps - 1
        outs = [shape(width, BF16), shape(width, BF16), shape(cols, F32)]
        if sending:
            outs = [shape(chunk, BF16)] + outs
        result = pl.pallas_call(
            functools.partial(forward_kernel, k, len(ins), len(weights), sending),
            out_shape=outs,
            in_specs=[SM] + [VM] * (len(ins) + 2) + [ANY] * len(weights),
            out_specs=[VM] * len(outs),
            scratch_shapes=[wscr, pltpu.VMEM((QUART, rows, chunk), BF16), pltpu.SemaphoreType.DMA],
            compiler_params=params,
            name="forward_step",
        )(scal, *ins, mods, gates, *weights)
        if sending:
            received = send([result[0]] * QUART)
            result = result[1:]
        saved.append(result)

    lows = [None] * steps
    sums = [None] * nj
    received = None
    for k in reversed(range(steps)):
        if k == steps - 1:
            ins = [leaving[1]]
        elif k == steps - 2:
            ins = [leaving[0]] + received
        else:
            ins = received
        weights = held(k)
        sending = k > 0
        outs = [shape(chunk, BF16)] * (QUART * sending) + [shape(cols, BF16)]
        hidden, _, projected = saved[k]
        result = pl.pallas_call(
            functools.partial(backward_kernel, k, len(ins), len(weights), sending),
            out_shape=outs,
            in_specs=[SM] + [VM] * (len(ins) + 4) + [ANY] * len(weights),
            out_specs=[VM] * len(outs),
            scratch_shapes=[
                wscr,
                pltpu.VMEM((rows, chunk), F32),
                pltpu.VMEM((rows, cols), F32),
                pltpu.VMEM((QUART, rows, chunk), F32),
                pltpu.SemaphoreType.DMA,
            ],
            compiler_params=params,
            name="backward_step",
        )(scal, *ins, mods, gates, hidden, projected, *weights)
        lows[k] = result[-1]
        if sending:
            received = send(result[:-1])
        if k % 2 == 0 and k < steps - 1:
            j = k // 2
            partial = pl.pallas_call(
                weight_grad_kernel,
                out_shape=jax.ShapeDtypeStruct((cores, depth, halves, share, cols), BF16),
                in_specs=[SM] + [ANY] * 6,
                out_specs=VM,
                scratch_shapes=[
                    pltpu.VMEM((2 * rows, width), BF16),
                    pltpu.VMEM((2 * rows, cols), BF16),
                    pltpu.SemaphoreType.DMA((4,)),
                ],
                compiler_params=params,
                cost_estimate=pl.CostEstimate(
                    flops=4 * rows * width * cols,
                    bytes_accessed=4 * width * cols,
                    transcendentals=0,
                ),
                name="weight_grad",
            )(scal, *[saved[k + i][1] for i in range(3)], *[lows[k + i] for i in range(3)])
            chip = partial[0] + swap(partial[1], "c")
            ring = lax.psum_scatter(chip, "z", scatter_dimension=0)
            if halves == 2:
                there = lax.dynamic_index_in_dim(ring, 1 - half, 0, keepdims=False)
                here = lax.dynamic_index_in_dim(ring, half, 0, keepdims=False)
                sums[j] = (here.astype(F32) + swap(there, "xh").astype(F32)).astype(BF16)
            else:
                sums[j] = ring[0]
    grads = lax.all_to_all(jnp.stack(sums), "y", 0, 0)
    grads = grads.reshape(QUART, share, 3, chunk).transpose(1, 2, 0, 3)
    return grads.reshape(1, share, 3 * width).astype(F32)


def solution(mesh):
    fine = Mesh(mesh.devices.reshape(4, 2, 2, 8, 2), ("y", "xl", "xh", "z", "c"))
    pipe = ("y", "xl")
    dp = ("xh", "z", "c")
    return jax.shard_map(
        shards,
        mesh=fine,
        in_specs=(
            P(None, dp, None, None),
            P(None, dp, None, None),
            P(pipe, dp, None),
            P(pipe, None, None, None),
            P(None, dp),
            P(None, dp),
        ),
        out_specs=P(pipe, dp, None),
        check_vma=False,
    )
```

time: 984 us -> 619 us (0.63)
  waiting for transfers between devices: 632 us -> 285 us
  matrix products: 97.5 us -> 0.3 us
  Pallas kernels: 0 us -> 90.3 us
  other arithmetic: 70.1 us -> 10.8 us
  blocking collectives: 0 us -> 35.5 us
  starting transfers between devices: 129 us -> 141 us
    ppermute x22 -> x77, waiting for transfers between devices: 306 us -> 92.9 us  [the longest x64 62.2 us: send(): lax.ppermute(parts[d], ('y', 'xl'), routes[d])]
    reduce_scatter x1 -> x4, waiting for transfers between devices: 198 us -> 27.4 us  [shards(): ring = lax.psum_scatter(chip, 'z', scatter_dimension=0)]
    dot_general x38 -> x1, matrix products: 97.5 us -> 0.3 us  [shards(): jnp.dot(onehot, table[0].reshape(levels, 3 * width), precision=lax.Precis...]
    pallas_call x0 -> x22, Pallas kernels: none -> 90.3 us  [the longest x9 43.2 us: shards(): pl.pallas_call(functools.partial(backward_kernel, k, len(ins), len(weight...]
    all_gather x1 -> x4, waiting for transfers between devices: 128 us -> 163 us  [shards(): own = lax.all_gather(both[j], 'z', axis=0)]
    scatter x12 -> x0, other arithmetic: 26.2 us -> none  [the longest x4 10.3 us: backward_compute(): update = kept.at[slot_index].set(proj_low)]
    all_to_all x0 -> x2, blocking collectives: none -> 22.6 us  [the longest x1 11.9 us: shards(): mine = lax.all_to_all(quarters, 'y', 0, 0)]
    unnamed x1 -> x126, local copies, waits for them, and re-layouts: 1.17 us -> 20.6 us
  transfers between devices with their start and end apart: 24 -> 85, of which waited for: 24 -> 48; matrix products, arithmetic and copies ran while one was open for 0% -> 2% of each run, Pallas kernels for 0% -> 10%
where the time goes in v1:
time: 619 us; the launch traced here: 608 us
  waiting for transfers between devices  285 us (46%)
  starting transfers between devices  141 us (23%)
  Pallas kernels  90.3 us (15%)
  blocking collectives  35.5 us (6%)
  local copies, waits for them, and re-layouts  30.1 us (5%)
  between operations  14.8 us (2%)
  other arithmetic  10.8 us (2%)
    all_gather x4, waiting for transfers between devices, shards(): own = lax.all_gather(both[j], 'z', axis=0)  163 us
    ppermute x64, starting transfers between devices, send(): lax.ppermute(parts[d], ('y', 'xl'), routes[d])  129 us
    ppermute x64, waiting for transfers between devices, send(): lax.ppermute(parts[d], ('y', 'xl'), routes[d])  62.2 us
    pallas_call x9, Pallas kernels, shards(): pl.pallas_call(functools.partial(backward_kernel, k, len(ins), len(weight...  43.2 us
    pallas_call x9, Pallas kernels, shards(): pl.pallas_call(functools.partial(forward_kernel, k, len(ins), len(weights...  36.2 us
    ppermute x13, waiting for transfers between devices, swap(): return lax.ppermute(value, axis, [(0, 1), (1, 0)])  30.7 us
    reduce_scatter x4, waiting for transfers between devices, shards(): ring = lax.psum_scatter(chip, 'z', scatter_dimension=0)  27.4 us
    unnamed x126, local copies, waits for them, and re-layouts  20.6 us
  transfers between devices with their start and end apart: 85, of which 48 were waited for; matrix products, arithmetic and copies ran while one was open for 2% of the time, Pallas kernels for 10%

profile of v1, /device:TPU:8, one launch (start us, length us, event | category | flops | bytes accessed | tf_op | source)
XLA Modules:
  0.0 608.0 jit_solution(7657031162809309646)
XLA Ops:
  8.3 11.9 %all_to_all.10 = bf16[4,48,1152]{2,1,0:T(8,128)(2,1)S(1)} all-to-all(bf16[4,48,1152]{2,1,0:T(8,128)(2,1)S(1)} %reshape.104), channel_id=1, replica_groups=mesh['y'=4,'xl'=2,'xh'=2,'z'=8,'c'=2] {'y'}, dimensions={0} | all-to-all | bytes 884736 | tf_op jit(solution)/shard_map/all_to_all | solution.py:315
  23.1 8.9 %collective-permute-done = bf16[4,48,1152]{2,1,0:T(8,128)(2,1)S(1)} collective-permute-done((bf16[4,48,1152]{2,1,0:T(8,128)(2,1)S(1)}, bf16[4,48,1152]{2,1,0:T(8,128)(2,1)S(1)}, u32[]{:S(2)}, u32[]{:S(2)}) %collective-permute-start) | collective-permute-done | bytes 442400 | tf_op jit(solution)/shard_map/ppermute | solution.py:311
  35.2 40.4 %all-gather.6.cloned.1.call-done.refs_3_.refs_7_.refs_8_.refs_10_ = bf16[8,2,48,1152]{3,2,1,0:T(8,128)(2,1)} async-done(((bf16[1,2,48,1152]{3,2,1,0:T(8,128)(2,1)}), bf16[8,2,48,1152]{3,2,1,0:T(8,128)(2,1)}) %all-gather.6.cloned.1.call-update) | async-done | bytes 1769488 | tf_op jit(solution)/shard_map/all_gather | solution.py:325
  75.7 40.9 %all-gather.8.cloned.1.call-done.refs_6_.refs_8_.refs_10_ = bf16[8,2,48,1152]{3,2,1,0:T(8,128)(2,1)} async-done(((bf16[1,2,48,1152]{3,2,1,0:T(8,128)(2,1)}), bf16[8,2,48,1152]{3,2,1,0:T(8,128)(2,1)}) %all-gather.8.cloned.1.call-update) | async-done | bytes 1769488 | tf_op jit(solution)/shard_map/all_gather | solution.py:325
  116.6 40.9 %all-gather.10.cloned.1.call-done.refs_6_.refs_8_.refs_10_ = bf16[8,2,48,1152]{3,2,1,0:T(8,128)(2,1)} async-done(((bf16[1,2,48,1152]{3,2,1,0:T(8,128)(2,1)}), bf16[8,2,48,1152]{3,2,1,0:T(8,128)(2,1)}) %all-gather.10.cloned.1.call-update) | async-done | bytes 1769488 | tf_op jit(solution)/shard_map/all_gather | solution.py:325
  157.5 40.8 %all-gather.12.cloned.1.call-done.refs_6_.refs_5_.refs_9_.refs_8_ = bf16[8,2,48,1152]{3,2,1,0:T(8,128)(2,1)} async-done(((bf16[1,2,48,1152]{3,2,1,0:T(8,128)(2,1)}), bf16[8,2,48,1152]{3,2,1,0:T(8,128)(2,1)}) %all-gather.12.cloned.1.call-update) | async-done | bytes 1769488 | tf_op jit(solution)/shard_map/all_gather | solution.py:325
  199.0 12.9 %all-gather = f32[16,3,1536]{2,1,0:T(4,128)S(1)} all-gather(f32[4,3,1536]{2,1,0:T(4,128)S(1)} %copy.25), channel_id=2, replica_groups=mesh['y'=4,'xl'=2,'xh'=2,'z'=8,'c'=2] {'y'}, dimensions={0}, use_global_device_ids=true | all-gather | bytes 368640 | tf_op jit(solution)/shard_map/all_gather | solution.py:333
  239.2 4.5 collective-permute-start.8
  290.2 11.1 %collective-permute-start.22 = (bf16[112,384]{1,0:T(8,128)(2,1)S(1)}, bf16[112,384]{1,0:T(8,128)(2,1)S(1)}, u32[]{:S(2)}, u32[]{:S(2)}) collective-permute-start(bf16[112,384]{1,0:T(8,128)(2,1)S(1)} %get-tuple-element.89), channel_id=1, source_target_pairs={{0,160},{32,128},{64,224},{96,192},{128,32},{160,0},{192,96},{224,... | collective-permute-start | bytes 258056 | tf_op jit(solution)/shard_map/ppermute | solution.py:353
  326.5 4.7 forward_step.15
  340.1 4.1 collective-permute-done.31.refs_2_
  345.7 4.4 forward_step.16
  365.4 5.1 backward_step.9
  380.5 4.7 backward_step.10
  396.1 5.1 backward_step.11
  425.0 5.2 backward_step.12
  440.8 4.9 backward_step.13
  461.6 4.1 collective-permute-done.55.refs_2_
  468.4 5.2 backward_step.14
  484.3 4.9 backward_step.15
  504.7 4.2 collective-permute-done.63.refs_2_
  509.9 5.2 backward_step.16
  552.1 27.4 %reduce-scatter.5.cloned.1.call-done = bf16[1,2,48,1152]{3,2,1,0:T(8,128)(2,1)} async-done(((bf16[8,2,48,1152]{3,2,1,0:T(8,128)(2,1)}), bf16[1,2,48,1152]{3,2,1,0:T(8,128)(2,1)}) %reduce-scatter.5.cloned.1.call-update) | async-done | bytes 221200 | tf_op jit(solution)/shard_map/reduce_scatter | solution.py:449
  587.8 10.8 %all_to_all.11 = bf16[4,48,1152]{2,1,0:T(8,128)(2,1)S(1)} all-to-all(bf16[4,48,1152]{2,1,0:T(8,128)(2,1)S(1)} %pad_maximum_fusion), channel_id=1, replica_groups=mesh['y'=4,'xl'=2,'xh'=2,'z'=8,'c'=2] {'y'}, dimensions={0} | all-to-all | bytes 884736 | tf_op jit(solution)/shard_map/all_to_all | solution.py:456
  (338 shorter events, 281.0 us)
Async XLA Ops:
  6.5 69.1 %all-gather.6.cloned.1.call-start = ((), (), s32[]{:S(2)}) async-start(), calls=%async_computation.6 | async-start | bytes 1990656 | tf_op jit(solution)/shard_map/all_gather | solution.py:325
  20.1 11.9 %collective-permute-start = (bf16[4,48,1152]{2,1,0:T(8,128)(2,1)S(1)}, bf16[4,48,1152]{2,1,0:T(8,128)(2,1)S(1)}, u32[]{:S(2)}, u32[]{:S(2)}) collective-permute-start(bf16[4,48,1152]{2,1,0:T(8,128)(2,1)S(1)} %all_to_all.10), channel_id=1, source_target_pairs={{0,16},{16,0},{1,17},{17,1},{2,18},{18,2},{3,19},{19,3},{4,20},{20... | collective-permute-start | bytes 1327112 | tf_op jit(solution)/shard_map/ppermute | solution.py:311
  33.1 83.4 %all-gather.8.cloned.1.call-start = ((), (), s32[]{:S(2)}) async-start(), calls=%async_computation.7 | async-start | bytes 1990656 | tf_op jit(solution)/shard_map/all_gather | solution.py:325
  33.9 123.6 %all-gather.10.cloned.1.call-start = ((), (), s32[]{:S(2)}) async-start(), calls=%async_computation.8 | async-start | bytes 1990656 | tf_op jit(solution)/shard_map/all_gather | solution.py:325
  34.6 163.6 %all-gather.12.cloned.1.call-start = ((), (), s32[]{:S(2)}) async-start(), calls=%async_computation.9 | async-start | bytes 1990656 | tf_op jit(solution)/shard_map/all_gather | solution.py:325
  35.2 502.1 %reduce-scatter.11.cloned.1.call-start = ((), (), s32[]{:S(2)}) async-start(), calls=%async_computation.13 | async-start | bytes 1990656 | tf_op jit(solution)/shard_map/reduce_scatter | solution.py:449
  75.7 136.4 %collective-permute-start.1 = (bf16[8,2,48,1152]{3,2,1,0:T(8,128)(2,1)}, bf16[8,2,48,1152]{3,2,1,0:T(8,128)(2,1)}, u32[]{:S(2)}, u32[]{:S(2)}) collective-permute-start(bf16[8,2,48,1152]{3,2,1,0:T(8,128)(2,1)} %all-gather.6.cloned.1.call-done.refs_3_.refs_7_.refs_8_.refs_10_), channel_id=1, source_target_pairs={{0,1},{1,0},{2,3},{3,2},{4,5},{5,4},{6,7},{7,6},{8,9},{9,8},{10,11... | collective-permute-start | bytes 5308424 | tf_op jit(solution)/shard_map/ppermute | solution.py:311
  116.6 122.6 %collective-permute-start.10 = (bf16[8,2,48,1152]{3,2,1,0:T(8,128)(2,1)}, bf16[8,2,48,1152]{3,2,1,0:T(8,128)(2,1)}, u32[]{:S(2)}, u32[]{:S(2)}) collective-permute-start(bf16[8,2,48,1152]{3,2,1,0:T(8,128)(2,1)} %all-gather.8.cloned.1.call-done.refs_6_.refs_8_.refs_10_), channel_id=1, source_target_pairs={{0,1},{1,0},{2,3},{3,2},{4,5},{5,4},{6,7},{7,6},{8,9},{9,8},{10,11... | collective-permute-start | bytes 5308424 | tf_op jit(solution)/shard_map/ppermute | solution.py:311
  157.5 119.9 %collective-permute-start.19 = (bf16[8,2,48,1152]{3,2,1,0:T(8,128)(2,1)}, bf16[8,2,48,1152]{3,2,1,0:T(8,128)(2,1)}, u32[]{:S(2)}, u32[]{:S(2)}) collective-permute-start(bf16[8,2,48,1152]{3,2,1,0:T(8,128)(2,1)} %all-gather.10.cloned.1.call-done.refs_6_.refs_8_.refs_10_), channel_id=1, source_target_pairs={{0,1},{1,0},{2,3},{3,2},{4,5},{5,4},{6,7},{7,6},{8,9},{9,8},{10,11... | collective-permute-start | bytes 5308424 | tf_op jit(solution)/shard_map/ppermute | solution.py:311
  198.3 123.9 %collective-permute-start.28 = (bf16[8,2,48,1152]{3,2,1,0:T(8,128)(2,1)}, bf16[8,2,48,1152]{3,2,1,0:T(8,128)(2,1)}, u32[]{:S(2)}, u32[]{:S(2)}) collective-permute-start(bf16[8,2,48,1152]{3,2,1,0:T(8,128)(2,1)} %all-gather.12.cloned.1.call-done.refs_6_.refs_5_.refs_9_.refs_8_), channel_id=1, source_target_pairs={{0,1},{1,0},{2,3},{3,2},{4,5},{5,4},{6,7},{7,6},{8,9},{9,8},{10,11... | collective-permute-start | bytes 5308424 | tf_op jit(solution)/shard_map/ppermute | solution.py:311
  287.3 17.0 %collective-permute-start.20 = (bf16[112,384]{1,0:T(8,128)(2,1)S(1)}, bf16[112,384]{1,0:T(8,128)(2,1)S(1)}, u32[]{:S(2)}, u32[]{:S(2)}) collective-permute-start(bf16[112,384]{1,0:T(8,128)(2,1)S(1)} %get-tuple-element.89), channel_id=1, source_target_pairs={{0,32},{32,0},{64,96},{96,64},{128,160},{160,128},{192,224},{224,1... | collective-permute-start | bytes 258056 | tf_op jit(solution)/shard_map/ppermute | solution.py:353
  288.0 16.3 %collective-permute-start.21 = (bf16[112,384]{1,0:T(8,128)(2,1)S(1)}, bf16[112,384]{1,0:T(8,128)(2,1)S(1)}, u32[]{:S(2)}, u32[]{:S(2)}) collective-permute-start(bf16[112,384]{1,0:T(8,128)(2,1)S(1)} %get-tuple-element.89), channel_id=1, source_target_pairs={{0,96},{32,64},{64,160},{96,128},{128,224},{160,192},{192,32},{224... | collective-permute-start | bytes 258056 | tf_op jit(solution)/shard_map/ppermute | solution.py:353
  290.2 15.5 %collective-permute-start.22 = (bf16[112,384]{1,0:T(8,128)(2,1)S(1)}, bf16[112,384]{1,0:T(8,128)(2,1)S(1)}, u32[]{:S(2)}, u32[]{:S(2)}) collective-permute-start(bf16[112,384]{1,0:T(8,128)(2,1)S(1)} %get-tuple-element.89), channel_id=1, source_target_pairs={{0,160},{32,128},{64,224},{96,192},{128,32},{160,0},{192,96},{224,... | collective-permute-start | bytes 258056 | tf_op jit(solution)/shard_map/ppermute | solution.py:353
  313.0 9.1 %collective-permute-start.24 = (bf16[112,384]{1,0:T(8,128)(2,1)S(1)}, bf16[112,384]{1,0:T(8,128)(2,1)S(1)}, u32[]{:S(2)}, u32[]{:S(2)}) collective-permute-start(bf16[112,384]{1,0:T(8,128)(2,1)S(1)} %get-tuple-element.90), channel_id=1, source_target_pairs={{0,32},{32,0},{64,96},{96,64},{128,160},{160,128},{192,224},{224,1... | collective-permute-start | bytes 258056 | tf_op jit(solution)/shard_map/ppermute | solution.py:353
  334.9 9.4 %collective-permute-start.31 = (bf16[112,384]{1,0:T(8,128)(2,1)}, bf16[112,384]{1,0:T(8,128)(2,1)S(1)}, u32[]{:S(2)}, u32[]{:S(2)}) collective-permute-start(bf16[112,384]{1,0:T(8,128)(2,1)} %get-tuple-element.91), channel_id=1, source_target_pairs={{0,160},{32,128},{64,224},{96,192},{128,32},{160,0},{192,96},{224,... | collective-permute-start | bytes 258056 | tf_op jit(solution)/shard_map/ppermute | solution.py:353
  350.2 8.4 %collective-permute-start.33 = (bf16[112,384]{1,0:T(8,128)(2,1)S(1)}, bf16[112,384]{1,0:T(8,128)(2,1)S(1)}, u32[]{:S(2)}, u32[]{:S(2)}) collective-permute-start(bf16[112,384]{1,0:T(8,128)(2,1)S(1)} %get-tuple-element.92), channel_id=1, source_target_pairs={{0,32},{32,0},{64,96},{96,64},{128,160},{160,128},{192,224},{224,1... | collective-permute-start | bytes 258056 | tf_op jit(solution)/shard_map/ppermute | solution.py:353
  352.9 8.9 %collective-permute-start.35 = (bf16[112,384]{1,0:T(8,128)(2,1)S(1)}, bf16[112,384]{1,0:T(8,128)(2,1)S(1)}, u32[]{:S(2)}, u32[]{:S(2)}) collective-permute-start(bf16[112,384]{1,0:T(8,128)(2,1)S(1)} %get-tuple-element.92), channel_id=1, source_target_pairs={{0,160},{32,128},{64,224},{96,192},{128,32},{160,0},{192,96},{224,... | collective-permute-start | bytes 258056 | tf_op jit(solution)/shard_map/ppermute | solution.py:353
  409.5 131.7 %reduce-scatter.9.cloned.1.call-start = ((), (), s32[]{:S(2)}) async-start(), calls=%async_computation.12 | async-start | bytes 1990656 | tf_op jit(solution)/shard_map/reduce_scatter | solution.py:449
  411.9 9.4 %collective-permute-start.47 = (bf16[112,384]{1,0:T(8,128)(2,1)}, bf16[112,384]{1,0:T(8,128)(2,1)S(1)}, u32[]{:S(2)}, u32[]{:S(2)}) collective-permute-start(bf16[112,384]{1,0:T(8,128)(2,1)} %copy-done.52), channel_id=1, source_target_pairs={{0,160},{32,128},{64,224},{96,192},{128,32},{160,0},{192,96},{224,... | collective-permute-start | bytes 258056 | tf_op jit(solution)/shard_map/ppermute | solution.py:353
  454.0 95.5 %reduce-scatter.7.cloned.1.call-start = ((), (), s32[]{:S(2)}) async-start(), calls=%async_computation.11 | async-start | bytes 1990656 | tf_op jit(solution)/shard_map/reduce_scatter | solution.py:449
  456.3 9.5 %collective-permute-start.55 = (bf16[112,384]{1,0:T(8,128)(2,1)}, bf16[112,384]{1,0:T(8,128)(2,1)S(1)}, u32[]{:S(2)}, u32[]{:S(2)}) collective-permute-start(bf16[112,384]{1,0:T(8,128)(2,1)} %copy-done.53), channel_id=1, source_target_pairs={{0,160},{32,128},{64,224},{96,192},{128,32},{160,0},{192,96},{224,... | collective-permute-start | bytes 258056 | tf_op jit(solution)/shard_map/ppermute | solution.py:353
  497.3 82.2 %reduce-scatter.5.cloned.1.call-start = ((), (), s32[]{:S(2)}) async-start(), calls=%async_computation.10 | async-start | bytes 1990656 | tf_op jit(solution)/shard_map/reduce_scatter | solution.py:449
  499.6 9.2 %collective-permute-start.63 = (bf16[112,384]{1,0:T(8,128)(2,1)S(1)}, bf16[112,384]{1,0:T(8,128)(2,1)S(1)}, u32[]{:S(2)}, u32[]{:S(2)}) collective-permute-start(bf16[112,384]{1,0:T(8,128)(2,1)S(1)} %get-tuple-element.133), channel_id=1, source_target_pairs={{0,160},{32,128},{64,224},{96,192},{128,32},{160,0},{192,96},{224,... | collective-permute-start | bytes 258056 | tf_op jit(solution)/shard_map/ppermute | solution.py:353
  550.4 33.1 %collective-permute-start.72 = (bf16[48,1152]{1,0:T(8,128)(2,1)S(1)}, bf16[48,1152]{1,0:T(8,128)(2,1)S(1)}, u32[]{:S(2)}, u32[]{:S(2)}) collective-permute-start(bf16[48,1152]{1,0:T(8,128)(2,1)S(1)} %dynamic-slice_bitcast_fusion.2), channel_id=1, source_target_pairs={{0,16},{16,0},{1,17},{17,1},{2,18},{18,2},{3,19},{19,3},{4,20},{20... | collective-permute-start | bytes 331784 | tf_op jit(solution)/shard_map/ppermute | solution.py:311
  (124 other events, 1623.5 us)
Sparse Core Ops, SparseCore 0:
  33.3 42.3 all-gather.5
  77.5 39.0 all-gather.7
  118.4 39.0 all-gather.9
  159.1 39.0 all-gather.11
  409.6 39.6 reduce-scatter.10
  454.1 39.3 reduce-scatter.8
  497.4 39.6 reduce-scatter.6
  539.7 39.7 reduce-scatter.4

commit v2 on v1

--- a/solution.py
+++ b/solution.py
@@ -17,6 +17,7 @@
 PAIR = 2
 F32 = jnp.float32
 BF16 = jnp.bfloat16
+VMEM_LIMIT = 16 * 1024 * 1024
 VM = pl.BlockSpec(memory_space=pltpu.VMEM)
 SM = pl.BlockSpec(memory_space=pltpu.SMEM)
 ANY = pl.BlockSpec(memory_space=pl.ANY)
@@ -26,17 +27,19 @@
     p = scal[2]
     j = lax.max((k - p + 2) // 2 - 1, 0)
     j = lax.min(j, BLOCKS // 2 - 1)
-    return lax.rem(k + p, 2), j
-
-
-def fetch_weights(scal, pieces, wscr, sem):
+    return lax.rem(k + p, 2), j, lax.rem(scal[0] + QUART - j, QUART)
+
+
+def fetch_weights(scal, j, pieces, wscr, sem):
     c = scal[1]
     halves = wscr.shape[0]
+    inner = lax.rem(j, 2)
 
     def start(own, other):
         for t in range(halves):
-            pltpu.make_async_copy(own.at[:, t], wscr.at[t, :, c], sem).start()
-            pltpu.make_async_copy(other.at[:, t], wscr.at[t, :, 1 - c], sem).start()
+            where = lax.rem(t + scal[3], halves)
+            pltpu.make_async_copy(own.at[:, inner, t], wscr.at[where, :, c], sem).start()
+            pltpu.make_async_copy(other.at[:, inner, t], wscr.at[where, :, 1 - c], sem).start()
 
     if len(pieces) == 2:
         start(*pieces)
@@ -99,50 +102,54 @@
     return weights / jnp.sum(weights, axis=-1, keepdims=True)
 
 
+def load_hidden(scal, ins, hs):
+    y = scal[0]
+    chunk = hs.shape[2]
+
+    def from_whole(ref):
+        for t in range(QUART):
+            hs[t] = ref[:, t * chunk : (t + 1) * chunk]
+
+    def from_chunks(parts):
+        for d in range(QUART):
+            hs[lax.rem(y + QUART - d, QUART)] = parts[d][...]
+
+    if len(ins) == 1:
+        from_whole(ins[0])
+    elif len(ins) == QUART:
+        from_chunks(ins)
+    else:
+
+        @pl.when(scal[2] == 0)
+        def _():
+            from_whole(ins[0])
+
+        @pl.when(scal[2] != 0)
+        def _():
+            from_chunks(ins[1:])
+
+    return jnp.concatenate([hs[t].astype(F32) for t in range(QUART)], axis=1)
+
+
 def forward_kernel(k, n_in, n_w, send, scal, *refs):
     ins, refs = refs[:n_in], refs[n_in:]
     mods, gates = refs[:2]
     pieces, refs = refs[2 : 2 + n_w], refs[2 + n_w :]
     if send:
         out_ref, refs = refs[0], refs[1:]
-    hidden_ref, normed_ref, proj_ref, wscr, hs, sem = refs
-    fetch_weights(scal, pieces, wscr, sem)
+    normed_ref, proj_ref, wscr, hs, sem = refs
     y = scal[0]
-    micro, j = place(scal, k)
+    micro, j, slot = place(scal, k)
+    fetch_weights(scal, j, pieces, wscr, sem)
     chunk = hs.shape[2]
-
-    def from_whole(ref):
-        for t in range(QUART):
-            hs[t] = ref[:, t * chunk : (t + 1) * chunk]
-
-    def from_chunks(parts):
-        for d in range(QUART):
-            hs[lax.rem(y + QUART - d, QUART)] = parts[d][...]
-
-    if n_in == 1:
-        from_whole(ins[0])
-    elif n_in == QUART:
-        from_chunks(ins)
-    else:
-
-        @pl.when(scal[2] == 0)
-        def _():
-            from_whole(ins[0])
-
-        @pl.when(scal[2] != 0)
-        def _():
-            from_chunks(ins[1:])
-
-    for t in range(QUART):
-        hidden_ref[:, t * chunk : (t + 1) * chunk] = hs[t]
-    rows, width = hidden_ref.shape
+    rows, width = normed_ref.shape
     seq = rows // PAIR
-    normal, _ = standardize(hidden_ref[...].astype(F32))
+    normal, _ = standardize(load_hidden(scal, ins, hs))
     normal = normal.reshape(PAIR, seq, width)
     normed = jnp.concatenate(
         [
-            (1.0 + mods[j, PAIR * micro + s, 1:2, :]) * normal[s]
-            + mods[j, PAIR * micro + s, 0:1, :]
+            (1.0 + mods[slot, PAIR * micro + s, 1:2, :]) * normal[s]
+            + mods[slot, PAIR * micro + s, 0:1, :]
             for s in range(PAIR)
         ],
         axis=0,
@@ -159,7 +166,7 @@
         return
     own = hs[y].astype(F32)
     for s in range(PAIR):
-        length = scal[3 + PAIR * micro + s]
+        length = scal[4 + PAIR * micro + s]
         r = slice(s * seq, (s + 1) * seq)
         mixed = []
         for h in range(chunk // HDIM):
@@ -169,33 +176,32 @@
             v = proj_ref[r, 2 * chunk + lo : 2 * chunk + lo + HDIM]
             mixed.append(nn(weights_of(q, key, length), v))
         mixture = jnp.concatenate(mixed, axis=1)
-        gate = gates[j, PAIR * micro + s]
+        gate = gates[slot, PAIR * micro + s]
         hs_rows = own[r] + gate * mixture
         if s == 0:
             first = hs_rows
     out_ref[...] = jnp.concatenate([first, hs_rows], axis=0).astype(BF16)
 
 
-def backward_kernel(k, n_in, n_w, send, scal, *refs):
+def backward_kernel(k, n_in, n_hid, n_w, send, scal, *refs):
     ins, refs = refs[:n_in], refs[n_in:]
-    mods, gates, hidden_ref, proj_ref = refs[:4]
-    pieces, refs = refs[4 : 4 + n_w], refs[4 + n_w :]
+    hidden, refs = refs[:n_hid], refs[n_hid:]
+    mods, gates, proj_ref = refs[:3]
+    pieces, refs = refs[3 : 3 + n_w], refs[3 + n_w :]
     outs, refs = refs[: QUART * send], refs[QUART * send :]
-    low_ref, wscr, gs, dp, ds, sem = refs
+    low_ref, wscr, hs, gs, dp, ds, sem = refs
+    y = scal[0]
+    micro, j, slot = place(scal, k)
     if send:
-        fetch_weights(scal, pieces, wscr, sem)
-    y = scal[0]
-    micro, j = place(scal, k)
-    rows, width = hidden_ref.shape
-    chunk = width // QUART
+        fetch_weights(scal, j, pieces, wscr, sem)
+    rows, chunk = gs.shape
+    width = chunk * QUART
     seq = rows // PAIR
 
     def total(parts):
         gs[...] = sum([part[...].astype(F32) for part in parts[1:]], parts[0][...].astype(F32))
 
-    if n_in == 1:
-        total(ins)
-    elif n_in == QUART:
+    if n_in in (1, QUART):
         total(ins)
     else:
 
@@ -209,12 +215,12 @@
 
     root = 1.0 / math.sqrt(HDIM)
     for s in range(PAIR):
-        length = scal[3 + PAIR * micro + s]
+        length = scal[4 + PAIR * micro + s]
         r = slice(s * seq, (s + 1) * seq)
         for h in range(chunk // HDIM):
             lo = h * HDIM
             c = slice(lo, lo + HDIM)
-            gate = gates[j, PAIR * micro + s, :, c]
+            gate = gates[slot, PAIR * micro + s, :, c]
             dmix = gs[r, c] * gate
             q, rq = unit(proj_ref[r, lo : lo + HDIM])
             key, rk = unit(proj_ref[r, chunk + lo : chunk + lo + HDIM])
@@ -233,13 +239,13 @@
     low_ref[...] = low
     if not send:
         return
-    normal, scale = standardize(hidden_ref[...].astype(F32))
+    normal, scale = standardize(load_hidden(scal, hidden, hs))
     await_weights(wscr, sem)
     halves = wscr.shape[0]
     norm_grad = jnp.concatenate([nt(low, half_weights(wscr, t)) for t in range(halves)], axis=1)
     norm_grad = norm_grad.reshape(PAIR, seq, width)
     grad = jnp.concatenate(
-        [(1.0 + mods[j, PAIR * micro + s, 1:2, :]) * norm_grad[s] for s in range(PAIR)], axis=0
+        [(1.0 + mods[slot, PAIR * micro + s, 1:2, :]) * norm_grad[s] for s in range(PAIR)], axis=0
     )
     back = scale * (
         grad
@@ -310,30 +316,60 @@
     def swap(value, axis):
         return lax.ppermute(value, axis, [(0, 1), (1, 0)])
 
+    turns = [
+        [
+            [
+                (yy * halves + hh, ((yy + dy) % QUART) * halves + (hh + dx) % halves)
+                for yy in range(QUART)
+                for hh in range(halves)
+            ]
+            for dy in range(QUART)
+        ]
+        for dx in range(halves)
+    ]
+
+    def turn(value, dx, dy):
+        if dx == 0 and dy == 0:
+            return value
+        return lax.ppermute(value, ("y", "xh"), turns[dx][dy])
+
+    def pick(stack, index):
+        return lax.dynamic_index_in_dim(stack, index, 0, keepdims=False)
+
     quarters = w_qkv[0].reshape(share, 3, QUART, chunk)
     quarters = quarters.transpose(2, 0, 1, 3).reshape(QUART, share, cols)
-    mine = lax.all_to_all(quarters, "y", 0, 0)
-    if halves == 2:
-        other = swap(mine, "xh")
-        both = jnp.stack(
-            [jnp.where(half == 0, mine, other), jnp.where(half == 0, other, mine)], axis=1
+    leaves = [pick(quarters, lax.rem(y + dy, QUART)) for dy in range(QUART)]
+    arrived = [
+        jnp.stack([turn(leaves[dy], dx, dy) for dy in range(QUART)]) for dx in range(halves)
+    ]
+    pieces = []
+    for g in range(nj // 2):
+        part = jnp.stack(
+            [
+                jnp.stack(
+                    [pick(arrived[dx], lax.rem(y + QUART - j, QUART)) for dx in range(halves)]
+                )
+                for j in (2 * g, 2 * g + 1)
+            ]
         )
-    else:
-        both = mine[:, None]
-    pieces = []
-    for j in range(nj):
-        own = lax.all_gather(both[j], "z", axis=0)
+        own = lax.all_gather(part, "z", axis=0)
         pieces.append((own, swap(own, "c")))
 
     onehot = (timesteps[:, 0][:, None] == jnp.arange(levels, dtype=jnp.int32)[None, :]).astype(F32)
-    table, _ = lax.optimization_barrier((mod_table, mine))
+    table, _ = lax.optimization_barrier((mod_table, arrived[0]))
     modulations = jnp.dot(
         onehot, table[0].reshape(levels, 3 * width), precision=lax.Precision.HIGHEST
     ).reshape(count, 3, width)
-    mods = lax.all_gather(modulations, "y", axis=0)
+    mods = jnp.stack(
+        [modulations]
+        + [
+            lax.ppermute(modulations, "y", [(yy, (yy + dy) % QUART) for yy in range(QUART)])
+            for dy in range(1, QUART)
+        ]
+    )
     gates = lax.dynamic_slice_in_dim(mods[:, :, 2:3, :], y * chunk, chunk, axis=3)
     scal = jnp.concatenate(
-        [jnp.stack([y, core, p]).astype(jnp.int32), text_len[:, 0].astype(jnp.int32)]
+        [jnp.stack([y, core, p, half]).astype(jnp.int32), text_len[:, 0].astype(jnp.int32)]
     )
     entering = latents.reshape(count // PAIR, rows, width)
     leaving = lax.dynamic_slice_in_dim(
@@ -353,10 +389,11 @@
         return [lax.ppermute(parts[d], ("y", "xl"), routes[d]) for d in range(QUART)]
 
     wscr = pltpu.VMEM((halves, depth, cores, share, cols), BF16)
-    params = pltpu.CompilerParams(vmem_limit_bytes=40 * 1024 * 1024)
+    params = pltpu.CompilerParams(vmem_limit_bytes=VMEM_LIMIT)
 
     def held(k):
         first, second = min(k // 2, nj - 1), max((k - 1) // 2, 0)
+        first, second = first // 2, second // 2
         if first == second:
             return pieces[first]
         return pieces[first] + pieces[second]
@@ -376,7 +413,7 @@
             ins = received
         weights = held(k)
         sending = k < steps - 1
-        outs = [shape(width, BF16), shape(width, BF16), shape(cols, F32)]
+        outs = [shape(width, BF16), shape(cols, F32)]
         if sending:
             outs = [shape(chunk, BF16)] + outs
         result = pl.pallas_call(
@@ -391,7 +428,7 @@
         if sending:
             received = send([result[0]] * QUART)
             result = result[1:]
-        saved.append(result)
+        saved.append((ins, *result))
 
     lows = [None] * steps
     sums = [None] * nj
@@ -407,13 +444,17 @@
         sending = k > 0
         outs = [shape(chunk, BF16)] * (QUART * sending) + [shape(cols, BF16)]
         hidden, _, projected = saved[k]
+        sources = len(ins) + len(hidden) + 3
         result = pl.pallas_call(
-            functools.partial(backward_kernel, k, len(ins), len(weights), sending),
+            functools.partial(
+                backward_kernel, k, len(ins), len(hidden), len(weights), sending
+            ),
             out_shape=outs,
-            in_specs=[SM] + [VM] * (len(ins) + 4) + [ANY] * len(weights),
+            in_specs=[SM] + [VM] * sources + [ANY] * len(weights),
             out_specs=[VM] * len(outs),
             scratch_shapes=[
                 wscr,
+                pltpu.VMEM((QUART, rows, chunk), BF16),
                 pltpu.VMEM((rows, chunk), F32),
                 pltpu.VMEM((rows, cols), F32),
                 pltpu.VMEM((QUART, rows, chunk), F32),
@@ -421,12 +462,15 @@
             ],
             compiler_params=params,
             name="backward_step",
-        )(scal, *ins, mods, gates, hidden, projected, *weights)
+        )(scal, *ins, *hidden, mods, gates, projected, *weights)
         lows[k] = result[-1]
         if sending:
             received = send(result[:-1])
         if k % 2 == 0 and k < steps - 1:
             j = k // 2
+            factors = [saved[k + i][1] for i in range(3)] + [lows[k + i] for i in range(3)]
+            if sending:
+                factors, received[0] = lax.optimization_barrier((factors, received[0]))
             partial = pl.pallas_call(
                 weight_grad_kernel,
                 out_shape=jax.ShapeDtypeStruct((cores, depth, halves, share, cols), BF16),
@@ -444,18 +488,18 @@
                     transcendentals=0,
                 ),
                 name="weight_grad",
-            )(scal, *[saved[k + i][1] for i in range(3)], *[lows[k + i] for i in range(3)])
+            )(scal, *factors)
             chip = partial[0] + swap(partial[1], "c")
-            ring = lax.psum_scatter(chip, "z", scatter_dimension=0)
-            if halves == 2:
-                there = lax.dynamic_index_in_dim(ring, 1 - half, 0, keepdims=False)
-                here = lax.dynamic_index_in_dim(ring, half, 0, keepdims=False)
-                sums[j] = (here.astype(F32) + swap(there, "xh").astype(F32)).astype(BF16)
-            else:
-                sums[j] = ring[0]
-    grads = lax.all_to_all(jnp.stack(sums), "y", 0, 0)
-    grads = grads.reshape(QUART, share, 3, chunk).transpose(1, 2, 0, 3)
-    return grads.reshape(1, share, 3 * width).astype(F32)
+            sums[j] = lax.psum_scatter(chip, "z", scatter_dimension=0)
+    sums = jnp.stack(sums)
+    finals = []
+    for dy in range(QUART):
+        block = pick(sums, lax.rem(y + dy, QUART))
+        here = [turn(pick(block, lax.rem(half + dx, halves)), dx, dy) for dx in range(halves)]
+        finals.append(sum([part.astype(F32) for part in here]).reshape(share, 3, chunk))
+    finals = jnp.stack(finals)
+    grads = jnp.stack([pick(finals, lax.rem(y + QUART - q, QUART)) for q in range(QUART)], axis=2)
+    return grads.reshape(1, share, 3 * width)
 
 
 def solution(mesh):

time: 619 us -> 632 us (1.021)
  waiting for transfers between devices: 285 us -> 322 us
  blocking collectives: 35.5 us -> 0 us
  starting transfers between devices: 141 us -> 149 us
    reduce_scatter x4, waiting for transfers between devices: 27.4 us -> 136 us  [shards(): sums[j] = lax.psum_scatter(chip, 'z', scatter_dimension=0)]
    all_gather x4 -> x2, waiting for transfers between devices: 163 us -> 98.6 us  [shards(): own = lax.all_gather(part, 'z', axis=0)]
    ppermute x0 -> x17, starting transfers between devices: none -> 33.6 us  [the longest x14 28.9 us: turn(): return lax.ppermute(value, ('y', 'xh'), turns[dx][dy])]
    all_to_all x2 -> x0, blocking collectives: 22.6 us -> none  [the longest x1 11.9 us: shards(): mine = lax.all_to_all(quarters, 'y', 0, 0)]
    ppermute x13 -> x6, waiting for transfers between devices: 30.7 us -> 14.3 us  [swap(): return lax.ppermute(value, axis, [(0, 1), (1, 0)])]
    ppermute x64, starting transfers between devices: 129 us -> 114 us  [send(): lax.ppermute(parts[d], ('y', 'xl'), routes[d])]
    all_gather x1 -> x0, blocking collectives: 12.9 us -> none  [shards(): mods = lax.all_gather(modulations, 'y', axis=0)]
    ppermute x13 -> x6, starting transfers between devices: 11.9 us -> 0.95 us  [swap(): return lax.ppermute(value, axis, [(0, 1), (1, 0)])]
  transfers between devices with their start and end apart: 85 -> 93, of which waited for: 48 -> 60; matrix products, arithmetic and copies ran while one was open for 2% -> 2% of each run, Pallas kernels for 10% -> 4%
where the time goes in v2:
time: 632 us; the launch traced here: 622 us
  waiting for transfers between devices  322 us (51%)
  starting transfers between devices  149 us (24%)
  Pallas kernels  93.3 us (15%)
  local copies, waits for them, and re-layouts  33.5 us (5%)
  between operations  15.3 us (2%)
  other arithmetic  8.95 us (1%)
    reduce_scatter x4, waiting for transfers between devices, shards(): sums[j] = lax.psum_scatter(chip, 'z', scatter_dimension=0)  136 us
    ppermute x64, starting transfers between devices, send(): lax.ppermute(parts[d], ('y', 'xl'), routes[d])  114 us
    all_gather x2, waiting for transfers between devices, shards(): own = lax.all_gather(part, 'z', axis=0)  98.6 us
    ppermute x64, waiting for transfers between devices, send(): lax.ppermute(parts[d], ('y', 'xl'), routes[d])  62.1 us
    pallas_call x9, Pallas kernels, shards(): pl.pallas_call(functools.partial(backward_kernel, k, len(ins), len(hidden...  45.8 us
    pallas_call x9, Pallas kernels, shards(): pl.pallas_call(functools.partial(forward_kernel, k, len(ins), len(weights...  36.7 us
    ppermute x14, starting transfers between devices, turn(): return lax.ppermute(value, ('y', 'xh'), turns[dx][dy])  28.9 us
    unnamed x229, local copies, waits for them, and re-layouts  22.7 us
  transfers between devices with their start and end apart: 93, of which 60 were waited for; matrix products, arithmetic and copies ran while one was open for 2% of the time, Pallas kernels for 4%

profile of v2, /device:TPU:8, one launch (start us, length us, event | category | flops | bytes accessed | tf_op | source)
XLA Modules:
  0.0 622.2 jit_solution(4351796033883845010)
XLA Ops:
  13.9 4.3 collective-permute-start.7
  30.1 49.5 %all-gather.5.cloned.1.call-done = bf16[16,2,48,1152]{3,2,1,0:T(8,128)(2,1)} async-done(((bf16[2,2,48,1152]{3,2,1,0:T(8,128)(2,1)}), bf16[16,2,48,1152]{3,2,1,0:T(8,128)(2,1)}) %all-gather.5.cloned.1.call-update) | async-done | bytes 3538960 | tf_op jit(solution)/shard_map/all_gather | solution.py:355
  79.6 49.1 %all-gather.7.cloned.1.call-done = bf16[16,2,48,1152]{3,2,1,0:T(8,128)(2,1)} async-done(((bf16[2,2,48,1152]{3,2,1,0:T(8,128)(2,1)}), bf16[16,2,48,1152]{3,2,1,0:T(8,128)(2,1)}) %all-gather.7.cloned.1.call-update) | async-done | bytes 3538960 | tf_op jit(solution)/shard_map/all_gather | solution.py:355
  142.2 4.1 forward_step.9
  150.9 4.2 collective-permute-start.13
  160.9 4.0 forward_step.10
  176.7 4.1 forward_step.11
  192.4 4.4 forward_step.12
  207.7 4.1 forward_step.13
  223.1 4.1 forward_step.14
  239.3 4.7 forward_step.15
  260.4 4.5 forward_step.16
  278.3 5.2 backward_step.9
  295.4 5.5 backward_step.10
  312.2 5.5 backward_step.11
  329.7 5.5 backward_step.12
  347.1 4.7 backward_step.13
  363.8 5.5 backward_step.14
  381.8 5.5 backward_step.15
  398.0 5.2 backward_step.16
  453.7 12.7 %reduce-scatter.5.cloned.1.call-done = bf16[1,2,48,1152]{3,2,1,0:T(8,128)(2,1)} async-done(((bf16[8,2,48,1152]{3,2,1,0:T(8,128)(2,1)}), bf16[1,2,48,1152]{3,2,1,0:T(8,128)(2,1)}) %reduce-scatter.5.cloned.1.call-update) | async-done | bytes 221200 | tf_op jit(solution)/shard_map/reduce_scatter | solution.py:493
  467.3 41.3 %reduce-scatter.7.cloned.1.call-done = bf16[1,2,48,1152]{3,2,1,0:T(8,128)(2,1)} async-done(((bf16[8,2,48,1152]{3,2,1,0:T(8,128)(2,1)}), bf16[1,2,48,1152]{3,2,1,0:T(8,128)(2,1)}) %reduce-scatter.7.cloned.1.call-update) | async-done | bytes 221200 | tf_op jit(solution)/shard_map/reduce_scatter | solution.py:493
  509.5 41.2 %reduce-scatter.9.cloned.1.call-done = bf16[1,2,48,1152]{3,2,1,0:T(8,128)(2,1)} async-done(((bf16[8,2,48,1152]{3,2,1,0:T(8,128)(2,1)}), bf16[1,2,48,1152]{3,2,1,0:T(8,128)(2,1)}) %reduce-scatter.9.cloned.1.call-update) | async-done | bytes 221200 | tf_op jit(solution)/shard_map/reduce_scatter | solution.py:493
  551.7 41.2 %reduce-scatter.11.cloned.1.call-done = bf16[1,2,48,1152]{3,2,1,0:T(8,128)(2,1)} async-done(((bf16[8,2,48,1152]{3,2,1,0:T(8,128)(2,1)}), bf16[1,2,48,1152]{3,2,1,0:T(8,128)(2,1)}) %reduce-scatter.11.cloned.1.call-update) | async-done | bytes 221200 | tf_op jit(solution)/shard_map/reduce_scatter | solution.py:493
  (468 shorter events, 286.7 us)
Async XLA Ops:
  6.5 73.0 %all-gather.5.cloned.1.call-start = ((), (), s32[]{:S(2)}) async-start(), calls=%async_computation.8 | async-start | bytes 3981312 | tf_op jit(solution)/shard_map/all_gather | solution.py:355
  8.4 10.5 %collective-permute-start.9 = (bf16[48,1152]{1,0:T(8,128)(2,1)S(1)}, bf16[48,1152]{1,0:T(8,128)(2,1)S(1)}, u32[]{:S(2)}, u32[]{:S(2)}) collective-permute-start(bf16[48,1152]{1,0:T(8,128)(2,1)S(1)} %get-tuple-element.205), channel_id=1, source_target_pairs={{0,208},{16,192},{64,16},{80,0},{128,80},{144,64},{192,144},{208,1... | collective-permute-start | bytes 331784 | tf_op jit(solution)/shard_map/ppermute | solution.py:334
  11.3 10.2 %collective-permute-start.8 = (bf16[48,1152]{1,0:T(8,128)(2,1)S(1)}, bf16[48,1152]{1,0:T(8,128)(2,1)S(1)}, u32[]{:S(2)}, u32[]{:S(2)}) collective-permute-start(bf16[48,1152]{1,0:T(8,128)(2,1)S(1)} %get-tuple-element.206), channel_id=1, source_target_pairs={{0,144},{16,128},{64,208},{80,192},{128,16},{144,0},{192,80},{208,... | collective-permute-start | bytes 331784 | tf_op jit(solution)/shard_map/ppermute | solution.py:334
  13.9 9.7 %collective-permute-start.7 = (bf16[48,1152]{1,0:T(8,128)(2,1)S(1)}, bf16[48,1152]{1,0:T(8,128)(2,1)S(1)}, u32[]{:S(2)}, u32[]{:S(2)}) collective-permute-start(bf16[48,1152]{1,0:T(8,128)(2,1)S(1)} %get-tuple-element.207), channel_id=1, source_target_pairs={{0,80},{16,64},{64,144},{80,128},{128,208},{144,192},{192,16},{208... | collective-permute-start | bytes 331784 | tf_op jit(solution)/shard_map/ppermute | solution.py:334
  29.0 99.6 %all-gather.7.cloned.1.call-start = ((), (), s32[]{:S(2)}) async-start(), calls=%async_computation.9 | async-start | bytes 3981312 | tf_op jit(solution)/shard_map/all_gather | solution.py:355
  30.0 436.3 %reduce-scatter.5.cloned.1.call-start = ((), (), s32[]{:S(2)}) async-start(), calls=%async_computation.4 | async-start | bytes 1990656 | tf_op jit(solution)/shard_map/reduce_scatter | solution.py:493
  79.6 61.7 %collective-permute-start.10 = (bf16[8,2,2,48,1152]{4,3,2,1,0:T(8,128)(2,1)}, bf16[8,2,2,48,1152]{4,3,2,1,0:T(8,128)(2,1)}, u32[]{:S(2)}, u32[]{:S(2)}) collective-permute-start(bf16[8,2,2,48,1152]{4,3,2,1,0:T(8,128)(2,1)} %bitcast.102), channel_id=1, source_target_pairs={{0,1},{1,0},{2,3},{3,2},{4,5},{5,4},{6,7},{7,6},{8,9},{9,8},{10,11... | collective-permute-start | bytes 10616840 | tf_op jit(solution)/shard_map/ppermute | solution.py:317
  128.7 75.9 %collective-permute-start.27 = (bf16[8,2,2,48,1152]{4,3,2,1,0:T(8,128)(2,1)}, bf16[8,2,2,48,1152]{4,3,2,1,0:T(8,128)(2,1)}, u32[]{:S(2)}, u32[]{:S(2)}) collective-permute-start(bf16[8,2,2,48,1152]{4,3,2,1,0:T(8,128)(2,1)} %bitcast.113), channel_id=1, source_target_pairs={{0,1},{1,0},{2,3},{3,2},{4,5},{5,4},{6,7},{7,6},{8,9},{9,8},{10,11... | collective-permute-start | bytes 10616840 | tf_op jit(solution)/shard_map/ppermute | solution.py:317
  130.6 7.8 %collective-permute-start.5 = (f32[4,3,1536]{2,1,0:T(4,128)}, f32[4,3,1536]{2,1,0:T(4,128)}, u32[]{:S(2)}, u32[]{:S(2)}) collective-permute-start(f32[4,3,1536]{2,1,0:T(4,128)} %copy.31), channel_id=1, source_target_pairs={{0,192},{64,0},{128,64},{192,128},{1,193},{65,1},{129,65},{193,129... | collective-permute-start | bytes 221192 | tf_op jit(solution)/shard_map/ppermute | solution.py:366
  131.1 8.0 %collective-permute-start.4 = (f32[4,3,1536]{2,1,0:T(4,128)}, f32[4,3,1536]{2,1,0:T(4,128)}, u32[]{:S(2)}, u32[]{:S(2)}) collective-permute-start(f32[4,3,1536]{2,1,0:T(4,128)} %copy.31), channel_id=1, source_target_pairs={{0,128},{64,192},{128,0},{192,64},{1,129},{65,193},{129,1},{193,65... | collective-permute-start | bytes 221192 | tf_op jit(solution)/shard_map/ppermute | solution.py:366
  149.4 7.9 %collective-permute-start.12 = (bf16[112,384]{1,0:T(8,128)(2,1)S(1)}, bf16[112,384]{1,0:T(8,128)(2,1)S(1)}, u32[]{:S(2)}, u32[]{:S(2)}) collective-permute-start(bf16[112,384]{1,0:T(8,128)(2,1)S(1)} %get-tuple-element.95), channel_id=1, source_target_pairs={{0,96},{32,64},{64,160},{96,128},{128,224},{160,192},{192,32},{224... | collective-permute-start | bytes 258056 | tf_op jit(solution)/shard_map/ppermute | solution.py:389
  150.9 9.5 %collective-permute-start.13 = (bf16[112,384]{1,0:T(8,128)(2,1)S(1)}, bf16[112,384]{1,0:T(8,128)(2,1)S(1)}, u32[]{:S(2)}, u32[]{:S(2)}) collective-permute-start(bf16[112,384]{1,0:T(8,128)(2,1)S(1)} %get-tuple-element.95), channel_id=1, source_target_pairs={{0,160},{32,128},{64,224},{96,192},{128,32},{160,0},{192,96},{224,... | collective-permute-start | bytes 258056 | tf_op jit(solution)/shard_map/ppermute | solution.py:389
  196.9 7.7 %collective-permute-start.23 = (bf16[112,384]{1,0:T(8,128)(2,1)S(1)}, bf16[112,384]{1,0:T(8,128)(2,1)S(1)}, u32[]{:S(2)}, u32[]{:S(2)}) collective-permute-start(bf16[112,384]{1,0:T(8,128)(2,1)S(1)} %get-tuple-element.101), channel_id=1, source_target_pairs={{0,32},{32,0},{64,96},{96,64},{128,160},{160,128},{192,224},{224,1... | collective-permute-start | bytes 258056 | tf_op jit(solution)/shard_map/ppermute | solution.py:389
  265.0 8.3 %collective-permute-start.40 = (bf16[112,384]{1,0:T(8,128)(2,1)S(1)}, bf16[112,384]{1,0:T(8,128)(2,1)S(1)}, u32[]{:S(2)}, u32[]{:S(2)}) collective-permute-start(bf16[112,384]{1,0:T(8,128)(2,1)S(1)} %get-tuple-element.109), channel_id=1, source_target_pairs={{0,32},{32,0},{64,96},{96,64},{128,160},{160,128},{192,224},{224,1... | collective-permute-start | bytes 258056 | tf_op jit(solution)/shard_map/ppermute | solution.py:389
  354.5 7.8 %collective-permute-start.62 = (bf16[112,384]{1,0:T(8,128)(2,1)S(1)}, bf16[112,384]{1,0:T(8,128)(2,1)S(1)}, u32[]{:S(2)}, u32[]{:S(2)}) collective-permute-start(bf16[112,384]{1,0:T(8,128)(2,1)S(1)} %get-tuple-element.141), channel_id=1, source_target_pairs={{0,160},{32,128},{64,224},{96,192},{128,32},{160,0},{192,96},{224,... | collective-permute-start | bytes 258056 | tf_op jit(solution)/shard_map/ppermute | solution.py:389
  370.0 7.9 %collective-permute-start.64 = (bf16[112,384]{1,0:T(8,128)(2,1)S(1)}, bf16[112,384]{1,0:T(8,128)(2,1)S(1)}, u32[]{:S(2)}, u32[]{:S(2)}) collective-permute-start(bf16[112,384]{1,0:T(8,128)(2,1)S(1)} %get-tuple-element.144), channel_id=1, source_target_pairs={{0,32},{32,0},{64,96},{96,64},{128,160},{160,128},{192,224},{224,1... | collective-permute-start | bytes 258056 | tf_op jit(solution)/shard_map/ppermute | solution.py:389
  372.5 9.0 %collective-permute-start.66 = (bf16[112,384]{1,0:T(8,128)(2,1)S(1)}, bf16[112,384]{1,0:T(8,128)(2,1)S(1)}, u32[]{:S(2)}, u32[]{:S(2)}) collective-permute-start(bf16[112,384]{1,0:T(8,128)(2,1)S(1)} %get-tuple-element.146), channel_id=1, source_target_pairs={{0,160},{32,128},{64,224},{96,192},{128,32},{160,0},{192,96},{224,... | collective-permute-start | bytes 258056 | tf_op jit(solution)/shard_map/ppermute | solution.py:389
  425.5 83.1 %reduce-scatter.7.cloned.1.call-start = ((), (), s32[]{:S(2)}) async-start(), calls=%async_computation.5 | async-start | bytes 1990656 | tf_op jit(solution)/shard_map/reduce_scatter | solution.py:493
  434.9 115.8 %reduce-scatter.9.cloned.1.call-start = ((), (), s32[]{:S(2)}) async-start(), calls=%async_computation.6 | async-start | bytes 1990656 | tf_op jit(solution)/shard_map/reduce_scatter | solution.py:493
  444.4 148.5 %reduce-scatter.11.cloned.1.call-start = ((), (), s32[]{:S(2)}) async-start(), calls=%async_computation.7 | async-start | bytes 1990656 | tf_op jit(solution)/shard_map/reduce_scatter | solution.py:493
  593.9 11.7 %collective-permute-start.82 = (bf16[48,1152]{1,0:T(8,128)(2,1)S(1)}, bf16[48,1152]{1,0:T(8,128)(2,1)S(1)}, u32[]{:S(2)}, u32[]{:S(2)}) collective-permute-start(bf16[48,1152]{1,0:T(8,128)(2,1)S(1)} %get-tuple-element.189), channel_id=1, source_target_pairs={{0,80},{16,64},{64,144},{80,128},{128,208},{144,192},{192,16},{208... | collective-permute-start | bytes 331784 | tf_op jit(solution)/shard_map/ppermute | solution.py:334
  597.9 8.6 %collective-permute-start.81 = (bf16[48,1152]{1,0:T(8,128)(2,1)S(1)}, bf16[48,1152]{1,0:T(8,128)(2,1)S(1)}, u32[]{:S(2)}, u32[]{:S(2)}) collective-permute-start(bf16[48,1152]{1,0:T(8,128)(2,1)S(1)} %get-tuple-element.190), channel_id=1, source_target_pairs={{0,64},{16,80},{64,128},{80,144},{128,192},{144,208},{192,0},{208,... | collective-permute-start | bytes 331784 | tf_op jit(solution)/shard_map/ppermute | solution.py:334
  599.1 9.1 %collective-permute-start.80 = (bf16[48,1152]{1,0:T(8,128)(2,1)S(1)}, bf16[48,1152]{1,0:T(8,128)(2,1)S(1)}, u32[]{:S(2)}, u32[]{:S(2)}) collective-permute-start(bf16[48,1152]{1,0:T(8,128)(2,1)S(1)} %get-tuple-element.191), channel_id=1, source_target_pairs={{0,16},{16,0},{64,80},{80,64},{128,144},{144,128},{192,208},{208,1... | collective-permute-start | bytes 331784 | tf_op jit(solution)/shard_map/ppermute | solution.py:334
  599.6 8.9 %collective-permute-start.84 = (bf16[48,1152]{1,0:T(8,128)(2,1)S(1)}, bf16[48,1152]{1,0:T(8,128)(2,1)S(1)}, u32[]{:S(2)}, u32[]{:S(2)}) collective-permute-start(bf16[48,1152]{1,0:T(8,128)(2,1)S(1)} %get-tuple-element.187), channel_id=1, source_target_pairs={{0,144},{16,128},{64,208},{80,192},{128,16},{144,0},{192,80},{208,... | collective-permute-start | bytes 331784 | tf_op jit(solution)/shard_map/ppermute | solution.py:334
  (180 other events, 1893.0 us)
Sparse Core Ops, SparseCore 0:
  29.2 50.3 all-gather.4
  81.4 47.2 all-gather.6
  425.6 40.7 reduce-scatter.4
  468.8 39.7 reduce-scatter.6
  511.0 39.6 reduce-scatter.8
  553.1 39.6 reduce-scatter.10

commit v3 on v2

--- a/solution.py
+++ b/solution.py
@@ -37,9 +37,8 @@
 
     def start(own, other):
         for t in range(halves):
-            where = lax.rem(t + scal[3], halves)
-            pltpu.make_async_copy(own.at[:, inner, t], wscr.at[where, :, c], sem).start()
-            pltpu.make_async_copy(other.at[:, inner, t], wscr.at[where, :, 1 - c], sem).start()
+            pltpu.make_async_copy(own.at[:, inner, t], wscr.at[t, :, c], sem).start()
+            pltpu.make_async_copy(other.at[:, inner, t], wscr.at[t, :, 1 - c], sem).start()
 
     if len(pieces) == 2:
         start(*pieces)
@@ -137,7 +136,9 @@
     pieces, refs = refs[2 : 2 + n_w], refs[2 + n_w :]
     if send:
         out_ref, refs = refs[0], refs[1:]
-    normed_ref, proj_ref, wscr, hs, sem = refs
+    normed_out, proj_out, normed_ref, proj_ref, wscr, hs, sem, sems = refs
+    normed_save = pltpu.make_async_copy(normed_ref, normed_out, sems.at[0])
+    proj_save = pltpu.make_async_copy(proj_ref, proj_out, sems.at[1])
     y = scal[0]
     micro, j, slot = place(scal, k)
     fetch_weights(scal, j, pieces, wscr, sem)
@@ -155,6 +156,7 @@
         axis=0,
     ).astype(BF16)
     normed_ref[...] = normed
+    normed_save.start()
     await_weights(wscr, sem)
     halves = wscr.shape[0]
     span = width // halves
@@ -162,11 +164,14 @@
     for t in range(1, halves):
         projected += nn(normed[:, t * span : (t + 1) * span], half_weights(wscr, t))
     proj_ref[...] = projected
+    proj_save.start()
     if not send:
+        normed_save.wait()
+        proj_save.wait()
         return
     own = hs[y].astype(F32)
     for s in range(PAIR):
-        length = scal[4 + PAIR * micro + s]
+        length = scal[3 + PAIR * micro + s]
         r = slice(s * seq, (s + 1) * seq)
         mixed = []
         for h in range(chunk // HDIM):
@@ -181,6 +186,8 @@
         if s == 0:
             first = hs_rows
     out_ref[...] = jnp.concatenate([first, hs_rows], axis=0).astype(BF16)
+    normed_save.wait()
+    proj_save.wait()
 
 
 def backward_kernel(k, n_in, n_hid, n_w, send, scal, *refs):
@@ -189,7 +196,8 @@
     mods, gates, proj_ref = refs[:3]
     pieces, refs = refs[3 : 3 + n_w], refs[3 + n_w :]
     outs, refs = refs[: QUART * send], refs[QUART * send :]
-    low_ref, wscr, hs, gs, dp, ds, sem = refs
+    low_out, low_ref, wscr, hs, gs, dp, ds, sem, low_sem = refs
+    low_save = pltpu.make_async_copy(low_ref, low_out, low_sem)
     y = scal[0]
     micro, j, slot = place(scal, k)
     if send:
@@ -215,7 +223,7 @@
 
     root = 1.0 / math.sqrt(HDIM)
     for s in range(PAIR):
-        length = scal[4 + PAIR * micro + s]
+        length = scal[3 + PAIR * micro + s]
         r = slice(s * seq, (s + 1) * seq)
         for h in range(chunk // HDIM):
             lo = h * HDIM
@@ -237,7 +245,9 @@
             dp[r, 2 * chunk + lo : 2 * chunk + lo + HDIM] = tn(att, dmix)
     low = dp[...].astype(BF16)
     low_ref[...] = low
+    low_save.start()
     if not send:
+        low_save.wait()
         return
     normal, scale = standardize(load_hidden(scal, hidden, hs))
     await_weights(wscr, sem)
@@ -257,6 +267,7 @@
     ds[y] = ds[y] + gs[...]
     for d in range(QUART):
         outs[d][...] = ds[lax.rem(y + d, QUART)].astype(BF16)
+    low_save.wait()
 
 
 def weight_grad_kernel(scal, n0, n1, n2, g0, g1, g2, out, nscr, gscr, sems):
@@ -300,7 +311,6 @@
 def shards(latents, out_grad, w_qkv, mod_table, timesteps, text_len):
     y = lax.axis_index("y")
     p = lax.axis_index("xl")
-    half = lax.axis_index("xh")
     core = lax.axis_index("c")
     halves = lax.axis_size("xh")
     depth = lax.axis_size("z")
@@ -316,47 +326,15 @@
     def swap(value, axis):
         return lax.ppermute(value, axis, [(0, 1), (1, 0)])
 
-    turns = [
-        [
-            [
-                (yy * halves + hh, ((yy + dy) % QUART) * halves + (hh + dx) % halves)
-                for yy in range(QUART)
-                for hh in range(halves)
-            ]
-            for dy in range(QUART)
-        ]
-        for dx in range(halves)
-    ]
-
-    def turn(value, dx, dy):
-        if dx == 0 and dy == 0:
-            return value
-        return lax.ppermute(value, ("y", "xh"), turns[dx][dy])
-
-    def pick(stack, index):
-        return lax.dynamic_index_in_dim(stack, index, 0, keepdims=False)
-
-    quarters = w_qkv[0].reshape(share, 3, QUART, chunk)
-    quarters = quarters.transpose(2, 0, 1, 3).reshape(QUART, share, cols)
-    leaves = [pick(quarters, lax.rem(y + dy, QUART)) for dy in range(QUART)]
-    arrived = [
-        jnp.stack([turn(leaves[dy], dx, dy) for dy in range(QUART)]) for dx in range(halves)
-    ]
-    pieces = []
-    for g in range(nj // 2):
-        part = jnp.stack(
-            [
-                jnp.stack(
-                    [pick(arrived[dx], lax.rem(y + QUART - j, QUART)) for dx in range(halves)]
-                )
-                for j in (2 * g, 2 * g + 1)
-            ]
-        )
-        own = lax.all_gather(part, "z", axis=0)
-        pieces.append((own, swap(own, "c")))
+    quarters = w_qkv[0].reshape(share, 3, QUART, chunk).transpose(2, 0, 1, 3)
+    quarters = quarters.reshape(QUART, 1, share, cols)
+    quarters = jnp.broadcast_to(quarters, (QUART, halves, share, cols))
+    quarters = quarters.reshape(QUART * halves, share, cols)
+    both = lax.all_to_all(quarters, ("y", "xh"), 0, 0).reshape(nj, halves, share, cols)
+    gathered = [lax.all_gather(both[2 * g : 2 * g + 2], "z", axis=0) for g in range(nj // 2)]
 
     onehot = (timesteps[:, 0][:, None] == jnp.arange(levels, dtype=jnp.int32)[None, :]).astype(F32)
-    table, _ = lax.optimization_barrier((mod_table, arrived[0]))
+    table, _ = lax.optimization_barrier((mod_table, both))
     modulations = jnp.dot(
         onehot, table[0].reshape(levels, 3 * width), precision=lax.Precision.HIGHEST
     ).reshape(count, 3, width)
@@ -367,9 +345,11 @@
             for dy in range(1, QUART)
         ]
     )
+    first, mods = lax.optimization_barrier((gathered[0], mods))
+    pieces = [(first, swap(first, "c"))]
     gates = lax.dynamic_slice_in_dim(mods[:, :, 2:3, :], y * chunk, chunk, axis=3)
     scal = jnp.concatenate(
-        [jnp.stack([y, core, p, half]).astype(jnp.int32), text_len[:, 0].astype(jnp.int32)]
+        [jnp.stack([y, core, p]).astype(jnp.int32), text_len[:, 0].astype(jnp.int32)]
     )
     entering = latents.reshape(count // PAIR, rows, width)
     leaving = lax.dynamic_slice_in_dim(
@@ -420,18 +400,29 @@
             functools.partial(forward_kernel, k, len(ins), len(weights), sending),
             out_shape=outs,
             in_specs=[SM] + [VM] * (len(ins) + 2) + [ANY] * len(weights),
-            out_specs=[VM] * len(outs),
-            scratch_shapes=[wscr, pltpu.VMEM((QUART, rows, chunk), BF16), pltpu.SemaphoreType.DMA],
+            out_specs=[VM] * sending + [ANY] * 2,
+            scratch_shapes=[
+                pltpu.VMEM((rows, width), BF16),
+                pltpu.VMEM((rows, cols), F32),
+                wscr,
+                pltpu.VMEM((QUART, rows, chunk), BF16),
+                pltpu.SemaphoreType.DMA,
+                pltpu.SemaphoreType.DMA((2,)),
+            ],
             compiler_params=params,
             name="forward_step",
         )(scal, *ins, mods, gates, *weights)
         if sending:
             received = send([result[0]] * QUART)
             result = result[1:]
+        if k == 2:
+            second, _ = lax.optimization_barrier((gathered[1], received[0]))
+            pieces.append((second, swap(second, "c")))
         saved.append((ins, *result))
 
     lows = [None] * steps
-    sums = [None] * nj
+    chips = [None] * nj
+    rings = [None] * (nj // 2)
     received = None
     for k in reversed(range(steps)):
         if k == steps - 1:
@@ -451,13 +442,15 @@
             ),
             out_shape=outs,
             in_specs=[SM] + [VM] * sources + [ANY] * len(weights),
-            out_specs=[VM] * len(outs),
+            out_specs=[VM] * (len(outs) - 1) + [ANY],
             scratch_shapes=[
+                pltpu.VMEM((rows, cols), BF16),
                 wscr,
                 pltpu.VMEM((QUART, rows, chunk), BF16),
                 pltpu.VMEM((rows, chunk), F32),
                 pltpu.VMEM((rows, cols), F32),
                 pltpu.VMEM((QUART, rows, chunk), F32),
+                pltpu.SemaphoreType.DMA,
                 pltpu.SemaphoreType.DMA,
             ],
             compiler_params=params,
@@ -489,16 +482,21 @@
                 ),
                 name="weight_grad",
             )(scal, *factors)
-            chip = partial[0] + swap(partial[1], "c")
-            sums[j] = lax.psum_scatter(chip, "z", scatter_dimension=0)
-    sums = jnp.stack(sums)
-    finals = []
-    for dy in range(QUART):
-        block = pick(sums, lax.rem(y + dy, QUART))
-        here = [turn(pick(block, lax.rem(half + dx, halves)), dx, dy) for dx in range(halves)]
-        finals.append(sum([part.astype(F32) for part in here]).reshape(share, 3, chunk))
-    finals = jnp.stack(finals)
-    grads = jnp.stack([pick(finals, lax.rem(y + QUART - q, QUART)) for q in range(QUART)], axis=2)
+            if sending:
+                partial, received[1] = lax.optimization_barrier((partial, received[1]))
+            chips[j] = (partial[0], swap(partial[1], "c"))
+        if k in (0, 3):
+            g = k // 3
+            total = jnp.stack([chips[2 * g + i][0] + chips[2 * g + i][1] for i in range(2)], axis=1)
+            total = total.reshape(depth, 2 * halves * share, cols)
+            if sending:
+                total, received[1] = lax.optimization_barrier((total, received[1]))
+            else:
+                total, _ = lax.optimization_barrier((total, rings[1]))
+            rings[g] = lax.psum_scatter(total, "z", scatter_dimension=0)
+    spread = jnp.stack(rings).reshape(nj * halves, share, cols)
+    quarters = lax.all_to_all(spread, ("y", "xh"), 0, 0).reshape(QUART, halves, share, 3, chunk)
+    grads = jnp.sum(quarters.astype(F32), axis=1).transpose(1, 2, 0, 3)
     return grads.reshape(1, share, 3 * width)
 
 

time: 632 us -> 493 us (0.78)
  the two profiles are of different devices: /device:TPU:8 before, /device:TPU:1 now
where the time goes in v3:
time: 493 us; the launch traced here: 483 us
  waiting for transfers between devices  162 us (33%)
  starting transfers between devices  116 us (24%)
  Pallas kernels  92.9 us (19%)
  local copies, waits for them, and re-layouts  50 us (10%)
  blocking collectives  42.3 us (9%)
  between operations  15 us (3%)
    ppermute x64, starting transfers between devices, send(): lax.ppermute(parts[d], ('y', 'xl'), routes[d])  83.2 us
    ppermute x64, waiting for transfers between devices, send(): lax.ppermute(parts[d], ('y', 'xl'), routes[d])  64.6 us
    pallas_call x9, Pallas kernels, shards(): pl.pallas_call(functools.partial(backward_kernel, k, len(ins), len(hidden...  47.7 us
    reduce_scatter x2, waiting for transfers between devices, shards(): rings[g] = lax.psum_scatter(total, 'z', scatter_dimension=0)  45.7 us
    all_gather x2, waiting for transfers between devices, shards(): lax.all_gather(both[2 * g:2 * g + 2], 'z', axis=0)  39.9 us
    unnamed x235, local copies, waits for them, and re-layouts  36.1 us
    pallas_call x9, Pallas kernels, shards(): pl.pallas_call(functools.partial(forward_kernel, k, len(ins), len(weights...  34.3 us
    ppermute x6, starting transfers between devices, swap(): return lax.ppermute(value, axis, [(0, 1), (1, 0)])  30.3 us
  transfers between devices with their start and end apart: 77, of which 42 were waited for; matrix products, arithmetic and copies ran while one was open for 2% of the time, Pallas kernels for 10%

profile of v3, /device:TPU:1, one launch (start us, length us, event | category | flops | bytes accessed | tf_op | source)
XLA Modules:
  0.0 483.4 jit_solution(17129970390052134017)
XLA Ops:
  8.3 21.5 %all_to_all.10 = bf16[8,48,1152]{2,1,0:T(8,128)(2,1)S(1)} all-to-all(bf16[8,48,1152]{2,1,0:T(8,128)(2,1)S(1)} %bitcast.73), channel_id=1, replica_groups=mesh['y'=4,'xl'=2,'xh'=2,'z'=8,'c'=2] {'y','xh'}, dimensions={0} | all-to-all | bytes 1769472 | tf_op jit(solution)/shard_map/all_to_all | solution.py:333
  40.2 39.9 %all-gather.3.cloned.1.call-done.refs_3_.refs_7_.refs_6_.refs_8_.refs_13_.refs_11_.refs_12_ = bf16[8,2,2,48,1152]{4,3,2,1,0:T(8,128)(2,1)} async-done(((bf16[1,2,2,48,1152]{4,3,2,1,0:T(8,128)(2,1)}), bf16[8,2,2,48,1152]{4,3,2,1,0:T(8,128)(2,1)}) %all-gather.3.cloned.1.call-update) | async-done | bytes 3538960 | tf_op jit(solution)/shard_map/all_gather | solution.py:334
  101.1 3.9 collective-permute-done.6.refs_3_.refs_7_
  123.7 4.3 forward_step.11
  133.5 3.7 collective-permute-start.20
  150.3 4.2 forward_step.12
  165.9 3.7 forward_step.13
  179.6 3.7 forward_step.14
  193.4 4.4 forward_step.15
  215.3 4.2 forward_step.16
  230.5 5.4 %backward_step.9 = (bf16[112,384]{1,0:T(8,128)(2,1)S(1)}, bf16[112,384]{1,0:T(8,128)(2,1)S(1)}, bf16[112,384]{1,0:T(8,128)(2,1)S(1)}, bf16[112,384]{1,0:T(8,128)(2,1)S(1)}, bf16[112,1152]{1,0:T(8,128)(2,1)S(1)}) custom-call(s32[7]{0:T(128)S(1)} %pad_add_fusion.scal, bf16[112,384]{1,0:T(8,128)(2,1)S(1)} %get-tuple-element.203.refs_0_, ...), custom_call_target="tpu_custom_call" | custom-call | tf_op jit(solution)/shard_map/backward_step/pallas_call | solution.py:439
  246.1 6.0 %backward_step.10 = (bf16[112,384]{1,0:T(8,128)(2,1)S(1)}, bf16[112,384]{1,0:T(8,128)(2,1)S(1)}, bf16[112,384]{1,0:T(8,128)(2,1)S(1)}, bf16[112,384]{1,0:T(8,128)(2,1)S(1)}, bf16[112,1152]{1,0:T(8,128)(2,1)S(1)}) custom-call(s32[7]{0:T(128)S(1)} %pad_add_fusion.scal, bf16[112,384]{1,0:T(8,128)(2,1)S(1)} %get-tuple-element.204.refs_0_, ...), custom_call_target="tpu_custom_call" | custom-call | tf_op jit(solution)/shard_map/backward_step/pallas_call | solution.py:439
  262.0 5.4 %backward_step.11 = (bf16[112,384]{1,0:T(8,128)(2,1)S(1)}, bf16[112,384]{1,0:T(8,128)(2,1)S(1)}, bf16[112,384]{1,0:T(8,128)(2,1)S(1)}, bf16[112,384]{1,0:T(8,128)(2,1)S(1)}, bf16[112,1152]{1,0:T(8,128)(2,1)S(1)}) custom-call(s32[7]{0:T(128)S(1)} %pad_add_fusion.scal, bf16[112,384]{1,0:T(8,128)(2,1)S(1)} %collective-permute-done.41.refs_0_, ...), custom_call_target="tpu_custom_call" | custom-call | tf_op jit(solution)/shard_map/backward_step/pallas_call | solution.py:439
  276.0 5.4 %backward_step.12 = (bf16[112,384]{1,0:T(8,128)(2,1)S(1)}, bf16[112,384]{1,0:T(8,128)(2,1)S(1)}, bf16[112,384]{1,0:T(8,128)(2,1)S(1)}, bf16[112,384]{1,0:T(8,128)(2,1)S(1)}, bf16[112,1152]{1,0:T(8,128)(2,1)S(1)}) custom-call(s32[7]{0:T(128)S(1)} %pad_add_fusion.scal, bf16[112,384]{1,0:T(8,128)(2,1)S(1)} %collective-permute-done.45.refs_0_, ...), custom_call_target="tpu_custom_call" | custom-call | tf_op jit(solution)/shard_map/backward_step/pallas_call | solution.py:439
  290.4 5.6 %backward_step.13 = (bf16[112,384]{1,0:T(8,128)(2,1)S(1)}, bf16[112,384]{1,0:T(8,128)(2,1)S(1)}, bf16[112,384]{1,0:T(8,128)(2,1)S(1)}, bf16[112,384]{1,0:T(8,128)(2,1)S(1)}, bf16[112,1152]{1,0:T(8,128)(2,1)S(1)}) custom-call(s32[7]{0:T(128)S(1)} %pad_add_fusion.scal, bf16[112,384]{1,0:T(8,128)(2,1)S(1)} %collective-permute-done.49.refs_0_, ...), custom_call_target="tpu_custom_call" | custom-call | tf_op jit(solution)/shard_map/backward_step/pallas_call | solution.py:439
  297.7 13.8 %collective-permute-start.59 = (bf16[8,2,48,1152]{3,2,1,0:T(8,128)(2,1)S(1)}, bf16[8,2,48,1152]{3,2,1,0:T(8,128)(2,1)S(1)}, u32[]{:S(2)}, u32[]{:S(2)}) collective-permute-start(bf16[8,2,48,1152]{3,2,1,0:T(8,128)(2,1)S(1)} %slice_bitcast_fusion.3), channel_id=1, source_target_pairs={{0,1},{1,0},{2,3},{3,2},{4,5},{5,4},{6,7},{7,6},{8,9},{9,8},{10,11... | collective-permute-start | bytes 5308424 | tf_op jit(solution)/shard_map/ppermute | solution.py:327
  324.5 5.8 %backward_step.14 = (bf16[112,384]{1,0:T(8,128)(2,1)S(1)}, bf16[112,384]{1,0:T(8,128)(2,1)S(1)}, bf16[112,384]{1,0:T(8,128)(2,1)S(1)}, bf16[112,384]{1,0:T(8,128)(2,1)S(1)}, bf16[112,1152]{1,0:T(8,128)(2,1)S(1)}) custom-call(s32[7]{0:T(128)S(1)} %pad_add_fusion.scal, bf16[112,384]{1,0:T(8,128)(2,1)S(1)} %collective-permute-done.53.refs_0_, ...), custom_call_target="tpu_custom_call" | custom-call | tf_op jit(solution)/shard_map/backward_step/pallas_call | solution.py:439
  342.8 4.0 collective-permute-done.61.refs_2_
  356.1 5.4 %backward_step.15 = (bf16[112,384]{1,0:T(8,128)(2,1)S(1)}, bf16[112,384]{1,0:T(8,128)(2,1)S(1)}, bf16[112,384]{1,0:T(8,128)(2,1)S(1)}, bf16[112,384]{1,0:T(8,128)(2,1)S(1)}, bf16[112,1152]{1,0:T(8,128)(2,1)S(1)}) custom-call(s32[7]{0:T(128)S(1)} %pad_add_fusion.scal, bf16[112,384]{1,0:T(8,128)(2,1)S(1)} %collective-permute-done.57.refs_0_, ...), custom_call_target="tpu_custom_call" | custom-call | tf_op jit(solution)/shard_map/backward_step/pallas_call | solution.py:439
  371.8 5.4 %backward_step.16 = (bf16[112,384]{1,0:T(8,128)(2,1)S(1)}, bf16[112,384]{1,0:T(8,128)(2,1)S(1)}, bf16[112,384]{1,0:T(8,128)(2,1)S(1)}, bf16[112,384]{1,0:T(8,128)(2,1)S(1)}, bf16[112,1152]{1,0:T(8,128)(2,1)S(1)}) custom-call(s32[7]{0:T(128)S(1)} %pad_add_fusion.scal, bf16[112,384]{1,0:T(8,128)(2,1)S(1)} %collective-permute-done.63.refs_0_, ...), custom_call_target="tpu_custom_call" | custom-call | tf_op jit(solution)/shard_map/backward_step/pallas_call | solution.py:439
  382.5 5.3 %collective-permute-start.72 = (bf16[8,2,48,1152]{3,2,1,0:T(8,128)(2,1)S(1)}, bf16[8,2,48,1152]{3,2,1,0:T(8,128)(2,1)S(1)}, u32[]{:S(2)}, u32[]{:S(2)}) collective-permute-start(bf16[8,2,48,1152]{3,2,1,0:T(8,128)(2,1)S(1)} %slice_bitcast_fusion.2), channel_id=1, source_target_pairs={{0,1},{1,0},{2,3},{3,2},{4,5},{5,4},{6,7},{7,6},{8,9},{9,8},{10,11... | collective-permute-start | bytes 5308424 | tf_op jit(solution)/shard_map/ppermute | solution.py:327
  394.1 4.8 collective-permute-start.71
  405.1 45.7 %reduce-scatter.3.cloned.1.call-done = bf16[1,192,1152]{2,1,0:T(8,128)(2,1)} async-done(((bf16[8,192,1152]{2,1,0:T(8,128)(2,1)}), bf16[1,192,1152]{2,1,0:T(8,128)(2,1)}) %reduce-scatter.3.cloned.1.call-update) | async-done | bytes 442384 | tf_op jit(solution)/shard_map/reduce_scatter | solution.py:496
  452.1 20.8 %all_to_all.11 = bf16[8,48,1152]{2,1,0:T(8,128)(2,1)S(1)} all-to-all(bf16[8,48,1152]{2,1,0:T(8,128)(2,1)S(1)} %bitcast.72), channel_id=1, replica_groups=mesh['y'=4,'xl'=2,'xh'=2,'z'=8,'c'=2] {'y','xh'}, dimensions={0} | all-to-all | bytes 1769472 | tf_op jit(solution)/shard_map/all_to_all | solution.py:498
  (425 shorter events, 236.0 us)
Async XLA Ops:
  6.5 73.6 %all-gather.3.cloned.1.call-start = ((), (), s32[]{:S(2)}) async-start(), calls=%async_computation.4 | async-start | bytes 3981312 | tf_op jit(solution)/shard_map/all_gather | solution.py:334
  30.9 100.4 %all-gather.5.cloned.1.call-start = ((), (), s32[]{:S(2)}) async-start(), calls=%async_computation.5 | async-start | bytes 3981312 | tf_op jit(solution)/shard_map/all_gather | solution.py:334
  31.6 373.5 %reduce-scatter.5.cloned.1.call-start = ((), (), s32[]{:S(2)}) async-start(), calls=%async_computation.7 | async-start | bytes 3981312 | tf_op jit(solution)/shard_map/reduce_scatter | solution.py:496
  80.1 6.7 %collective-permute-start.3 = (bf16[8,2,2,48,1152]{4,3,2,1,0:T(8,128)(2,1)}, bf16[8,2,2,48,1152]{4,3,2,1,0:T(8,128)(2,1)S(1)}, u32[]{:S(2)}, u32[]{:S(2)}) collective-permute-start(bf16[8,2,2,48,1152]{4,3,2,1,0:T(8,128)(2,1)} %all-gather.3.cloned.1.call-done.refs_3_.refs_7_.refs_6_.refs_8_.refs_13_.refs_11_.r, ...), channel_id=1, source_target_pairs={{0,1},{1,0},{2,3},{3,2},{4,5},{5,4},{6,7},{7,6},{8,9},{9,8},{10,11... | collective-permute-start | bytes 10616840 | tf_op jit(solution)/shard_map/ppermute | solution.py:327
  133.5 32.4 %collective-permute-start.20 = (bf16[8,2,2,48,1152]{4,3,2,1,0:T(8,128)(2,1)}, bf16[8,2,2,48,1152]{4,3,2,1,0:T(8,128)(2,1)S(1)}, u32[]{:S(2)}, u32[]{:S(2)}) collective-permute-start(bf16[8,2,2,48,1152]{4,3,2,1,0:T(8,128)(2,1)} %all-gather.5.cloned.1.call-done.refs_6_.refs_8_.refs_12_.refs_11_), channel_id=1, source_target_pairs={{0,1},{1,0},{2,3},{3,2},{4,5},{5,4},{6,7},{7,6},{8,9},{9,8},{10,11... | collective-permute-start | bytes 10616840 | tf_op jit(solution)/shard_map/ppermute | solution.py:327
  139.5 7.0 %collective-permute-start.13 = (bf16[112,384]{1,0:T(8,128)(2,1)}, bf16[112,384]{1,0:T(8,128)(2,1)S(1)}, u32[]{:S(2)}, u32[]{:S(2)}) collective-permute-start(bf16[112,384]{1,0:T(8,128)(2,1)} %get-tuple-element.110), channel_id=1, source_target_pairs={{0,96},{32,64},{64,160},{96,128},{128,224},{160,192},{192,32},{224... | collective-permute-start | bytes 258056 | tf_op jit(solution)/shard_map/ppermute | solution.py:369
  203.0 6.6 %collective-permute-start.30 = (bf16[112,384]{1,0:T(8,128)(2,1)}, bf16[112,384]{1,0:T(8,128)(2,1)}, u32[]{:S(2)}, u32[]{:S(2)}) collective-permute-start(bf16[112,384]{1,0:T(8,128)(2,1)} %get-tuple-element.119), channel_id=1, source_target_pairs={{0,96},{32,64},{64,160},{96,128},{128,224},{160,192},{192,32},{224... | collective-permute-start | bytes 258056 | tf_op jit(solution)/shard_map/ppermute | solution.py:369
  235.9 7.0 %collective-permute-start.37 = (bf16[112,384]{1,0:T(8,128)(2,1)S(1)}, bf16[112,384]{1,0:T(8,128)(2,1)S(1)}, u32[]{:S(2)}, u32[]{:S(2)}) collective-permute-start(bf16[112,384]{1,0:T(8,128)(2,1)S(1)} %get-tuple-element.124), channel_id=1, source_target_pairs={{0,32},{32,0},{64,96},{96,64},{128,160},{160,128},{192,224},{224,1... | collective-permute-start | bytes 258056 | tf_op jit(solution)/shard_map/ppermute | solution.py:369
  253.7 6.5 %collective-permute-start.43 = (bf16[112,384]{1,0:T(8,128)(2,1)S(1)}, bf16[112,384]{1,0:T(8,128)(2,1)S(1)}, u32[]{:S(2)}, u32[]{:S(2)}) collective-permute-start(bf16[112,384]{1,0:T(8,128)(2,1)S(1)} %get-tuple-element.131), channel_id=1, source_target_pairs={{0,160},{32,128},{64,224},{96,192},{128,32},{160,0},{192,96},{224,... | collective-permute-start | bytes 258056 | tf_op jit(solution)/shard_map/ppermute | solution.py:369
  268.0 6.9 %collective-permute-start.46 = (bf16[112,384]{1,0:T(8,128)(2,1)S(1)}, bf16[112,384]{1,0:T(8,128)(2,1)S(1)}, u32[]{:S(2)}, u32[]{:S(2)}) collective-permute-start(bf16[112,384]{1,0:T(8,128)(2,1)S(1)} %get-tuple-element.145), channel_id=1, source_target_pairs={{0,96},{32,64},{64,160},{96,128},{128,224},{160,192},{192,32},{224... | collective-permute-start | bytes 258056 | tf_op jit(solution)/shard_map/ppermute | solution.py:369
  296.0 15.4 %collective-permute-start.53 = (bf16[112,384]{1,0:T(8,128)(2,1)S(1)}, bf16[112,384]{1,0:T(8,128)(2,1)S(1)}, u32[]{:S(2)}, u32[]{:S(2)}) collective-permute-start(bf16[112,384]{1,0:T(8,128)(2,1)S(1)} %get-tuple-element.157), channel_id=1, source_target_pairs={{0,32},{32,0},{64,96},{96,64},{128,160},{160,128},{192,224},{224,1... | collective-permute-start | bytes 258056 | tf_op jit(solution)/shard_map/ppermute | solution.py:369
  297.2 17.1 %collective-permute-start.54 = (bf16[112,384]{1,0:T(8,128)(2,1)S(1)}, bf16[112,384]{1,0:T(8,128)(2,1)S(1)}, u32[]{:S(2)}, u32[]{:S(2)}) collective-permute-start(bf16[112,384]{1,0:T(8,128)(2,1)S(1)} %get-tuple-element.165), channel_id=1, source_target_pairs={{0,96},{32,64},{64,160},{96,128},{128,224},{160,192},{192,32},{224... | collective-permute-start | bytes 258056 | tf_op jit(solution)/shard_map/ppermute | solution.py:369
  297.7 36.4 %collective-permute-start.59 = (bf16[8,2,48,1152]{3,2,1,0:T(8,128)(2,1)S(1)}, bf16[8,2,48,1152]{3,2,1,0:T(8,128)(2,1)S(1)}, u32[]{:S(2)}, u32[]{:S(2)}) collective-permute-start(bf16[8,2,48,1152]{3,2,1,0:T(8,128)(2,1)S(1)} %slice_bitcast_fusion.3), channel_id=1, source_target_pairs={{0,1},{1,0},{2,3},{3,2},{4,5},{5,4},{6,7},{7,6},{8,9},{9,8},{10,11... | collective-permute-start | bytes 5308424 | tf_op jit(solution)/shard_map/ppermute | solution.py:327
  314.4 19.9 %collective-permute-start.58 = (bf16[8,2,48,1152]{3,2,1,0:T(8,128)(2,1)S(1)}, bf16[8,2,48,1152]{3,2,1,0:T(8,128)(2,1)S(1)}, u32[]{:S(2)}, u32[]{:S(2)}) collective-permute-start(bf16[8,2,48,1152]{3,2,1,0:T(8,128)(2,1)S(1)} %slice_bitcast_fusion.4), channel_id=1, source_target_pairs={{0,1},{1,0},{2,3},{3,2},{4,5},{5,4},{6,7},{7,6},{8,9},{9,8},{10,11... | collective-permute-start | bytes 5308424 | tf_op jit(solution)/shard_map/ppermute | solution.py:327
  316.4 6.5 %collective-permute-start.55 = (bf16[112,384]{1,0:T(8,128)(2,1)S(1)}, bf16[112,384]{1,0:T(8,128)(2,1)S(1)}, u32[]{:S(2)}, u32[]{:S(2)}) collective-permute-start(bf16[112,384]{1,0:T(8,128)(2,1)S(1)} %get-tuple-element.167), channel_id=1, source_target_pairs={{0,160},{32,128},{64,224},{96,192},{128,32},{160,0},{192,96},{224,... | collective-permute-start | bytes 258056 | tf_op jit(solution)/shard_map/ppermute | solution.py:369
  339.0 111.9 %reduce-scatter.3.cloned.1.call-start = ((), (), s32[]{:S(2)}) async-start(), calls=%async_computation.6 | async-start | bytes 3981312 | tf_op jit(solution)/shard_map/reduce_scatter | solution.py:496
  340.2 6.7 %collective-permute-start.61 = (bf16[112,384]{1,0:T(8,128)(2,1)}, bf16[112,384]{1,0:T(8,128)(2,1)S(1)}, u32[]{:S(2)}, u32[]{:S(2)}) collective-permute-start(bf16[112,384]{1,0:T(8,128)(2,1)} %copy-done.112), channel_id=1, source_target_pairs={{0,160},{32,128},{64,224},{96,192},{128,32},{160,0},{192,96},{224,... | collective-permute-start | bytes 258056 | tf_op jit(solution)/shard_map/ppermute | solution.py:369
  362.0 8.0 %collective-permute-start.64 = (bf16[112,384]{1,0:T(8,128)(2,1)S(1)}, bf16[112,384]{1,0:T(8,128)(2,1)S(1)}, u32[]{:S(2)}, u32[]{:S(2)}) collective-permute-start(bf16[112,384]{1,0:T(8,128)(2,1)S(1)} %get-tuple-element.188), channel_id=1, source_target_pairs={{0,96},{32,64},{64,160},{96,128},{128,224},{160,192},{192,32},{224... | collective-permute-start | bytes 258056 | tf_op jit(solution)/shard_map/ppermute | solution.py:369
  363.4 6.6 %collective-permute-start.65 = (bf16[112,384]{1,0:T(8,128)(2,1)S(1)}, bf16[112,384]{1,0:T(8,128)(2,1)S(1)}, u32[]{:S(2)}, u32[]{:S(2)}) collective-permute-start(bf16[112,384]{1,0:T(8,128)(2,1)S(1)} %get-tuple-element.190), channel_id=1, source_target_pairs={{0,160},{32,128},{64,224},{96,192},{128,32},{160,0},{192,96},{224,... | collective-permute-start | bytes 258056 | tf_op jit(solution)/shard_map/ppermute | solution.py:369
  377.2 10.6 %collective-permute-start.67 = (bf16[112,384]{1,0:T(8,128)(2,1)S(1)}, bf16[112,384]{1,0:T(8,128)(2,1)S(1)}, u32[]{:S(2)}, u32[]{:S(2)}) collective-permute-start(bf16[112,384]{1,0:T(8,128)(2,1)S(1)} %get-tuple-element.193), channel_id=1, source_target_pairs={{0,32},{32,0},{64,96},{96,64},{128,160},{160,128},{192,224},{224,1... | collective-permute-start | bytes 258056 | tf_op jit(solution)/shard_map/ppermute | solution.py:369
  378.1 9.7 %collective-permute-start.68 = (bf16[112,384]{1,0:T(8,128)(2,1)S(1)}, bf16[112,384]{1,0:T(8,128)(2,1)S(1)}, u32[]{:S(2)}, u32[]{:S(2)}) collective-permute-start(bf16[112,384]{1,0:T(8,128)(2,1)S(1)} %get-tuple-element.194), channel_id=1, source_target_pairs={{0,96},{32,64},{64,160},{96,128},{128,224},{160,192},{192,32},{224... | collective-permute-start | bytes 258056 | tf_op jit(solution)/shard_map/ppermute | solution.py:369
  378.1 9.7 %collective-permute-start.69 = (bf16[112,384]{1,0:T(8,128)(2,1)S(1)}, bf16[112,384]{1,0:T(8,128)(2,1)S(1)}, u32[]{:S(2)}, u32[]{:S(2)}) collective-permute-start(bf16[112,384]{1,0:T(8,128)(2,1)S(1)} %get-tuple-element.195), channel_id=1, source_target_pairs={{0,160},{32,128},{64,224},{96,192},{128,32},{160,0},{192,96},{224,... | collective-permute-start | bytes 258056 | tf_op jit(solution)/shard_map/ppermute | solution.py:369
  382.5 16.5 %collective-permute-start.72 = (bf16[8,2,48,1152]{3,2,1,0:T(8,128)(2,1)S(1)}, bf16[8,2,48,1152]{3,2,1,0:T(8,128)(2,1)S(1)}, u32[]{:S(2)}, u32[]{:S(2)}) collective-permute-start(bf16[8,2,48,1152]{3,2,1,0:T(8,128)(2,1)S(1)} %slice_bitcast_fusion.2), channel_id=1, source_target_pairs={{0,1},{1,0},{2,3},{3,2},{4,5},{5,4},{6,7},{7,6},{8,9},{9,8},{10,11... | collective-permute-start | bytes 5308424 | tf_op jit(solution)/shard_map/ppermute | solution.py:327
  394.1 8.1 %collective-permute-start.71 = (bf16[8,2,48,1152]{3,2,1,0:T(8,128)(2,1)S(1)}, bf16[8,2,48,1152]{3,2,1,0:T(8,128)(2,1)S(1)}, u32[]{:S(2)}, u32[]{:S(2)}) collective-permute-start(bf16[8,2,48,1152]{3,2,1,0:T(8,128)(2,1)S(1)} %slice_bitcast_fusion), channel_id=1, source_target_pairs={{0,1},{1,0},{2,3},{3,2},{4,5},{5,4},{6,7},{7,6},{8,9},{9,8},{10,11... | collective-permute-start | bytes 5308424 | tf_op jit(solution)/shard_map/ppermute | solution.py:327
  (170 other events, 1172.3 us)
Sparse Core Ops, SparseCore 0:
  31.0 49.0 all-gather.2
  81.9 47.4 all-gather.4
  339.1 47.5 reduce-scatter.4
  405.2 45.5 reduce-scatter.2

commit v4 on v3

--- a/solution.py
+++ b/solution.py
@@ -20,7 +20,7 @@
 VMEM_LIMIT = 16 * 1024 * 1024
 VM = pl.BlockSpec(memory_space=pltpu.VMEM)
 SM = pl.BlockSpec(memory_space=pltpu.SMEM)
-ANY = pl.BlockSpec(memory_space=pl.ANY)
+HBM = pl.BlockSpec(memory_space=pltpu.HBM)
 
 
 def place(scal, k):
@@ -127,6 +127,8 @@
         def _():
             from_chunks(ins[1:])
 
+
+def whole(hs):
     return jnp.concatenate([hs[t].astype(F32) for t in range(QUART)], axis=1)
 
 
@@ -136,7 +138,8 @@
     pieces, refs = refs[2 : 2 + n_w], refs[2 + n_w :]
     if send:
         out_ref, refs = refs[0], refs[1:]
-    normed_out, proj_out, normed_ref, proj_ref, wscr, hs, sem, sems = refs
+    hidden_out, normed_out, proj_out, normed_ref, proj_ref, wscr, hs, sem, sems = refs
+    hidden_save = pltpu.make_async_copy(hs, hidden_out, sems.at[2])
     normed_save = pltpu.make_async_copy(normed_ref, normed_out, sems.at[0])
     proj_save = pltpu.make_async_copy(proj_ref, proj_out, sems.at[1])
     y = scal[0]
@@ -145,7 +148,9 @@
     chunk = hs.shape[2]
     rows, width = normed_ref.shape
     seq = rows // PAIR
-    normal, _ = standardize(load_hidden(scal, ins, hs))
+    load_hidden(scal, ins, hs)
+    hidden_save.start()
+    normal, _ = standardize(whole(hs))
     normal = normal.reshape(PAIR, seq, width)
     normed = jnp.concatenate(
         [
@@ -167,6 +172,7 @@
     proj_save.start()
     if not send:
         normed_save.wait()
+        hidden_save.wait()
         proj_save.wait()
         return
     own = hs[y].astype(F32)
@@ -187,20 +193,24 @@
             first = hs_rows
     out_ref[...] = jnp.concatenate([first, hs_rows], axis=0).astype(BF16)
     normed_save.wait()
+    hidden_save.wait()
     proj_save.wait()
 
 
-def backward_kernel(k, n_in, n_hid, n_w, send, scal, *refs):
+def backward_kernel(k, n_in, n_w, send, scal, *refs):
     ins, refs = refs[:n_in], refs[n_in:]
-    hidden, refs = refs[:n_hid], refs[n_hid:]
-    mods, gates, proj_ref = refs[:3]
-    pieces, refs = refs[3 : 3 + n_w], refs[3 + n_w :]
+    mods, gates, hidden, projected = refs[:4]
+    pieces, refs = refs[4 : 4 + n_w], refs[4 + n_w :]
     outs, refs = refs[: QUART * send], refs[QUART * send :]
-    low_out, low_ref, wscr, hs, gs, dp, ds, sem, low_sem = refs
-    low_save = pltpu.make_async_copy(low_ref, low_out, low_sem)
+    low_out, low_ref, proj_ref, wscr, hs, gs, dp, ds, sem, sems = refs
+    low_save = pltpu.make_async_copy(low_ref, low_out, sems.at[0])
+    proj_load = pltpu.make_async_copy(projected, proj_ref, sems.at[1])
+    proj_load.start()
     y = scal[0]
     micro, j, slot = place(scal, k)
     if send:
+        hidden_load = pltpu.make_async_copy(hidden, hs, sems.at[2])
+        hidden_load.start()
         fetch_weights(scal, j, pieces, wscr, sem)
     rows, chunk = gs.shape
     width = chunk * QUART
@@ -221,6 +231,7 @@
         def _():
             total(ins[1:])
 
+    proj_load.wait()
     root = 1.0 / math.sqrt(HDIM)
     for s in range(PAIR):
         length = scal[3 + PAIR * micro + s]
@@ -249,7 +260,8 @@
     if not send:
         low_save.wait()
         return
-    normal, scale = standardize(load_hidden(scal, hidden, hs))
+    hidden_load.wait()
+    normal, scale = standardize(whole(hs))
     await_weights(wscr, sem)
     halves = wscr.shape[0]
     norm_grad = jnp.concatenate([nt(low, half_weights(wscr, t)) for t in range(halves)], axis=1)
@@ -270,7 +282,7 @@
     low_save.wait()
 
 
-def weight_grad_kernel(scal, n0, n1, n2, g0, g1, g2, out, nscr, gscr, sems):
+def weight_grad_kernel(scal, n0, n1, n2, g0, g1, g2, out, nscr, gscr, held, sems):
     c = scal[1]
     rows = n0.shape[0]
 
@@ -293,24 +305,34 @@
     pltpu.make_async_copy(g0, gscr.at[0:rows], sems.at[1]).wait()
     pltpu.make_async_copy(n1, nscr.at[rows : 2 * rows], sems.at[2]).wait()
     pltpu.make_async_copy(g1, gscr.at[rows : 2 * rows], sems.at[3]).wait()
-    cores, depth, halves, share, _ = out.shape
-    width = nscr.shape[1]
-    per = 384
-    groups = per // share
+    share = out.shape[3]
+    depth = out.shape[1]
+    steps, cores, count = held.shape[:3]
+    per = cores * count * share
     right = gscr[...]
-    for t in range(width // per):
+    saves = []
+    for t in range(steps):
         value = tn(nscr[:, t * per : (t + 1) * per], right).astype(BF16)
-        for u in range(groups):
-            at = t * groups + u
-            core = at % cores
-            half, z = divmod(at // cores, depth)
-            where = lax.rem(core + c, cores)
-            out[where, z, half] = value[u * share : (u + 1) * share]
+        half, z = divmod(t * count, depth)
+        for core in range(cores):
+            for u in range(count):
+                at = (u * cores + core) * share
+                held[t, core, u] = value[at : at + share]
+            save = pltpu.make_async_copy(
+                held.at[t, core],
+                out.at[lax.rem(core + c, cores), z : z + count, half],
+                sems.at[4 + t * cores + core],
+            )
+            save.start()
+            saves.append(save)
+    for save in saves:
+        save.wait()
 
 
 def shards(latents, out_grad, w_qkv, mod_table, timesteps, text_len):
     y = lax.axis_index("y")
-    p = lax.axis_index("xl")
+    p = lax.rem(lax.axis_index("xl") + y, 2)
+    half = lax.axis_index("xh")
     core = lax.axis_index("c")
     halves = lax.axis_size("xh")
     depth = lax.axis_size("z")
@@ -321,29 +343,60 @@
     cols = 3 * chunk
     rows = PAIR * seq
     nj = BLOCKS // 2
+    count_z = max(384 // (cores * share), 1)
+    strips = width // (cores * count_z * share)
     levels = mod_table.shape[1]
 
     def swap(value, axis):
         return lax.ppermute(value, axis, [(0, 1), (1, 0)])
 
+    fine = ("y", "xl", "xh")
+
+    def route(dx, dy, back, group):
+        pairs = []
+        for yy in range(QUART):
+            to = (yy + dy) % QUART
+            if group is not None and to // 2 != group:
+                continue
+            for xx in range(2):
+                there = (xx + (yy if back else to)) % 2
+                for hh in range(halves):
+                    pairs.append(
+                        (
+                            (yy * 2 + xx) * halves + hh,
+                            (to * 2 + there) * halves + (hh + dx) % halves,
+                        )
+                    )
+        return pairs
+
+    def pick(stack, index):
+        return lax.dynamic_index_in_dim(stack, index, 0, keepdims=False)
+
     quarters = w_qkv[0].reshape(share, 3, QUART, chunk).transpose(2, 0, 1, 3)
-    quarters = quarters.reshape(QUART, 1, share, cols)
-    quarters = jnp.broadcast_to(quarters, (QUART, halves, share, cols))
-    quarters = quarters.reshape(QUART * halves, share, cols)
-    both = lax.all_to_all(quarters, ("y", "xh"), 0, 0).reshape(nj, halves, share, cols)
-    gathered = [lax.all_gather(both[2 * g : 2 * g + 2], "z", axis=0) for g in range(nj // 2)]
+    quarters = quarters.reshape(QUART, share, cols)
+    leaves = [pick(quarters, lax.rem(y + dy, QUART)) for dy in range(QUART)]
+    arrived = [
+        [lax.ppermute(leaves[dy], fine, route(dx, dy, False, None)) for dy in range(QUART)]
+        for dx in range(halves)
+    ]
+    arrived = [jnp.stack(row) for row in arrived]
+    gathered = []
+    for g in range(nj // 2):
+        part = []
+        for j in (2 * g, 2 * g + 1):
+            mine = [pick(arrived[dx], lax.rem(y + QUART - j, QUART)) for dx in range(halves)]
+            if halves == 2:
+                mine = [jnp.where(half == h, mine[0], mine[1]) for h in range(2)]
+            part.append(jnp.stack(mine))
+        gathered.append(lax.all_gather(jnp.stack(part), "z", axis=0))
 
     onehot = (timesteps[:, 0][:, None] == jnp.arange(levels, dtype=jnp.int32)[None, :]).astype(F32)
-    table, _ = lax.optimization_barrier((mod_table, both))
+    table, _ = lax.optimization_barrier((mod_table, arrived[0]))
     modulations = jnp.dot(
         onehot, table[0].reshape(levels, 3 * width), precision=lax.Precision.HIGHEST
     ).reshape(count, 3, width)
     mods = jnp.stack(
-        [modulations]
-        + [
-            lax.ppermute(modulations, "y", [(yy, (yy + dy) % QUART) for yy in range(QUART)])
-            for dy in range(1, QUART)
-        ]
+        [lax.ppermute(modulations, fine, route(0, dy, False, None)) for dy in range(QUART)]
     )
     first, mods = lax.optimization_barrier((gathered[0], mods))
     pieces = [(first, swap(first, "c"))]
@@ -358,9 +411,9 @@
 
     routes = [
         [
-            (yy * 2 + pp, ((yy + d) % QUART) * 2 + (1 - pp))
+            (yy * 2 + xx, ((yy + d) % QUART) * 2 + (1 + xx + d) % 2)
             for yy in range(QUART)
-            for pp in range(2)
+            for xx in range(2)
         ]
         for d in range(QUART)
     ]
@@ -393,21 +446,22 @@
             ins = received
         weights = held(k)
         sending = k < steps - 1
-        outs = [shape(width, BF16), shape(cols, F32)]
+        state = jax.ShapeDtypeStruct((QUART, rows, chunk), BF16)
+        outs = [state, shape(width, BF16), shape(cols, F32)]
         if sending:
             outs = [shape(chunk, BF16)] + outs
         result = pl.pallas_call(
             functools.partial(forward_kernel, k, len(ins), len(weights), sending),
             out_shape=outs,
-            in_specs=[SM] + [VM] * (len(ins) + 2) + [ANY] * len(weights),
-            out_specs=[VM] * sending + [ANY] * 2,
+            in_specs=[SM] + [VM] * (len(ins) + 2) + [HBM] * len(weights),
+            out_specs=[VM] * sending + [HBM] * 3,
             scratch_shapes=[
                 pltpu.VMEM((rows, width), BF16),
                 pltpu.VMEM((rows, cols), F32),
                 wscr,
                 pltpu.VMEM((QUART, rows, chunk), BF16),
                 pltpu.SemaphoreType.DMA,
-                pltpu.SemaphoreType.DMA((2,)),
+                pltpu.SemaphoreType.DMA((3,)),
             ],
             compiler_params=params,
             name="forward_step",
@@ -418,7 +472,7 @@
         if k == 2:
             second, _ = lax.optimization_barrier((gathered[1], received[0]))
             pieces.append((second, swap(second, "c")))
-        saved.append((ins, *result))
+        saved.append(result)
 
     lows = [None] * steps
     chips = [None] * nj
@@ -435,27 +489,25 @@
         sending = k > 0
         outs = [shape(chunk, BF16)] * (QUART * sending) + [shape(cols, BF16)]
         hidden, _, projected = saved[k]
-        sources = len(ins) + len(hidden) + 3
         result = pl.pallas_call(
-            functools.partial(
-                backward_kernel, k, len(ins), len(hidden), len(weights), sending
-            ),
+            functools.partial(backward_kernel, k, len(ins), len(weights), sending),
             out_shape=outs,
-            in_specs=[SM] + [VM] * sources + [ANY] * len(weights),
-            out_specs=[VM] * (len(outs) - 1) + [ANY],
+            in_specs=[SM] + [VM] * (len(ins) + 2) + [HBM] * (2 + len(weights)),
+            out_specs=[VM] * (len(outs) - 1) + [HBM],
             scratch_shapes=[
                 pltpu.VMEM((rows, cols), BF16),
+                pltpu.VMEM((rows, cols), F32),
                 wscr,
                 pltpu.VMEM((QUART, rows, chunk), BF16),
                 pltpu.VMEM((rows, chunk), F32),
                 pltpu.VMEM((rows, cols), F32),
                 pltpu.VMEM((QUART, rows, chunk), F32),
                 pltpu.SemaphoreType.DMA,
-                pltpu.SemaphoreType.DMA,
+                pltpu.SemaphoreType.DMA((3,)),
             ],
             compiler_params=params,
             name="backward_step",
-        )(scal, *ins, *hidden, mods, gates, projected, *weights)
+        )(scal, *ins, mods, gates, hidden, projected, *weights)
         lows[k] = result[-1]
         if sending:
             received = send(result[:-1])
@@ -467,12 +519,13 @@
             partial = pl.pallas_call(
                 weight_grad_kernel,
                 out_shape=jax.ShapeDtypeStruct((cores, depth, halves, share, cols), BF16),
-                in_specs=[SM] + [ANY] * 6,
-                out_specs=VM,
+                in_specs=[SM] + [HBM] * 6,
+                out_specs=HBM,
                 scratch_shapes=[
                     pltpu.VMEM((2 * rows, width), BF16),
                     pltpu.VMEM((2 * rows, cols), BF16),
-                    pltpu.SemaphoreType.DMA((4,)),
+                    pltpu.VMEM((strips, cores, count_z, share, cols), BF16),
+                    pltpu.SemaphoreType.DMA((4 + strips * cores,)),
                 ],
                 compiler_params=params,
                 cost_estimate=pl.CostEstimate(
@@ -487,16 +540,38 @@
             chips[j] = (partial[0], swap(partial[1], "c"))
         if k in (0, 3):
             g = k // 3
-            total = jnp.stack([chips[2 * g + i][0] + chips[2 * g + i][1] for i in range(2)], axis=1)
-            total = total.reshape(depth, 2 * halves * share, cols)
+            total = jnp.concatenate(
+                [
+                    (chips[i][0] + chips[i][1]).reshape(depth, halves * share, cols)
+                    for i in (2 * g, 2 * g + 1)
+                ],
+                axis=1,
+            )
             if sending:
                 total, received[1] = lax.optimization_barrier((total, received[1]))
             else:
-                total, _ = lax.optimization_barrier((total, rings[1]))
+                total, rings[1] = lax.optimization_barrier((total, rings[1]))
             rings[g] = lax.psum_scatter(total, "z", scatter_dimension=0)
-    spread = jnp.stack(rings).reshape(nj * halves, share, cols)
-    quarters = lax.all_to_all(spread, ("y", "xh"), 0, 0).reshape(QUART, halves, share, 3, chunk)
-    grads = jnp.sum(quarters.astype(F32), axis=1).transpose(1, 2, 0, 3)
+
+    def hand_back(g):
+        ring = rings[g].reshape(2 * halves, share, cols)
+        parts = []
+        for dy in range(QUART):
+            for dx in range(halves):
+                index = lax.rem(y + dy, 2) * halves + lax.rem(half + dx, halves)
+                parts.append(lax.ppermute(pick(ring, index), fine, route(dx, dy, True, g)))
+        return parts
+
+    upper = hand_back(1)
+    rings[0], upper = lax.optimization_barrier((rings[0], upper))
+    lower = hand_back(0)
+    finals = []
+    for dy in range(QUART):
+        near = slice(dy * halves, (dy + 1) * halves)
+        parts = [part.astype(F32) for part in upper[near] + lower[near]]
+        finals.append(sum(parts).reshape(share, 3, chunk))
+    finals = jnp.stack(finals)
+    grads = jnp.stack([pick(finals, lax.rem(y + QUART - q, QUART)) for q in range(QUART)], axis=2)
     return grads.reshape(1, share, 3 * width)
 
 

time: 493 us -> 496 us (level)
  the two profiles are of different devices: /device:TPU:1 before, /device:TPU:8 now
where the time goes in v4:
time: 496 us; the launch traced here: 486 us
  waiting for transfers between devices  155 us (31%)
  starting transfers between devices  154 us (31%)
  Pallas kernels  105 us (21%)
  local copies, waits for them, and re-layouts  46.5 us (9%)
  between operations  14.7 us (3%)
  other arithmetic  10.7 us (2%)
    ppermute x64, starting transfers between devices, send(): lax.ppermute(parts[d], ('y', 'xl'), routes[d])  96 us
    ppermute x64, waiting for transfers between devices, send(): lax.ppermute(parts[d], ('y', 'xl'), routes[d])  60.6 us
    pallas_call x9, Pallas kernels, shards(): pl.pallas_call(functools.partial(backward_kernel, k, len(ins), len(weight...  51.7 us
    all_gather x2, waiting for transfers between devices, shards(): gathered.append(lax.all_gather(jnp.stack(part), 'z', axis=0))  38.3 us
    unnamed x162, local copies, waits for them, and re-layouts  36.5 us
    pallas_call x9, Pallas kernels, shards(): pl.pallas_call(functools.partial(forward_kernel, k, len(ins), len(weights...  35.4 us
    ppermute x16, starting transfers between devices, hand_back(): parts.append(lax.ppermute(pick(ring, index), fine, route(dx, dy, True, g)))  32.9 us
    reduce_scatter x2, waiting for transfers between devices, shards(): rings[g] = lax.psum_scatter(total, 'z', scatter_dimension=0)  27.7 us
  transfers between devices with their start and end apart: 102, of which 48 were waited for; matrix products, arithmetic and copies ran while one was open for 3% of the time, Pallas kernels for 12%

profile of v4, /device:TPU:8, one launch (start us, length us, event | category | flops | bytes accessed | tf_op | source)
XLA Modules:
  0.0 486.1 jit_solution(4151452689073546453)
XLA Ops:
  44.2 38.3 %all-gather.5.cloned.1.call-done = bf16[16,2,48,1152]{3,2,1,0:T(8,128)(2,1)} async-done(((bf16[2,2,48,1152]{3,2,1,0:T(8,128)(2,1)}), bf16[16,2,48,1152]{3,2,1,0:T(8,128)(2,1)}) %all-gather.5.cloned.1.call-update) | async-done | bytes 3538960 | tf_op jit(solution)/shard_map/all_gather | solution.py:391
  84.9 4.0 collective-permute-done.12.refs_4_.refs_8_.refs_7_.refs_9_.refs_11_
  125.1 4.5 forward_step.11
  150.7 4.3 forward_step.12
  195.3 4.5 forward_step.15
  217.2 4.3 forward_step.16
  233.9 5.8 %backward_step.9 = (bf16[112,384]{1,0:T(8,128)(2,1)S(1)}, bf16[112,384]{1,0:T(8,128)(2,1)S(1)}, bf16[112,384]{1,0:T(8,128)(2,1)S(1)}, bf16[112,384]{1,0:T(8,128)(2,1)S(1)}, bf16[112,1152]{1,0:T(8,128)(2,1)S(1)}) custom-call(s32[7]{0:T(128)S(1)} %pad_add_fusion.scal, bf16[112,384]{1,0:T(8,128)(2,1)S(1)} %get-tuple-element.255.refs_0_, ...), custom_call_target="tpu_custom_call" | custom-call | tf_op jit(solution)/shard_map/backward_step/pallas_call | solution.py:492
  249.5 5.8 %backward_step.10 = (bf16[112,384]{1,0:T(8,128)(2,1)S(1)}, bf16[112,384]{1,0:T(8,128)(2,1)S(1)}, bf16[112,384]{1,0:T(8,128)(2,1)S(1)}, bf16[112,384]{1,0:T(8,128)(2,1)S(1)}, bf16[112,1152]{1,0:T(8,128)(2,1)S(1)}) custom-call(s32[7]{0:T(128)S(1)} %pad_add_fusion.scal, bf16[112,384]{1,0:T(8,128)(2,1)S(1)} %get-tuple-element.256.refs_0_, ...), custom_call_target="tpu_custom_call" | custom-call | tf_op jit(solution)/shard_map/backward_step/pallas_call | solution.py:492
  264.7 5.9 %backward_step.11 = (bf16[112,384]{1,0:T(8,128)(2,1)S(1)}, bf16[112,384]{1,0:T(8,128)(2,1)S(1)}, bf16[112,384]{1,0:T(8,128)(2,1)S(1)}, bf16[112,384]{1,0:T(8,128)(2,1)S(1)}, bf16[112,1152]{1,0:T(8,128)(2,1)S(1)}) custom-call(s32[7]{0:T(128)S(1)} %pad_add_fusion.scal, bf16[112,384]{1,0:T(8,128)(2,1)S(1)} %collective-permute-done.50.refs_0_, ...), custom_call_target="tpu_custom_call" | custom-call | tf_op jit(solution)/shard_map/backward_step/pallas_call | solution.py:492
  277.5 4.5 weight_grad.4
  282.1 5.9 %backward_step.12 = (bf16[112,384]{1,0:T(8,128)(2,1)S(1)}, bf16[112,384]{1,0:T(8,128)(2,1)S(1)}, bf16[112,384]{1,0:T(8,128)(2,1)S(1)}, bf16[112,384]{1,0:T(8,128)(2,1)S(1)}, bf16[112,1152]{1,0:T(8,128)(2,1)S(1)}) custom-call(s32[7]{0:T(128)S(1)} %pad_add_fusion.scal, bf16[112,384]{1,0:T(8,128)(2,1)S(1)} %collective-permute-done.54.refs_0_, ...), custom_call_target="tpu_custom_call" | custom-call | tf_op jit(solution)/shard_map/backward_step/pallas_call | solution.py:492
  297.7 5.9 %backward_step.13 = (bf16[112,384]{1,0:T(8,128)(2,1)S(1)}, bf16[112,384]{1,0:T(8,128)(2,1)S(1)}, bf16[112,384]{1,0:T(8,128)(2,1)S(1)}, bf16[112,384]{1,0:T(8,128)(2,1)S(1)}, bf16[112,1152]{1,0:T(8,128)(2,1)S(1)}) custom-call(s32[7]{0:T(128)S(1)} %pad_add_fusion.scal, bf16[112,384]{1,0:T(8,128)(2,1)S(1)} %collective-permute-done.58.refs_0_, ...), custom_call_target="tpu_custom_call" | custom-call | tf_op jit(solution)/shard_map/backward_step/pallas_call | solution.py:492
  308.2 4.5 weight_grad.5
  316.3 4.2 collective-permute-done.64.refs_2_
  322.3 6.5 %backward_step.14 = (bf16[112,384]{1,0:T(8,128)(2,1)S(1)}, bf16[112,384]{1,0:T(8,128)(2,1)}, bf16[112,384]{1,0:T(8,128)(2,1)S(1)}, bf16[112,384]{1,0:T(8,128)(2,1)S(1)}, bf16[112,1152]{1,0:T(8,128)(2,1)S(1)}) custom-call(s32[7]{0:T(128)S(1)} %pad_add_fusion.scal, bf16[112,384]{1,0:T(8,128)(2,1)S(1)} %collective-permute-done.62.refs_0_, ...), custom_call_target="tpu_custom_call" | custom-call | tf_op jit(solution)/shard_map/backward_step/pallas_call | solution.py:492
  350.7 6.3 %backward_step.15 = (bf16[112,384]{1,0:T(8,128)(2,1)S(1)}, bf16[112,384]{1,0:T(8,128)(2,1)S(1)}, bf16[112,384]{1,0:T(8,128)(2,1)S(1)}, bf16[112,384]{1,0:T(8,128)(2,1)S(1)}, bf16[112,1152]{1,0:T(8,128)(2,1)S(1)}) custom-call(s32[7]{0:T(128)S(1)} %pad_add_fusion.scal, bf16[112,384]{1,0:T(8,128)(2,1)S(1)} %collective-permute-done.66.refs_0_, ...), custom_call_target="tpu_custom_call" | custom-call | tf_op jit(solution)/shard_map/backward_step/pallas_call | solution.py:492
  364.2 4.3 weight_grad.6
  368.6 5.9 %backward_step.16 = (bf16[112,384]{1,0:T(8,128)(2,1)S(1)}, bf16[112,384]{1,0:T(8,128)(2,1)S(1)}, bf16[112,384]{1,0:T(8,128)(2,1)S(1)}, bf16[112,384]{1,0:T(8,128)(2,1)S(1)}, bf16[112,1152]{1,0:T(8,128)(2,1)S(1)}) custom-call(s32[7]{0:T(128)S(1)} %pad_add_fusion.scal, bf16[112,384]{1,0:T(8,128)(2,1)S(1)} %collective-permute-done.72.refs_0_, ...), custom_call_target="tpu_custom_call" | custom-call | tf_op jit(solution)/shard_map/backward_step/pallas_call | solution.py:492
  387.1 4.5 weight_grad.7
  400.5 8.7 %collective-permute-start.87 = (bf16[48,1152]{1,0:T(8,128)(2,1)S(1)}, bf16[48,1152]{1,0:T(8,128)(2,1)S(1)}, u32[]{:S(2)}, u32[]{:S(2)}) collective-permute-start(bf16[48,1152]{1,0:T(8,128)(2,1)S(1)} %get-tuple-element.269), channel_id=1, source_target_pairs={{0,144},{16,128},{32,176},{48,160},{64,240},{80,224},{96,208},{112... | collective-permute-start | bytes 331784 | tf_op jit(solution)/shard_map/ppermute | solution.py:562
  418.1 27.7 %reduce-scatter.5.cloned.1.call-done = bf16[1,192,1152]{2,1,0:T(8,128)(2,1)} async-done(((bf16[8,192,1152]{2,1,0:T(8,128)(2,1)}), bf16[1,192,1152]{2,1,0:T(8,128)(2,1)}) %reduce-scatter.5.cloned.1.call-update) | async-done | bytes 442384 | tf_op jit(solution)/shard_map/reduce_scatter | solution.py:554
  447.1 4.6 collective-permute-start.97
  461.1 6.5 %collective-permute-done.95 = bf16[48,1152]{1,0:T(8,128)(2,1)S(1)} collective-permute-done((bf16[48,1152]{1,0:T(8,128)(2,1)S(1)}, bf16[48,1152]{1,0:T(8,128)(2,1)S(1)}, u32[]{:S(2)}, u32[]{:S(2)}) %collective-permute-start.95) | collective-permute-done | bytes 110624 | tf_op jit(solution)/shard_map/ppermute | solution.py:562
  470.8 4.6 collective-permute-done.91
  (412 shorter events, 289.5 us)
Async XLA Ops:
  6.5 76.0 %all-gather.5.cloned.1.call-start = ((), (), s32[]{:S(2)}) async-start(), calls=%async_computation.4 | async-start | bytes 3981312 | tf_op jit(solution)/shard_map/all_gather | solution.py:391
  8.3 12.3 %collective-permute-start.4 = (bf16[48,1152]{1,0:T(8,128)(2,1)S(1)}, bf16[48,1152]{1,0:T(8,128)(2,1)S(1)}, u32[]{:S(2)}, u32[]{:S(2)}) collective-permute-start(bf16[48,1152]{1,0:T(8,128)(2,1)S(1)} %get-tuple-element.275), channel_id=1, source_target_pairs={{0,16},{16,0},{32,48},{48,32},{64,112},{80,96},{96,80},{112,64},{1... | collective-permute-start | bytes 331784 | tf_op jit(solution)/shard_map/ppermute | solution.py:379
  11.2 9.6 %collective-permute-start.7 = (bf16[48,1152]{1,0:T(8,128)(2,1)S(1)}, bf16[48,1152]{1,0:T(8,128)(2,1)S(1)}, u32[]{:S(2)}, u32[]{:S(2)}) collective-permute-start(bf16[48,1152]{1,0:T(8,128)(2,1)S(1)} %get-tuple-element.276), channel_id=1, source_target_pairs={{0,240},{16,224},{32,208},{48,192},{64,16},{80,0},{96,48},{112,32}... | collective-permute-start | bytes 331784 | tf_op jit(solution)/shard_map/ppermute | solution.py:379
  13.6 10.7 %collective-permute-start.6 = (bf16[48,1152]{1,0:T(8,128)(2,1)S(1)}, bf16[48,1152]{1,0:T(8,128)(2,1)S(1)}, u32[]{:S(2)}, u32[]{:S(2)}) collective-permute-start(bf16[48,1152]{1,0:T(8,128)(2,1)S(1)} %get-tuple-element.277), channel_id=1, source_target_pairs={{0,144},{16,128},{32,176},{48,160},{64,240},{80,224},{96,208},{112... | collective-permute-start | bytes 331784 | tf_op jit(solution)/shard_map/ppermute | solution.py:379
  16.6 9.2 %collective-permute-start.5 = (bf16[48,1152]{1,0:T(8,128)(2,1)S(1)}, bf16[48,1152]{1,0:T(8,128)(2,1)S(1)}, u32[]{:S(2)}, u32[]{:S(2)}) collective-permute-start(bf16[48,1152]{1,0:T(8,128)(2,1)S(1)} %get-tuple-element.278), channel_id=1, source_target_pairs={{0,112},{16,96},{32,80},{48,64},{64,144},{80,128},{96,176},{112,16... | collective-permute-start | bytes 331784 | tf_op jit(solution)/shard_map/ppermute | solution.py:379
  31.1 102.5 %all-gather.7.cloned.1.call-start = ((), (), s32[]{:S(2)}) async-start(), calls=%async_computation.5 | async-start | bytes 3981312 | tf_op jit(solution)/shard_map/all_gather | solution.py:391
  32.0 366.1 %reduce-scatter.3.cloned.1.call-start = ((), (), s32[]{:S(2)}) async-start(), calls=%async_computation.2 | async-start | bytes 3981312 | tf_op jit(solution)/shard_map/reduce_scatter | solution.py:554
  137.3 30.0 %collective-permute-start.29 = (bf16[8,2,2,48,1152]{4,3,2,1,0:T(8,128)(2,1)}, bf16[8,2,2,48,1152]{4,3,2,1,0:T(8,128)(2,1)S(1)}, u32[]{:S(2)}, u32[]{:S(2)}) collective-permute-start(bf16[8,2,2,48,1152]{4,3,2,1,0:T(8,128)(2,1)} %bitcast.137), channel_id=1, source_target_pairs={{0,1},{1,0},{2,3},{3,2},{4,5},{5,4},{6,7},{7,6},{8,9},{9,8},{10,11... | collective-permute-start | bytes 10616840 | tf_op jit(solution)/shard_map/ppermute | solution.py:351
  271.8 10.2 %collective-permute-start.55 = (bf16[112,384]{1,0:T(8,128)(2,1)S(1)}, bf16[112,384]{1,0:T(8,128)(2,1)S(1)}, u32[]{:S(2)}, u32[]{:S(2)}) collective-permute-start(bf16[112,384]{1,0:T(8,128)(2,1)S(1)} %get-tuple-element.170), channel_id=1, source_target_pairs={{0,64},{32,96},{64,128},{96,160},{128,192},{160,224},{192,0},{224,... | collective-permute-start | bytes 258056 | tf_op jit(solution)/shard_map/ppermute | solution.py:422
  305.5 25.4 %collective-permute-start.68 = (bf16[8,2,48,1152]{3,2,1,0:T(8,128)(2,1)S(1)}, bf16[8,2,48,1152]{3,2,1,0:T(8,128)(2,1)S(1)}, u32[]{:S(2)}, u32[]{:S(2)}) collective-permute-start(bf16[8,2,48,1152]{3,2,1,0:T(8,128)(2,1)S(1)} %slice_bitcast_fusion.3), channel_id=1, source_target_pairs={{0,1},{1,0},{2,3},{3,2},{4,5},{5,4},{6,7},{7,6},{8,9},{9,8},{10,11... | collective-permute-start | bytes 5308424 | tf_op jit(solution)/shard_map/ppermute | solution.py:351
  312.9 18.5 %collective-permute-start.67 = (bf16[8,2,48,1152]{3,2,1,0:T(8,128)(2,1)S(1)}, bf16[8,2,48,1152]{3,2,1,0:T(8,128)(2,1)S(1)}, u32[]{:S(2)}, u32[]{:S(2)}) collective-permute-start(bf16[8,2,48,1152]{3,2,1,0:T(8,128)(2,1)S(1)} %slice_bitcast_fusion.4), channel_id=1, source_target_pairs={{0,1},{1,0},{2,3},{3,2},{4,5},{5,4},{6,7},{7,6},{8,9},{9,8},{10,11... | collective-permute-start | bytes 5308424 | tf_op jit(solution)/shard_map/ppermute | solution.py:351
  335.5 110.3 %reduce-scatter.5.cloned.1.call-start = ((), (), s32[]{:S(2)}) async-start(), calls=%async_computation.3 | async-start | bytes 3981312 | tf_op jit(solution)/shard_map/reduce_scatter | solution.py:554
  358.6 9.9 %collective-permute-start.73 = (bf16[112,384]{1,0:T(8,128)(2,1)S(1)}, bf16[112,384]{1,0:T(8,128)(2,1)S(1)}, u32[]{:S(2)}, u32[]{:S(2)}) collective-permute-start(bf16[112,384]{1,0:T(8,128)(2,1)S(1)} %get-tuple-element.217), channel_id=1, source_target_pairs={{0,64},{32,96},{64,128},{96,160},{128,192},{160,224},{192,0},{224,... | collective-permute-start | bytes 258056 | tf_op jit(solution)/shard_map/ppermute | solution.py:422
  358.9 9.6 %collective-permute-start.74 = (bf16[112,384]{1,0:T(8,128)(2,1)S(1)}, bf16[112,384]{1,0:T(8,128)(2,1)S(1)}, u32[]{:S(2)}, u32[]{:S(2)}) collective-permute-start(bf16[112,384]{1,0:T(8,128)(2,1)S(1)} %get-tuple-element.219), channel_id=1, source_target_pairs={{0,160},{32,128},{64,224},{96,192},{128,32},{160,0},{192,96},{224,... | collective-permute-start | bytes 258056 | tf_op jit(solution)/shard_map/ppermute | solution.py:422
  379.5 12.3 %collective-permute-start.81 = (bf16[8,2,48,1152]{3,2,1,0:T(8,128)(2,1)S(1)}, bf16[8,2,48,1152]{3,2,1,0:T(8,128)(2,1)S(1)}, u32[]{:S(2)}, u32[]{:S(2)}) collective-permute-start(bf16[8,2,48,1152]{3,2,1,0:T(8,128)(2,1)S(1)} %slice_bitcast_fusion.2), channel_id=1, source_target_pairs={{0,1},{1,0},{2,3},{3,2},{4,5},{5,4},{6,7},{7,6},{8,9},{9,8},{10,11... | collective-permute-start | bytes 5308424 | tf_op jit(solution)/shard_map/ppermute | solution.py:351
  399.2 12.6 %collective-permute-start.89 = (bf16[48,1152]{1,0:T(8,128)(2,1)S(1)}, bf16[48,1152]{1,0:T(8,128)(2,1)S(1)}, u32[]{:S(2)}, u32[]{:S(2)}) collective-permute-start(bf16[48,1152]{1,0:T(8,128)(2,1)S(1)} %get-tuple-element.267), channel_id=1, source_target_pairs={{0,208},{16,192},{32,240},{48,224},{192,176},{208,160},{224,144},{... | collective-permute-start | bytes 331784 | tf_op jit(solution)/shard_map/ppermute | solution.py:562
  399.9 14.7 %collective-permute-start.88 = (bf16[48,1152]{1,0:T(8,128)(2,1)S(1)}, bf16[48,1152]{1,0:T(8,128)(2,1)S(1)}, u32[]{:S(2)}, u32[]{:S(2)}) collective-permute-start(bf16[48,1152]{1,0:T(8,128)(2,1)S(1)} %get-tuple-element.268), channel_id=1, source_target_pairs={{0,192},{16,208},{32,224},{48,240},{192,160},{208,176},{224,128},{... | collective-permute-start | bytes 331784 | tf_op jit(solution)/shard_map/ppermute | solution.py:562
  400.5 14.8 %collective-permute-start.87 = (bf16[48,1152]{1,0:T(8,128)(2,1)S(1)}, bf16[48,1152]{1,0:T(8,128)(2,1)S(1)}, u32[]{:S(2)}, u32[]{:S(2)}) collective-permute-start(bf16[48,1152]{1,0:T(8,128)(2,1)S(1)} %get-tuple-element.269), channel_id=1, source_target_pairs={{0,144},{16,128},{32,176},{48,160},{64,240},{80,224},{96,208},{112... | collective-permute-start | bytes 331784 | tf_op jit(solution)/shard_map/ppermute | solution.py:562
  447.1 11.3 %collective-permute-start.97 = (bf16[48,1152]{1,0:T(8,128)(2,1)S(1)}, bf16[48,1152]{1,0:T(8,128)(2,1)S(1)}, u32[]{:S(2)}, u32[]{:S(2)}) collective-permute-start(bf16[48,1152]{1,0:T(8,128)(2,1)S(1)} %get-tuple-element.260), channel_id=1, source_target_pairs={{64,48},{80,32},{96,16},{112,0},{128,80},{144,64},{160,112},{176,9... | collective-permute-start | bytes 331784 | tf_op jit(solution)/shard_map/ppermute | solution.py:562
  453.6 17.2 %collective-permute-start.90 = (bf16[48,1152]{1,0:T(8,128)(2,1)S(1)}, bf16[48,1152]{1,0:T(8,128)(2,1)S(1)}, u32[]{:S(2)}, u32[]{:S(2)}) collective-permute-start(bf16[48,1152]{1,0:T(8,128)(2,1)S(1)} %get-tuple-element.259), channel_id=1, source_target_pairs={{0,0},{16,16},{32,32},{48,48},{64,96},{80,112},{96,64},{112,80},{1... | collective-permute-start | bytes 331784 | tf_op jit(solution)/shard_map/ppermute | solution.py:562
  455.8 11.8 %collective-permute-start.95 = (bf16[48,1152]{1,0:T(8,128)(2,1)S(1)}, bf16[48,1152]{1,0:T(8,128)(2,1)S(1)}, u32[]{:S(2)}, u32[]{:S(2)}) collective-permute-start(bf16[48,1152]{1,0:T(8,128)(2,1)S(1)} %get-tuple-element.262), channel_id=1, source_target_pairs={{128,16},{144,0},{160,48},{176,32},{192,112},{208,96},{224,80},{24... | collective-permute-start | bytes 331784 | tf_op jit(solution)/shard_map/ppermute | solution.py:562
  457.1 12.9 %collective-permute-start.94 = (bf16[48,1152]{1,0:T(8,128)(2,1)S(1)}, bf16[48,1152]{1,0:T(8,128)(2,1)S(1)}, u32[]{:S(2)}, u32[]{:S(2)}) collective-permute-start(bf16[48,1152]{1,0:T(8,128)(2,1)S(1)} %get-tuple-element.263), channel_id=1, source_target_pairs={{128,0},{144,16},{160,32},{176,48},{192,96},{208,112},{224,64},{24... | collective-permute-start | bytes 331784 | tf_op jit(solution)/shard_map/ppermute | solution.py:562
  458.4 11.6 %collective-permute-start.93 = (bf16[48,1152]{1,0:T(8,128)(2,1)S(1)}, bf16[48,1152]{1,0:T(8,128)(2,1)S(1)}, u32[]{:S(2)}, u32[]{:S(2)}) collective-permute-start(bf16[48,1152]{1,0:T(8,128)(2,1)S(1)} %get-tuple-element.264), channel_id=1, source_target_pairs={{0,80},{16,64},{32,112},{48,96},{192,48},{208,32},{224,16},{240,0}... | collective-permute-start | bytes 331784 | tf_op jit(solution)/shard_map/ppermute | solution.py:562
  459.7 10.3 %collective-permute-start.92 = (bf16[48,1152]{1,0:T(8,128)(2,1)S(1)}, bf16[48,1152]{1,0:T(8,128)(2,1)S(1)}, u32[]{:S(2)}, u32[]{:S(2)}) collective-permute-start(bf16[48,1152]{1,0:T(8,128)(2,1)S(1)} %get-tuple-element.265), channel_id=1, source_target_pairs={{0,64},{16,80},{32,96},{48,112},{192,32},{208,48},{224,0},{240,16}... | collective-permute-start | bytes 331784 | tf_op jit(solution)/shard_map/ppermute | solution.py:562
  (159 other events, 1017.3 us)
Sparse Core Ops, SparseCore 0:
  31.2 51.2 all-gather.4
  84.3 47.2 all-gather.6
  335.6 47.8 reduce-scatter.2
  398.3 47.5 reduce-scatter.4

commit v5 on v4

--- a/solution.py
+++ b/solution.py
@@ -350,9 +350,9 @@
     def swap(value, axis):
         return lax.ppermute(value, axis, [(0, 1), (1, 0)])
 
-    fine = ("y", "xl", "xh")
-
-    def route(dx, dy, back, group):
+    fine = ("y", "xl")
+
+    def route(dy, back, group):
         pairs = []
         for yy in range(QUART):
             to = (yy + dy) % QUART
@@ -360,13 +360,7 @@
                 continue
             for xx in range(2):
                 there = (xx + (yy if back else to)) % 2
-                for hh in range(halves):
-                    pairs.append(
-                        (
-                            (yy * 2 + xx) * halves + hh,
-                            (to * 2 + there) * halves + (hh + dx) % halves,
-                        )
-                    )
+                pairs.append((yy * 2 + xx, to * 2 + there))
         return pairs
 
     def pick(stack, index):
@@ -375,31 +369,32 @@
     quarters = w_qkv[0].reshape(share, 3, QUART, chunk).transpose(2, 0, 1, 3)
     quarters = quarters.reshape(QUART, share, cols)
     leaves = [pick(quarters, lax.rem(y + dy, QUART)) for dy in range(QUART)]
-    arrived = [
-        [lax.ppermute(leaves[dy], fine, route(dx, dy, False, None)) for dy in range(QUART)]
-        for dx in range(halves)
-    ]
-    arrived = [jnp.stack(row) for row in arrived]
+    arrived = jnp.stack(
+        [lax.ppermute(leaves[dy], fine, route(dy, False, None)) for dy in range(QUART)]
+    )
     gathered = []
     for g in range(nj // 2):
-        part = []
-        for j in (2 * g, 2 * g + 1):
-            mine = [pick(arrived[dx], lax.rem(y + QUART - j, QUART)) for dx in range(halves)]
-            if halves == 2:
-                mine = [jnp.where(half == h, mine[0], mine[1]) for h in range(2)]
-            part.append(jnp.stack(mine))
-        gathered.append(lax.all_gather(jnp.stack(part), "z", axis=0))
+        mine = jnp.stack(
+            [pick(arrived, lax.rem(y + QUART - j, QUART)) for j in (2 * g, 2 * g + 1)]
+        )
+        if g > 0:
+            mine, _ = lax.optimization_barrier((mine, part))
+        if halves == 2:
+            other = swap(mine, "xh")
+            mine = [jnp.where(half == h, mine, other) for h in range(2)]
+            part = jnp.stack(mine, axis=1)
+        else:
+            part = mine[:, None]
+        gathered.append(lax.all_gather(part, "z", axis=0))
 
     onehot = (timesteps[:, 0][:, None] == jnp.arange(levels, dtype=jnp.int32)[None, :]).astype(F32)
-    table, _ = lax.optimization_barrier((mod_table, arrived[0]))
+    table, _ = lax.optimization_barrier((mod_table, arrived))
     modulations = jnp.dot(
         onehot, table[0].reshape(levels, 3 * width), precision=lax.Precision.HIGHEST
     ).reshape(count, 3, width)
     mods = jnp.stack(
-        [lax.ppermute(modulations, fine, route(0, dy, False, None)) for dy in range(QUART)]
-    )
-    first, mods = lax.optimization_barrier((gathered[0], mods))
-    pieces = [(first, swap(first, "c"))]
+        [lax.ppermute(modulations, fine, route(dy, False, None)) for dy in range(QUART)]
+    )
     gates = lax.dynamic_slice_in_dim(mods[:, :, 2:3, :], y * chunk, chunk, axis=3)
     scal = jnp.concatenate(
         [jnp.stack([y, core, p]).astype(jnp.int32), text_len[:, 0].astype(jnp.int32)]
@@ -409,6 +404,8 @@
         out_grad.reshape(count // PAIR, rows, width), y * chunk, chunk, axis=2
     )
 
+    first, mods, gates, entering = lax.optimization_barrier((gathered[0], mods, gates, entering))
+    pieces = [(first, swap(first, "c"))]
     routes = [
         [
             (yy * 2 + xx, ((yy + d) % QUART) * 2 + (1 + xx + d) % 2)
@@ -433,6 +430,12 @@
 
     def shape(cols, kind):
         return jax.ShapeDtypeStruct((rows, cols), kind)
+
+    def kept(dims, kind):
+        return pltpu.HBM(dims, kind)
+
+    def pinned(values):
+        return [pltpu.with_memory_space_constraint(value, pltpu.HBM) for value in values]
 
     steps = BLOCKS + 1
     saved = []
@@ -446,8 +449,11 @@
             ins = received
         weights = held(k)
         sending = k < steps - 1
-        state = jax.ShapeDtypeStruct((QUART, rows, chunk), BF16)
-        outs = [state, shape(width, BF16), shape(cols, F32)]
+        outs = [
+            kept((QUART, rows, chunk), BF16),
+            kept((rows, width), BF16),
+            kept((rows, cols), F32),
+        ]
         if sending:
             outs = [shape(chunk, BF16)] + outs
         result = pl.pallas_call(
@@ -465,12 +471,12 @@
             ],
             compiler_params=params,
             name="forward_step",
-        )(scal, *ins, mods, gates, *weights)
+        )(scal, *ins, mods, gates, *pinned(weights))
         if sending:
             received = send([result[0]] * QUART)
             result = result[1:]
-        if k == 2:
-            second, _ = lax.optimization_barrier((gathered[1], received[0]))
+        if k == 3:
+            second, _ = lax.optimization_barrier((gathered[1], result[1]))
             pieces.append((second, swap(second, "c")))
         saved.append(result)
 
@@ -487,7 +493,7 @@
             ins = received
         weights = held(k)
         sending = k > 0
-        outs = [shape(chunk, BF16)] * (QUART * sending) + [shape(cols, BF16)]
+        outs = [shape(chunk, BF16)] * (QUART * sending) + [kept((rows, cols), BF16)]
         hidden, _, projected = saved[k]
         result = pl.pallas_call(
             functools.partial(backward_kernel, k, len(ins), len(weights), sending),
@@ -507,7 +513,7 @@
             ],
             compiler_params=params,
             name="backward_step",
-        )(scal, *ins, mods, gates, hidden, projected, *weights)
+        )(scal, *ins, mods, gates, *pinned([hidden, projected, *weights]))
         lows[k] = result[-1]
         if sending:
             received = send(result[:-1])
@@ -518,7 +524,7 @@
                 factors, received[0] = lax.optimization_barrier((factors, received[0]))
             partial = pl.pallas_call(
                 weight_grad_kernel,
-                out_shape=jax.ShapeDtypeStruct((cores, depth, halves, share, cols), BF16),
+                out_shape=kept((cores, depth, halves, share, cols), BF16),
                 in_specs=[SM] + [HBM] * 6,
                 out_specs=HBM,
                 scratch_shapes=[
@@ -534,12 +540,21 @@
                     transcendentals=0,
                 ),
                 name="weight_grad",
-            )(scal, *factors)
+            )(scal, *pinned(factors))
             if sending:
                 partial, received[1] = lax.optimization_barrier((partial, received[1]))
-            chips[j] = (partial[0], swap(partial[1], "c"))
-        if k in (0, 3):
-            g = k // 3
+            chips[j] = partial
+        if k in (1, 3, 5):
+            j = (k + 1) // 2
+            chips[j], _ = lax.optimization_barrier((chips[j], lows[k]))
+        if k in (0, 1, 3, 5):
+            j = (k + 1) // 2
+            chips[j] = (chips[j][0], swap(chips[j][1], "c"))
+        if k == 4:
+            keep, received[1] = lax.optimization_barrier((chips[3][1], received[1]))
+            chips[3] = (chips[3][0], keep)
+        if k in (0, 2):
+            g = k // 2
             total = jnp.concatenate(
                 [
                     (chips[i][0] + chips[i][1]).reshape(depth, halves * share, cols)
@@ -554,22 +569,23 @@
             rings[g] = lax.psum_scatter(total, "z", scatter_dimension=0)
 
     def hand_back(g):
-        ring = rings[g].reshape(2 * halves, share, cols)
-        parts = []
-        for dy in range(QUART):
-            for dx in range(halves):
-                index = lax.rem(y + dy, 2) * halves + lax.rem(half + dx, halves)
-                parts.append(lax.ppermute(pick(ring, index), fine, route(dx, dy, True, g)))
-        return parts
+        ring = rings[g].reshape(2, halves, share, cols)
+        ours = lax.dynamic_index_in_dim(ring, half, 1, keepdims=False)
+        if halves == 2:
+            theirs = swap(lax.dynamic_index_in_dim(ring, 1 - half, 1, keepdims=False), "xh")
+            ours = (ours.astype(F32) + theirs.astype(F32)).astype(BF16)
+        return [
+            lax.ppermute(pick(ours, lax.rem(y + dy, 2)), fine, route(dy, True, g))
+            for dy in range(QUART)
+        ]
 
     upper = hand_back(1)
     rings[0], upper = lax.optimization_barrier((rings[0], upper))
     lower = hand_back(0)
-    finals = []
-    for dy in range(QUART):
-        near = slice(dy * halves, (dy + 1) * halves)
-        parts = [part.astype(F32) for part in upper[near] + lower[near]]
-        finals.append(sum(parts).reshape(share, 3, chunk))
+    finals = [
+        (upper[dy].astype(F32) + lower[dy].astype(F32)).reshape(share, 3, chunk)
+        for dy in range(QUART)
+    ]
     finals = jnp.stack(finals)
     grads = jnp.stack([pick(finals, lax.rem(y + QUART - q, QUART)) for q in range(QUART)], axis=2)
     return grads.reshape(1, share, 3 * width)

time: 496 us -> 477 us (0.962)
  the two profiles are of different devices: /device:TPU:8 before, /device:TPU:4 now
where the time goes in v5:
time: 477 us; the launch traced here: 468 us
  waiting for transfers between devices  188 us (39%)
  starting transfers between devices  122 us (26%)
  Pallas kernels  119 us (25%)
  local copies, waits for them, and re-layouts  14.2 us (3%)
  between operations  14.2 us (3%)
  other arithmetic  10.5 us (2%)
    ppermute x64, starting transfers between devices, send(): lax.ppermute(parts[d], ('y', 'xl'), routes[d])  89.9 us
    pallas_call x9, Pallas kernels, shards(): pl.pallas_call(functools.partial(backward_kernel, k, len(ins), len(weight...  58.2 us
    ppermute x64, waiting for transfers between devices, send(): lax.ppermute(parts[d], ('y', 'xl'), routes[d])  57.7 us
    pallas_call x9, Pallas kernels, shards(): pl.pallas_call(functools.partial(forward_kernel, k, len(ins), len(weights...  43.5 us
    ppermute x10, waiting for transfers between devices, swap(): return lax.ppermute(value, axis, [(0, 1), (1, 0)])  41 us
    reduce_scatter x2, waiting for transfers between devices, shards(): rings[g] = lax.psum_scatter(total, 'z', scatter_dimension=0)  37.5 us
    all_gather x2, waiting for transfers between devices, shards(): gathered.append(lax.all_gather(part, 'z', axis=0))  34 us
    ppermute x8, starting transfers between devices, hand_back(): lax.ppermute(pick(ours, lax.rem(y + dy, 2)), fine, route(dy, True, g))  17.3 us
  transfers between devices with their start and end apart: 94, of which 53 were waited for; matrix products, arithmetic and copies ran while one was open for 2% of the time, Pallas kernels for 12%

profile of v5, /device:TPU:4, one launch (start us, length us, event | category | flops | bytes accessed | tf_op | source)
XLA Modules:
  0.0 468.2 jit_solution(5307885963721427751)
XLA Ops:
  9.0 5.8 %collective-permute-start.3 = (bf16[48,1152]{1,0:T(8,128)(2,1)S(1)}, bf16[48,1152]{1,0:T(8,128)(2,1)S(1)}, u32[]{:S(2)}, u32[]{:S(2)}) collective-permute-start(bf16[48,1152]{1,0:T(8,128)(2,1)S(1)} %get-tuple-element.268), channel_id=1, source_target_pairs={{0,224},{32,192},{64,0},{96,32},{128,96},{160,64},{192,128},{224,1... | collective-permute-start | bytes 331784 | tf_op jit(solution)/shard_map/ppermute | solution.py:373
  23.7 7.6 %collective-permute-done.4 = bf16[2,48,1152]{2,1,0:T(8,128)(2,1)S(1)} collective-permute-done((bf16[2,48,1152]{2,1,0:T(8,128)(2,1)S(1)}, bf16[2,48,1152]{2,1,0:T(8,128)(2,1)S(1)}, u32[]{:S(2)}, u32[]{:S(2)}) %collective-permute-start.4) | collective-permute-done | bytes 221216 | tf_op jit(solution)/shard_map/ppermute | solution.py:351
  32.7 7.2 %collective-permute-done.26 = bf16[2,48,1152]{2,1,0:T(8,128)(2,1)S(1)} collective-permute-done((bf16[2,48,1152]{2,1,0:T(8,128)(2,1)S(1)}, bf16[2,48,1152]{2,1,0:T(8,128)(2,1)S(1)}, u32[]{:S(2)}, u32[]{:S(2)}) %collective-permute-start.26) | collective-permute-done | bytes 221216 | tf_op jit(solution)/shard_map/ppermute | solution.py:351
  50.2 31.2 %all-gather.5.cloned.1.call-done = bf16[16,2,48,1152]{3,2,1,0:T(8,128)(2,1)} async-done(((bf16[2,2,48,1152]{3,2,1,0:T(8,128)(2,1)}), bf16[16,2,48,1152]{3,2,1,0:T(8,128)(2,1)}) %all-gather.5.cloned.1.call-update) | async-done | bytes 3538960 | tf_op jit(solution)/shard_map/all_gather | solution.py:388
  81.5 6.4 %collective-permute-done.9.refs_4_.refs_8_.refs_7_.refs_9_.refs_11_ = bf16[8,2,2,48,1152]{4,3,2,1,0:T(8,128)(2,1)} collective-permute-done((bf16[8,2,2,48,1152]{4,3,2,1,0:T(8,128)(2,1)}, bf16[8,2,2,48,1152]{4,3,2,1,0:T(8,128)(2,1)}, u32[]{:S(2)}, u32[]{:S(2)}) %collective-permute-start.9) | collective-permute-done | bytes 3538976 | tf_op jit(solution)/shard_map/ppermute | solution.py:351
  118.2 4.9 %forward_step.11 = (bf16[112,384]{1,0:T(8,128)(2,1)S(1)}, bf16[4,112,384]{2,1,0:T(8,128)(2,1)}, bf16[112,1536]{1,0:T(8,128)(2,1)}, f32[112,1152]{1,0:T(8,128)}) custom-call(s32[7]{0:T(128)S(1)} %pad_add_fusion.scal, bf16[112,384]{1,0:T(8,128)(2,1)S(1)} %collective-permute-done.14.refs_0_, bf16[112,384]{1,0:T(8,128)(2,1)S(1)} %collective-permute-done.15.refs_1_, ...), custom_call_target="tpu_custom_call" | custom-call | tf_op jit(solution)/shard_map/forward_step/pallas_call | solution.py:459
  132.8 5.4 %forward_step.12 = (bf16[112,384]{1,0:T(8,128)(2,1)S(1)}, bf16[4,112,384]{2,1,0:T(8,128)(2,1)}, bf16[112,1536]{1,0:T(8,128)(2,1)}, f32[112,1152]{1,0:T(8,128)}) custom-call(s32[7]{0:T(128)S(1)} %pad_add_fusion.scal, bf16[112,384]{1,0:T(8,128)(2,1)S(1)} %collective-permute-done.18.refs_0_, bf16[112,384]{1,0:T(8,128)(2,1)S(1)} %collective-permute-done.19.refs_1_, ...), custom_call_target="tpu_custom_call" | custom-call | tf_op jit(solution)/shard_map/forward_step/pallas_call | solution.py:459
  151.8 4.8 %forward_step.13 = (bf16[112,384]{1,0:T(8,128)(2,1)S(1)}, bf16[4,112,384]{2,1,0:T(8,128)(2,1)}, bf16[112,1536]{1,0:T(8,128)(2,1)}, f32[112,1152]{1,0:T(8,128)}) custom-call(s32[7]{0:T(128)S(1)} %pad_add_fusion.scal, bf16[112,384]{1,0:T(8,128)(2,1)S(1)} %collective-permute-done.22.refs_0_, bf16[112,384]{1,0:T(8,128)(2,1)S(1)} %collective-permute-done.23.refs_1_, ...), custom_call_target="tpu_custom_call" | custom-call | tf_op jit(solution)/shard_map/forward_step/pallas_call | solution.py:459
  165.4 4.8 %forward_step.14 = (bf16[112,384]{1,0:T(8,128)(2,1)S(1)}, bf16[4,112,384]{2,1,0:T(8,128)(2,1)}, bf16[112,1536]{1,0:T(8,128)(2,1)}, f32[112,1152]{1,0:T(8,128)}) custom-call(s32[7]{0:T(128)S(1)} %pad_add_fusion.scal, bf16[112,384]{1,0:T(8,128)(2,1)S(1)} %collective-permute-done.28.refs_0_, bf16[112,384]{1,0:T(8,128)(2,1)S(1)} %collective-permute-done.29.refs_1_, ...), custom_call_target="tpu_custom_call" | custom-call | tf_op jit(solution)/shard_map/forward_step/pallas_call | solution.py:459
  179.6 4.8 %forward_step.15 = (bf16[112,384]{1,0:T(8,128)(2,1)S(1)}, bf16[4,112,384]{2,1,0:T(8,128)(2,1)}, bf16[112,1536]{1,0:T(8,128)(2,1)}, f32[112,1152]{1,0:T(8,128)}) custom-call(s32[7]{0:T(128)S(1)} %pad_add_fusion.scal, bf16[112,384]{1,0:T(8,128)(2,1)S(1)} %collective-permute-done.32.refs_0_, bf16[112,384]{1,0:T(8,128)(2,1)S(1)} %collective-permute-done.33.refs_1_, ...), custom_call_target="tpu_custom_call" | custom-call | tf_op jit(solution)/shard_map/forward_step/pallas_call | solution.py:459
  193.9 4.8 %forward_step.16 = (bf16[112,384]{1,0:T(8,128)(2,1)S(1)}, bf16[4,112,384]{2,1,0:T(8,128)(2,1)}, bf16[112,1536]{1,0:T(8,128)(2,1)}, f32[112,1152]{1,0:T(8,128)}) custom-call(s32[7]{0:T(128)S(1)} %pad_add_fusion.scal, bf16[112,384]{1,0:T(8,128)(2,1)S(1)} %collective-permute-done.36.refs_0_, bf16[112,384]{1,0:T(8,128)(2,1)S(1)} %collective-permute-done.37.refs_1_, ...), custom_call_target="tpu_custom_call" | custom-call | tf_op jit(solution)/shard_map/forward_step/pallas_call | solution.py:459
  212.7 6.3 %backward_step.9 = (bf16[112,384]{1,0:T(8,128)(2,1)S(1)}, bf16[112,384]{1,0:T(8,128)(2,1)S(1)}, bf16[112,384]{1,0:T(8,128)(2,1)S(1)}, bf16[112,384]{1,0:T(8,128)(2,1)S(1)}, bf16[112,1152]{1,0:T(8,128)(2,1)}) custom-call(s32[7]{0:T(128)S(1)} %pad_add_fusion.scal, bf16[112,384]{1,0:T(8,128)(2,1)S(1)} %get-tuple-element.255.refs_0_, ...), custom_call_target="tpu_custom_call" | custom-call | tf_op jit(solution)/shard_map/backward_step/pallas_call | solution.py:498
  228.6 6.3 %backward_step.10 = (bf16[112,384]{1,0:T(8,128)(2,1)S(1)}, bf16[112,384]{1,0:T(8,128)(2,1)S(1)}, bf16[112,384]{1,0:T(8,128)(2,1)S(1)}, bf16[112,384]{1,0:T(8,128)(2,1)S(1)}, bf16[112,1152]{1,0:T(8,128)(2,1)}) custom-call(s32[7]{0:T(128)S(1)} %pad_add_fusion.scal, bf16[112,384]{1,0:T(8,128)(2,1)S(1)} %get-tuple-element.256.refs_0_, ...), custom_call_target="tpu_custom_call" | custom-call | tf_op jit(solution)/shard_map/backward_step/pallas_call | solution.py:498
  245.2 6.6 %backward_step.11 = (bf16[112,384]{1,0:T(8,128)(2,1)S(1)}, bf16[112,384]{1,0:T(8,128)(2,1)S(1)}, bf16[112,384]{1,0:T(8,128)(2,1)S(1)}, bf16[112,384]{1,0:T(8,128)(2,1)S(1)}, bf16[112,1152]{1,0:T(8,128)(2,1)}) custom-call(s32[7]{0:T(128)S(1)} %pad_add_fusion.scal, bf16[112,384]{1,0:T(8,128)(2,1)S(1)} %collective-permute-done.48.refs_0_, ...), custom_call_target="tpu_custom_call" | custom-call | tf_op jit(solution)/shard_map/backward_step/pallas_call | solution.py:498
  262.2 6.8 %backward_step.12 = (bf16[112,384]{1,0:T(8,128)(2,1)S(1)}, bf16[112,384]{1,0:T(8,128)(2,1)S(1)}, bf16[112,384]{1,0:T(8,128)(2,1)S(1)}, bf16[112,384]{1,0:T(8,128)(2,1)S(1)}, bf16[112,1152]{1,0:T(8,128)(2,1)}) custom-call(s32[7]{0:T(128)S(1)} %pad_add_fusion.scal, bf16[112,384]{1,0:T(8,128)(2,1)S(1)} %collective-permute-done.52.refs_0_, ...), custom_call_target="tpu_custom_call" | custom-call | tf_op jit(solution)/shard_map/backward_step/pallas_call | solution.py:498
  279.8 6.8 %backward_step.13 = (bf16[112,384]{1,0:T(8,128)(2,1)S(1)}, bf16[112,384]{1,0:T(8,128)(2,1)S(1)}, bf16[112,384]{1,0:T(8,128)(2,1)S(1)}, bf16[112,384]{1,0:T(8,128)(2,1)S(1)}, bf16[112,1152]{1,0:T(8,128)(2,1)}) custom-call(s32[7]{0:T(128)S(1)} %pad_add_fusion.scal, bf16[112,384]{1,0:T(8,128)(2,1)S(1)} %collective-permute-done.56.refs_0_, ...), custom_call_target="tpu_custom_call" | custom-call | tf_op jit(solution)/shard_map/backward_step/pallas_call | solution.py:498
  296.6 6.8 %backward_step.14 = (bf16[112,384]{1,0:T(8,128)(2,1)S(1)}, bf16[112,384]{1,0:T(8,128)(2,1)S(1)}, bf16[112,384]{1,0:T(8,128)(2,1)S(1)}, bf16[112,384]{1,0:T(8,128)(2,1)S(1)}, bf16[112,1152]{1,0:T(8,128)(2,1)}) custom-call(s32[7]{0:T(128)S(1)} %pad_add_fusion.scal, bf16[112,384]{1,0:T(8,128)(2,1)S(1)} %collective-permute-done.60.refs_0_, ...), custom_call_target="tpu_custom_call" | custom-call | tf_op jit(solution)/shard_map/backward_step/pallas_call | solution.py:498
  314.0 6.6 %backward_step.15 = (bf16[112,384]{1,0:T(8,128)(2,1)S(1)}, bf16[112,384]{1,0:T(8,128)(2,1)S(1)}, bf16[112,384]{1,0:T(8,128)(2,1)S(1)}, bf16[112,384]{1,0:T(8,128)(2,1)S(1)}, bf16[112,1152]{1,0:T(8,128)(2,1)}) custom-call(s32[7]{0:T(128)S(1)} %pad_add_fusion.scal, bf16[112,384]{1,0:T(8,128)(2,1)S(1)} %collective-permute-done.65.refs_0_, ...), custom_call_target="tpu_custom_call" | custom-call | tf_op jit(solution)/shard_map/backward_step/pallas_call | solution.py:498
  339.9 7.2 %backward_step.16 = (bf16[112,384]{1,0:T(8,128)(2,1)S(1)}, bf16[112,384]{1,0:T(8,128)(2,1)S(1)}, bf16[112,384]{1,0:T(8,128)(2,1)S(1)}, bf16[112,384]{1,0:T(8,128)(2,1)S(1)}, bf16[112,1152]{1,0:T(8,128)(2,1)}) custom-call(s32[7]{0:T(128)S(1)} %pad_add_fusion.scal, bf16[112,384]{1,0:T(8,128)(2,1)S(1)} %collective-permute-done.69.refs_0_, ...), custom_call_target="tpu_custom_call" | custom-call | tf_op jit(solution)/shard_map/backward_step/pallas_call | solution.py:498
  374.5 5.1 %reduce-scatter.3.cloned.1.call-done = bf16[1,192,1152]{2,1,0:T(8,128)(2,1)} async-done(((bf16[8,192,1152]{2,1,0:T(8,128)(2,1)}), bf16[1,192,1152]{2,1,0:T(8,128)(2,1)}) %reduce-scatter.3.cloned.1.call-update) | async-done | bytes 442384 | tf_op jit(solution)/shard_map/reduce_scatter | solution.py:569
  381.3 8.1 %collective-permute-done.80 = bf16[2,48,1152]{2,1,0:T(8,128)(2,1)S(1)} collective-permute-done((bf16[2,48,1152]{2,1,0:T(8,128)(2,1)S(1)}, bf16[2,48,1152]{2,1,0:T(8,128)(2,1)S(1)}, u32[]{:S(2)}, u32[]{:S(2)}) %collective-permute-start.80) | collective-permute-done | bytes 221216 | tf_op jit(solution)/shard_map/ppermute | solution.py:351
  398.1 32.4 %reduce-scatter.5.cloned.1.call-done = bf16[1,192,1152]{2,1,0:T(8,128)(2,1)} async-done(((bf16[8,192,1152]{2,1,0:T(8,128)(2,1)}), bf16[1,192,1152]{2,1,0:T(8,128)(2,1)}) %reduce-scatter.5.cloned.1.call-update) | async-done | bytes 442384 | tf_op jit(solution)/shard_map/reduce_scatter | solution.py:569
  432.1 8.2 %collective-permute-done.85 = bf16[2,48,1152]{2,1,0:T(8,128)(2,1)S(1)} collective-permute-done((bf16[2,48,1152]{2,1,0:T(8,128)(2,1)S(1)}, bf16[2,48,1152]{2,1,0:T(8,128)(2,1)S(1)}, u32[]{:S(2)}, u32[]{:S(2)}) %collective-permute-start.85) | collective-permute-done | bytes 221216 | tf_op jit(solution)/shard_map/ppermute | solution.py:351
  444.6 6.4 %collective-permute-start.87 = (bf16[48,1152]{1,0:T(8,128)(2,1)S(1)}, bf16[48,1152]{1,0:T(8,128)(2,1)S(1)}, u32[]{:S(2)}, u32[]{:S(2)}) collective-permute-start(bf16[48,1152]{1,0:T(8,128)(2,1)S(1)} %get-tuple-element.274), channel_id=1, source_target_pairs={{0,64},{32,96},{192,32},{224,0},{1,65},{33,97},{193,33},{225,1},{2... | collective-permute-start | bytes 331784 | tf_op jit(solution)/shard_map/ppermute | solution.py:578
  (262 shorter events, 252.6 us)
Async XLA Ops:
  6.5 74.8 %all-gather.5.cloned.1.call-start = ((), (), s32[]{:S(2)}) async-start(), calls=%async_computation.4 | async-start | bytes 3981312 | tf_op jit(solution)/shard_map/all_gather | solution.py:388
  8.4 8.1 %collective-permute-start = (bf16[48,1152]{1,0:T(8,128)(2,1)S(1)}, bf16[48,1152]{1,0:T(8,128)(2,1)S(1)}, u32[]{:S(2)}, u32[]{:S(2)}) collective-permute-start(bf16[48,1152]{1,0:T(8,128)(2,1)S(1)} %get-tuple-element.267), channel_id=1, source_target_pairs={{0,0},{32,32},{64,96},{96,64},{128,128},{160,160},{192,224},{224,1... | collective-permute-start | bytes 331784 | tf_op jit(solution)/shard_map/ppermute | solution.py:373
  9.0 9.1 %collective-permute-start.3 = (bf16[48,1152]{1,0:T(8,128)(2,1)S(1)}, bf16[48,1152]{1,0:T(8,128)(2,1)S(1)}, u32[]{:S(2)}, u32[]{:S(2)}) collective-permute-start(bf16[48,1152]{1,0:T(8,128)(2,1)S(1)} %get-tuple-element.268), channel_id=1, source_target_pairs={{0,224},{32,192},{64,0},{96,32},{128,96},{160,64},{192,128},{224,1... | collective-permute-start | bytes 331784 | tf_op jit(solution)/shard_map/ppermute | solution.py:373
  14.8 8.1 %collective-permute-start.2 = (bf16[48,1152]{1,0:T(8,128)(2,1)S(1)}, bf16[48,1152]{1,0:T(8,128)(2,1)S(1)}, u32[]{:S(2)}, u32[]{:S(2)}) collective-permute-start(bf16[48,1152]{1,0:T(8,128)(2,1)S(1)} %get-tuple-element.269), channel_id=1, source_target_pairs={{0,128},{32,160},{64,224},{96,192},{128,0},{160,32},{192,96},{224,... | collective-permute-start | bytes 331784 | tf_op jit(solution)/shard_map/ppermute | solution.py:373
  23.1 8.2 %collective-permute-start.4 = (bf16[2,48,1152]{2,1,0:T(8,128)(2,1)S(1)}, bf16[2,48,1152]{2,1,0:T(8,128)(2,1)S(1)}, u32[]{:S(2)}, u32[]{:S(2)}) collective-permute-start(bf16[2,48,1152]{2,1,0:T(8,128)(2,1)S(1)} %pad_maximum_fusion.8), channel_id=1, source_target_pairs={{0,16},{16,0},{1,17},{17,1},{2,18},{18,2},{3,19},{19,3},{4,20},{20... | collective-permute-start | bytes 663560 | tf_op jit(solution)/shard_map/ppermute | solution.py:351
  32.2 98.2 %all-gather.7.cloned.1.call-start = ((), (), s32[]{:S(2)}) async-start(), calls=%async_computation.5 | async-start | bytes 3981312 | tf_op jit(solution)/shard_map/all_gather | solution.py:388
  40.8 338.8 %reduce-scatter.3.cloned.1.call-start = ((), (), s32[]{:S(2)}) async-start(), calls=%async_computation.2 | async-start | bytes 3981312 | tf_op jit(solution)/shard_map/reduce_scatter | solution.py:569
  123.0 9.8 %collective-permute-start.21 = (bf16[112,384]{1,0:T(8,128)(2,1)S(1)}, bf16[112,384]{1,0:T(8,128)(2,1)S(1)}, u32[]{:S(2)}, u32[]{:S(2)}) collective-permute-start(bf16[112,384]{1,0:T(8,128)(2,1)S(1)} %get-tuple-element.138), channel_id=1, source_target_pairs={{0,192},{32,224},{64,0},{96,32},{128,64},{160,96},{192,128},{224,1... | collective-permute-start | bytes 258056 | tf_op jit(solution)/shard_map/ppermute | solution.py:419
  124.5 8.3 %collective-permute-start.20 = (bf16[112,384]{1,0:T(8,128)(2,1)S(1)}, bf16[112,384]{1,0:T(8,128)(2,1)S(1)}, u32[]{:S(2)}, u32[]{:S(2)}) collective-permute-start(bf16[112,384]{1,0:T(8,128)(2,1)S(1)} %get-tuple-element.138), channel_id=1, source_target_pairs={{0,160},{32,128},{64,224},{96,192},{128,32},{160,0},{192,96},{224,... | collective-permute-start | bytes 258056 | tf_op jit(solution)/shard_map/ppermute | solution.py:419
  138.2 11.8 %collective-permute-start.27 = (bf16[8,2,2,48,1152]{4,3,2,1,0:T(8,128)(2,1)S(1)}, bf16[8,2,2,48,1152]{4,3,2,1,0:T(8,128)(2,1)S(1)}, u32[]{:S(2)}, u32[]{:S(2)}) collective-permute-start(bf16[8,2,2,48,1152]{4,3,2,1,0:T(8,128)(2,1)S(1)} %bitcast.121), channel_id=1, source_target_pairs={{0,1},{1,0},{2,3},{3,2},{4,5},{5,4},{6,7},{7,6},{8,9},{9,8},{10,11... | collective-permute-start | bytes 10616840 | tf_op jit(solution)/shard_map/ppermute | solution.py:351
  252.8 9.3 %collective-permute-start.53 = (bf16[112,384]{1,0:T(8,128)(2,1)S(1)}, bf16[112,384]{1,0:T(8,128)(2,1)S(1)}, u32[]{:S(2)}, u32[]{:S(2)}) collective-permute-start(bf16[112,384]{1,0:T(8,128)(2,1)S(1)} %get-tuple-element.177), channel_id=1, source_target_pairs={{0,64},{32,96},{64,128},{96,160},{128,192},{160,224},{192,0},{224,... | collective-permute-start | bytes 258056 | tf_op jit(solution)/shard_map/ppermute | solution.py:419
  253.3 8.8 %collective-permute-start.54 = (bf16[112,384]{1,0:T(8,128)(2,1)S(1)}, bf16[112,384]{1,0:T(8,128)(2,1)S(1)}, u32[]{:S(2)}, u32[]{:S(2)}) collective-permute-start(bf16[112,384]{1,0:T(8,128)(2,1)S(1)} %get-tuple-element.179), channel_id=1, source_target_pairs={{0,160},{32,128},{64,224},{96,192},{128,32},{160,0},{192,96},{224,... | collective-permute-start | bytes 258056 | tf_op jit(solution)/shard_map/ppermute | solution.py:419
  269.2 27.4 %collective-permute-start.61 = (bf16[8,2,48,1152]{3,2,1,0:T(8,128)(2,1)S(1)}, bf16[8,2,48,1152]{3,2,1,0:T(8,128)(2,1)S(1)}, u32[]{:S(2)}, u32[]{:S(2)}) collective-permute-start(bf16[8,2,48,1152]{3,2,1,0:T(8,128)(2,1)S(1)} %slice_bitcast_fusion.4), channel_id=1, source_target_pairs={{0,1},{1,0},{2,3},{3,2},{4,5},{5,4},{6,7},{7,6},{8,9},{9,8},{10,11... | collective-permute-start | bytes 5308424 | tf_op jit(solution)/shard_map/ppermute | solution.py:351
  287.1 9.5 %collective-permute-start.62 = (bf16[112,384]{1,0:T(8,128)(2,1)S(1)}, bf16[112,384]{1,0:T(8,128)(2,1)S(1)}, u32[]{:S(2)}, u32[]{:S(2)}) collective-permute-start(bf16[112,384]{1,0:T(8,128)(2,1)S(1)} %get-tuple-element.201), channel_id=1, source_target_pairs={{0,64},{32,96},{64,128},{96,160},{128,192},{160,224},{192,0},{224,... | collective-permute-start | bytes 258056 | tf_op jit(solution)/shard_map/ppermute | solution.py:419
  288.7 7.9 %collective-permute-start.63 = (bf16[112,384]{1,0:T(8,128)(2,1)S(1)}, bf16[112,384]{1,0:T(8,128)(2,1)S(1)}, u32[]{:S(2)}, u32[]{:S(2)}) collective-permute-start(bf16[112,384]{1,0:T(8,128)(2,1)S(1)} %get-tuple-element.204), channel_id=1, source_target_pairs={{0,160},{32,128},{64,224},{96,192},{128,32},{160,0},{192,96},{224,... | collective-permute-start | bytes 258056 | tf_op jit(solution)/shard_map/ppermute | solution.py:419
  303.6 25.7 %collective-permute-start.70 = (bf16[8,2,48,1152]{3,2,1,0:T(8,128)(2,1)S(1)}, bf16[8,2,48,1152]{3,2,1,0:T(8,128)(2,1)S(1)}, u32[]{:S(2)}, u32[]{:S(2)}) collective-permute-start(bf16[8,2,48,1152]{3,2,1,0:T(8,128)(2,1)S(1)} %slice_bitcast_fusion.3), channel_id=1, source_target_pairs={{0,1},{1,0},{2,3},{3,2},{4,5},{5,4},{6,7},{7,6},{8,9},{9,8},{10,11... | collective-permute-start | bytes 5308424 | tf_op jit(solution)/shard_map/ppermute | solution.py:351
  332.0 98.5 %reduce-scatter.5.cloned.1.call-start = ((), (), s32[]{:S(2)}) async-start(), calls=%async_computation.3 | async-start | bytes 3981312 | tf_op jit(solution)/shard_map/reduce_scatter | solution.py:569
  353.1 15.1 %collective-permute-start.79 = (bf16[8,2,48,1152]{3,2,1,0:T(8,128)(2,1)S(1)}, bf16[8,2,48,1152]{3,2,1,0:T(8,128)(2,1)S(1)}, u32[]{:S(2)}, u32[]{:S(2)}) collective-permute-start(bf16[8,2,48,1152]{3,2,1,0:T(8,128)(2,1)S(1)} %slice_bitcast_fusion.2), channel_id=1, source_target_pairs={{0,1},{1,0},{2,3},{3,2},{4,5},{5,4},{6,7},{7,6},{8,9},{9,8},{10,11... | collective-permute-start | bytes 5308424 | tf_op jit(solution)/shard_map/ppermute | solution.py:351
  380.6 8.8 %collective-permute-start.80 = (bf16[2,48,1152]{2,1,0:T(8,128)(2,1)S(1)}, bf16[2,48,1152]{2,1,0:T(8,128)(2,1)S(1)}, u32[]{:S(2)}, u32[]{:S(2)}) collective-permute-start(bf16[2,48,1152]{2,1,0:T(8,128)(2,1)S(1)} %dynamic-slice_bitcast_fusion.5), channel_id=1, source_target_pairs={{0,16},{16,0},{1,17},{17,1},{2,18},{18,2},{3,19},{19,3},{4,20},{20... | collective-permute-start | bytes 663560 | tf_op jit(solution)/shard_map/ppermute | solution.py:351
  431.5 8.8 %collective-permute-start.85 = (bf16[2,48,1152]{2,1,0:T(8,128)(2,1)S(1)}, bf16[2,48,1152]{2,1,0:T(8,128)(2,1)S(1)}, u32[]{:S(2)}, u32[]{:S(2)}) collective-permute-start(bf16[2,48,1152]{2,1,0:T(8,128)(2,1)S(1)} %dynamic-slice_bitcast_fusion.4), channel_id=1, source_target_pairs={{0,16},{16,0},{1,17},{17,1},{2,18},{18,2},{3,19},{19,3},{4,20},{20... | collective-permute-start | bytes 663560 | tf_op jit(solution)/shard_map/ppermute | solution.py:351
  441.4 9.7 %collective-permute-start.86 = (bf16[48,1152]{1,0:T(8,128)(2,1)S(1)}, bf16[48,1152]{1,0:T(8,128)(2,1)S(1)}, u32[]{:S(2)}, u32[]{:S(2)}) collective-permute-start(bf16[48,1152]{1,0:T(8,128)(2,1)S(1)} %get-tuple-element.271), channel_id=1, source_target_pairs={{0,0},{32,32},{64,96},{96,64},{1,1},{33,33},{65,97},{97,65},{2,2},... | collective-permute-start | bytes 331784 | tf_op jit(solution)/shard_map/ppermute | solution.py:578
  442.0 9.2 %collective-permute-start.89 = (bf16[48,1152]{1,0:T(8,128)(2,1)S(1)}, bf16[48,1152]{1,0:T(8,128)(2,1)S(1)}, u32[]{:S(2)}, u32[]{:S(2)}) collective-permute-start(bf16[48,1152]{1,0:T(8,128)(2,1)S(1)} %get-tuple-element.272), channel_id=1, source_target_pairs={{64,32},{96,0},{128,64},{160,96},{65,33},{97,1},{129,65},{161,97},... | collective-permute-start | bytes 331784 | tf_op jit(solution)/shard_map/ppermute | solution.py:578
  443.3 10.6 %collective-permute-start.88 = (bf16[48,1152]{1,0:T(8,128)(2,1)S(1)}, bf16[48,1152]{1,0:T(8,128)(2,1)S(1)}, u32[]{:S(2)}, u32[]{:S(2)}) collective-permute-start(bf16[48,1152]{1,0:T(8,128)(2,1)S(1)} %get-tuple-element.273), channel_id=1, source_target_pairs={{128,0},{160,32},{192,96},{224,64},{129,1},{161,33},{193,97},{225,... | collective-permute-start | bytes 331784 | tf_op jit(solution)/shard_map/ppermute | solution.py:578
  444.6 12.9 %collective-permute-start.87 = (bf16[48,1152]{1,0:T(8,128)(2,1)S(1)}, bf16[48,1152]{1,0:T(8,128)(2,1)S(1)}, u32[]{:S(2)}, u32[]{:S(2)}) collective-permute-start(bf16[48,1152]{1,0:T(8,128)(2,1)S(1)} %get-tuple-element.274), channel_id=1, source_target_pairs={{0,64},{32,96},{192,32},{224,0},{1,65},{33,97},{193,33},{225,1},{2... | collective-permute-start | bytes 331784 | tf_op jit(solution)/shard_map/ppermute | solution.py:578
  (81 other events, 562.3 us)
Sparse Core Ops, SparseCore 0:
  32.4 48.9 all-gather.4
  83.1 47.2 all-gather.6
  332.1 47.4 reduce-scatter.2
  382.2 48.2 reduce-scatter.4
